TPU v7x, 1024 devices: a whole 4x4x32 slice. The times are simulated.
1024 devices in a mesh: gx: 128 (over y, z), gy: 8 (over x, core).
Axes of the slice: x: 4, y: 4, z: 32, core: 2. Of those that a mesh axis runs over, the one named last changes fastest.
Arguments:
- density: float32 [512, 256, 256], P('gx', 'gy'), may hold values from -6 to 6
- field: float32 [512, 256, 256], P('gx', 'gy'), may hold values from -4 to 4
Outputs:
- updated: float32 [512, 256, 256], P('gx', 'gy')
All inputs are finite; a program needn't handle non-finite values.
Results may differ from a plain program's by a relative error of at most 0.00002.
Values sent between devices are 32-bit elements; how exact they have to be, the bound alone decides.
No kernel may reach another device: no remote copies, remote signals or barrier semaphores. Data moves between devices by JAX's collectives and lax.ppermute only.
A program may use at most 64 MiB of HBM per device.

v0:
```python
import jax
import jax.numpy as jnp
from jax import lax
from jax.sharding import PartitionSpec as P

PRE_SWEEPS = 2
POST_SWEEPS = 2
COARSE_SWEEPS = 6


mass_term = 0.02
damping = 0.8


def padded_2(cells, sides, width):
    for axis, dim in sides:
        count = lax.axis_size(axis)
        head = lax.slice_in_dim(cells, 0, width, axis=dim)
        tail = lax.slice_in_dim(cells, cells.shape[dim] - width, cells.shape[dim], axis=dim)
        cells = jnp.concatenate(
            [
                lax.ppermute(tail, axis, [(i, (i + 1) % count) for i in range(count)]),
                cells,
                lax.ppermute(head, axis, [((i + 1) % count, i) for i in range(count)]),
            ],
            axis=dim,
        )
    return cells


def around_cells(padded):
    center = padded[1:-1, 1:-1]
    total = padded[2:, 1:-1] + padded[:-2, 1:-1]
    total = total + padded[1:-1, 2:] + padded[1:-1, :-2]
    total = total + jnp.roll(center, -1, 2) + jnp.roll(center, 1, 2)
    return total


def operator(values, around, inv_step):
    return inv_step * (around - 6.0 * values) - mass_term * (
        values + values * values * values / 3.0
    )


def smooth_cells(padded, source, inv_step):
    values = padded[1:-1, 1:-1]
    misfit = operator(values, around_cells(padded), inv_step) - source
    slope = -6.0 * inv_step - mass_term * (1.0 + values * values)
    return values - damping * misfit / slope


def restrict(values):
    first, second, third = values.shape
    return values.reshape(first // 2, 2, second // 2, 2, third // 2, 2).mean(axis=(1, 3, 5))


def spread(center, minus, plus, axis):
    even = 0.75 * center + 0.25 * minus
    odd = 0.75 * center + 0.25 * plus
    both = jnp.stack([even, odd], axis=axis + 1)
    shape = list(center.shape)
    shape[axis] = shape[axis] * 2
    return both.reshape(shape)


def prolong_padded(padded):
    wider = spread(padded[1:-1], padded[:-2], padded[2:], 0)
    wider = spread(wider[:, 1:-1], wider[:, :-2], wider[:, 2:], 1)
    return spread(wider, jnp.roll(wider, 1, 2), jnp.roll(wider, -1, 2), 2)


def fine_pad(values):
    return padded_2(values, (("gx", 0), ("gy", 1)), 1)


def smooth_phase(values, density, sweeps):
    for sweep in range(sweeps):
        values = smooth_cells(fine_pad(values), density, 1.0)
    return values


def defect_pad(values):
    return fine_pad(values)


def coarse_pad(values):
    return padded_2(values, (("gx", 0), ("gy", 1)), 1)


def body(density, field):
    current = smooth_phase(field, density, PRE_SWEEPS)
    defect = density - operator(current, around_cells(defect_pad(current)), 1.0)
    start = restrict(current)
    coarse_defect = restrict(defect)
    coarse_source = operator(start, around_cells(coarse_pad(start)), 0.25) + coarse_defect
    coarse = start
    for sweep in range(COARSE_SWEEPS):
        coarse = smooth_cells(coarse_pad(coarse), coarse_source, 0.25)
    padded_change = coarse_pad(coarse - start)
    current = current + prolong_padded(padded_change)
    current = smooth_phase(current, density, POST_SWEEPS)
    return current


def solution(mesh):
    placed = (P("gx", "gy", None), P("gx", "gy", None))
    return jax.shard_map(
        body, mesh=mesh, in_specs=placed, out_specs=P("gx", "gy", None), check_vma=False
    )
```

profile of v0, /device:TPU:1, one launch (start us, length us, event | category | flops | bytes accessed | tf_op | source)
XLA Modules:
  0.0 229.2 jit_solution(17367048123916971437)
XLA Ops:
  0.0 0.8 fusion.201
  0.8 21.7 %collective-permute-start = (f32[1,32,256]{2,1,0:T(8,128)S(1)}, f32[1,32,256]{2,1,0:T(8,128)S(1)}, u32[]{:S(2)}, u32[]{:S(2)}) collective-permute-start(f32[1,32,256]{2,1,0:T(8,128)S(1)} %get-tuple-element.45), channel_id=1, source_target_pairs={{8,0},{16,8},{24,16},{32,24},{40,32},{48,40},{56,48},{64,56},{72,6... | collective-permute-start | bytes 98312 | tf_op jit(solution)/shard_map/ppermute | solution.py:24
  22.5 1.9 collective-permute-start.1
  24.4 1.1 fusion.200
  25.5 5.0 %collective-permute-done.1 = f32[1,32,256]{2,1,0:T(8,128)S(1)} collective-permute-done((f32[1,32,256]{2,1,0:T(8,128)S(1)}, f32[1,32,256]{2,1,0:T(8,128)S(1)}, u32[]{:S(2)}, u32[]{:S(2)}) %collective-permute-start.1) | collective-permute-done | bytes 32800 | tf_op jit(solution)/shard_map/ppermute | solution.py:22
  30.4 0.9 constant_dynamic-update-slice_fusion.1
  31.4 2.1 collective-permute-start.2
  33.5 1.1 collective-permute-start.3
  34.6 0.9 fusion.199
  35.9 1.2 fusion.7
  37.2 1.9 collective-permute-start.5
  39.1 6.7 %collective-permute-start.4 = (f32[1,32,256]{2,1,0:T(8,128)S(1)}, f32[1,32,256]{2,1,0:T(8,128)S(1)}, u32[]{:S(2)}, u32[]{:S(2)}) collective-permute-start(f32[1,32,256]{2,1,0:T(8,128)S(1)} %get-tuple-element.40), channel_id=1, source_target_pairs={{8,0},{16,8},{24,16},{32,24},{40,32},{48,40},{56,48},{64,56},{72,6... | collective-permute-start | bytes 98312 | tf_op jit(solution)/shard_map/ppermute | solution.py:24
  45.9 0.9 collective-permute-done.4
  46.8 3.8 %collective-permute-start.6 = (f32[6,1,256]{2,1,0:T(1,128)S(1)}, f32[6,1,256]{2,1,0:T(1,128)S(1)}, u32[]{:S(2)}, u32[]{:S(2)}) collective-permute-start(f32[6,1,256]{2,1,0:T(1,128)S(1)} %get-tuple-element.13), channel_id=1, source_target_pairs={{1,0},{2,1},{3,2},{4,3},{5,4},{6,5},{7,6},{0,7},{9,8},{10,9},{11,1... | collective-permute-start | bytes 18440 | tf_op jit(solution)/shard_map/ppermute | solution.py:24
  50.7 0.7 collective-permute-done.6
  51.7 1.1 fusion.17
  53.0 9.8 %reshape.95 = f32[2,2,16,2,128,2]{5,4,3,2,1,0:T(8,128)} reshape(f32[4,32,256]{2,1,0:T(8,128)S(1)} %fusion.17) | data formatting | bytes 262144 | tf_op jit(solution)/shard_map/reshape | solution.py:54
  62.8 4.0 %reduce_sum.18 = f32[2,16,128]{2,1,0:T(8,128)S(1)} reduce(f32[2,2,16,2,128,2]{5,4,3,2,1,0:T(8,128)} %reshape.95, f32[]{:T(128)} %constant.20.clone.1), dimensions={1,3,5}, to_apply=%region_0.1 | reduce | flops 28672 | bytes 147460 | tf_op jit(solution)/shard_map/reduce_sum | solution.py:54
  67.0 1.9 collective-permute-start.13
  68.9 7.3 %collective-permute-start.12 = (f32[1,32,256]{2,1,0:T(8,128)S(1)}, f32[1,32,256]{2,1,0:T(8,128)S(1)}, u32[]{:S(2)}, u32[]{:S(2)}) collective-permute-start(f32[1,32,256]{2,1,0:T(8,128)S(1)} %get-tuple-element.34), channel_id=1, source_target_pairs={{8,0},{16,8},{24,16},{32,24},{40,32},{48,40},{56,48},{64,56},{72,6... | collective-permute-start | bytes 98312 | tf_op jit(solution)/shard_map/ppermute | solution.py:24
  76.2 1.9 collective-permute-start.9
  78.1 6.7 %collective-permute-start.8 = (f32[1,16,128]{2,1,0:T(8,128)S(1)}, f32[1,16,128]{2,1,0:T(8,128)S(1)}, u32[]{:S(2)}, u32[]{:S(2)}) collective-permute-start(f32[1,16,128]{2,1,0:T(8,128)S(1)} %get-tuple-element.110), channel_id=1, source_target_pairs={{8,0},{16,8},{24,16},{32,24},{40,32},{48,40},{56,48},{64,56},{72,6... | collective-permute-start | bytes 24584 | tf_op jit(solution)/shard_map/ppermute | solution.py:24
  84.8 4.0 %collective-permute-start.14 = (f32[6,1,256]{2,1,0:T(1,128)S(1)}, f32[6,1,256]{2,1,0:T(1,128)S(1)}, u32[]{:S(2)}, u32[]{:S(2)}) collective-permute-start(f32[6,1,256]{2,1,0:T(1,128)S(1)} %get-tuple-element.11), channel_id=1, source_target_pairs={{1,0},{2,1},{3,2},{4,3},{5,4},{6,5},{7,6},{0,7},{9,8},{10,9},{11,1... | collective-permute-start | bytes 18440 | tf_op jit(solution)/shard_map/ppermute | solution.py:24
  88.8 1.3 collective-permute-start.10
  90.7 9.8 %reshape.96 = f32[2,2,16,2,128,2]{5,4,3,2,1,0:T(8,128)} reshape(f32[4,32,256]{2,1,0:T(8,128)S(1)} %fusion.44) | data formatting | bytes 262144 | tf_op jit(solution)/shard_map/reshape | solution.py:54
  100.5 4.0 %reduce_sum.19 = f32[2,16,128]{2,1,0:T(8,128)S(1)} reduce(f32[2,2,16,2,128,2]{5,4,3,2,1,0:T(8,128)} %reshape.96, f32[]{:T(128)} %constant.20.clone.1), dimensions={1,3,5}, to_apply=%region_1.2 | reduce | flops 28672 | bytes 147460 | tf_op jit(solution)/shard_map/reduce_sum | solution.py:54
  104.7 1.9 collective-permute-start.17
  106.6 6.8 %collective-permute-start.16 = (f32[1,16,128]{2,1,0:T(8,128)S(1)}, f32[1,16,128]{2,1,0:T(8,128)S(1)}, u32[]{:S(2)}, u32[]{:S(2)}) collective-permute-start(f32[1,16,128]{2,1,0:T(8,128)S(1)} %get-tuple-element.104), channel_id=1, source_target_pairs={{8,0},{16,8},{24,16},{32,24},{40,32},{48,40},{56,48},{64,56},{72,6... | collective-permute-start | bytes 24584 | tf_op jit(solution)/shard_map/ppermute | solution.py:24
  114.2 3.5 %collective-permute-start.18 = (f32[4,1,128]{2,1,0:T(1,128)S(1)}, f32[4,1,128]{2,1,0:T(1,128)S(1)}, u32[]{:S(2)}, u32[]{:S(2)}) collective-permute-start(f32[4,1,128]{2,1,0:T(1,128)S(1)} %get-tuple-element.69), channel_id=1, source_target_pairs={{1,0},{2,1},{3,2},{4,3},{5,4},{6,5},{7,6},{0,7},{9,8},{10,9},{11,1... | collective-permute-start | bytes 6152 | tf_op jit(solution)/shard_map/ppermute | solution.py:24
  117.8 0.7 collective-permute-done.18
  119.0 1.9 collective-permute-start.21
  120.9 7.2 %collective-permute-start.20 = (f32[1,16,128]{2,1,0:T(8,128)S(1)}, f32[1,16,128]{2,1,0:T(8,128)S(1)}, u32[]{:S(2)}, u32[]{:S(2)}) collective-permute-start(f32[1,16,128]{2,1,0:T(8,128)S(1)} %get-tuple-element.98), channel_id=1, source_target_pairs={{8,0},{16,8},{24,16},{32,24},{40,32},{48,40},{56,48},{64,56},{72,6... | collective-permute-start | bytes 24584 | tf_op jit(solution)/shard_map/ppermute | solution.py:24
  128.9 4.2 %collective-permute-start.22 = (f32[4,1,128]{2,1,0:T(1,128)S(1)}, f32[4,1,128]{2,1,0:T(1,128)S(1)}, u32[]{:S(2)}, u32[]{:S(2)}) collective-permute-start(f32[4,1,128]{2,1,0:T(1,128)S(1)} %get-tuple-element.67), channel_id=1, source_target_pairs={{1,0},{2,1},{3,2},{4,3},{5,4},{6,5},{7,6},{0,7},{9,8},{10,9},{11,1... | collective-permute-start | bytes 6152 | tf_op jit(solution)/shard_map/ppermute | solution.py:24
  133.2 0.7 collective-permute-done.22
  134.4 1.9 collective-permute-start.25
  136.3 7.2 %collective-permute-start.24 = (f32[1,16,128]{2,1,0:T(8,128)S(1)}, f32[1,16,128]{2,1,0:T(8,128)S(1)}, u32[]{:S(2)}, u32[]{:S(2)}) collective-permute-start(f32[1,16,128]{2,1,0:T(8,128)S(1)} %get-tuple-element.92), channel_id=1, source_target_pairs={{8,0},{16,8},{24,16},{32,24},{40,32},{48,40},{56,48},{64,56},{72,6... | collective-permute-start | bytes 24584 | tf_op jit(solution)/shard_map/ppermute | solution.py:24
  144.3 3.9 %collective-permute-start.26 = (f32[4,1,128]{2,1,0:T(1,128)S(1)}, f32[4,1,128]{2,1,0:T(1,128)S(1)}, u32[]{:S(2)}, u32[]{:S(2)}) collective-permute-start(f32[4,1,128]{2,1,0:T(1,128)S(1)} %get-tuple-element.65), channel_id=1, source_target_pairs={{1,0},{2,1},{3,2},{4,3},{5,4},{6,5},{7,6},{0,7},{9,8},{10,9},{11,1... | collective-permute-start | bytes 6152 | tf_op jit(solution)/shard_map/ppermute | solution.py:24
  148.3 0.7 collective-permute-done.26
  149.5 1.9 collective-permute-start.29
  151.4 7.2 %collective-permute-start.28 = (f32[1,16,128]{2,1,0:T(8,128)S(1)}, f32[1,16,128]{2,1,0:T(8,128)S(1)}, u32[]{:S(2)}, u32[]{:S(2)}) collective-permute-start(f32[1,16,128]{2,1,0:T(8,128)S(1)} %get-tuple-element.86), channel_id=1, source_target_pairs={{8,0},{16,8},{24,16},{32,24},{40,32},{48,40},{56,48},{64,56},{72,6... | collective-permute-start | bytes 24584 | tf_op jit(solution)/shard_map/ppermute | solution.py:24
  159.5 3.9 %collective-permute-start.30 = (f32[4,1,128]{2,1,0:T(1,128)S(1)}, f32[4,1,128]{2,1,0:T(1,128)S(1)}, u32[]{:S(2)}, u32[]{:S(2)}) collective-permute-start(f32[4,1,128]{2,1,0:T(1,128)S(1)} %get-tuple-element.63), channel_id=1, source_target_pairs={{1,0},{2,1},{3,2},{4,3},{5,4},{6,5},{7,6},{0,7},{9,8},{10,9},{11,1... | collective-permute-start | bytes 6152 | tf_op jit(solution)/shard_map/ppermute | solution.py:24
  163.5 0.7 collective-permute-done.30
  164.6 1.9 collective-permute-start.33
  166.6 7.2 %collective-permute-start.32 = (f32[1,16,128]{2,1,0:T(8,128)S(1)}, f32[1,16,128]{2,1,0:T(8,128)S(1)}, u32[]{:S(2)}, u32[]{:S(2)}) collective-permute-start(f32[1,16,128]{2,1,0:T(8,128)S(1)} %get-tuple-element.80), channel_id=1, source_target_pairs={{8,0},{16,8},{24,16},{32,24},{40,32},{48,40},{56,48},{64,56},{72,6... | collective-permute-start | bytes 24584 | tf_op jit(solution)/shard_map/ppermute | solution.py:24
  174.6 3.9 %collective-permute-start.34 = (f32[4,1,128]{2,1,0:T(1,128)S(1)}, f32[4,1,128]{2,1,0:T(1,128)S(1)}, u32[]{:S(2)}, u32[]{:S(2)}) collective-permute-start(f32[4,1,128]{2,1,0:T(1,128)S(1)} %get-tuple-element.61), channel_id=1, source_target_pairs={{1,0},{2,1},{3,2},{4,3},{5,4},{6,5},{7,6},{0,7},{9,8},{10,9},{11,1... | collective-permute-start | bytes 6152 | tf_op jit(solution)/shard_map/ppermute | solution.py:24
  178.6 0.7 collective-permute-done.34
  179.8 1.9 collective-permute-start.36
  181.7 7.2 %collective-permute-start.37 = (f32[1,16,128]{2,1,0:T(8,128)S(1)}, f32[1,16,128]{2,1,0:T(8,128)S(1)}, u32[]{:S(2)}, u32[]{:S(2)}) collective-permute-start(f32[1,16,128]{2,1,0:T(8,128)S(1)} %get-tuple-element.74), channel_id=1, source_target_pairs={{8,0},{16,8},{24,16},{32,24},{40,32},{48,40},{56,48},{64,56},{72,6... | collective-permute-start | bytes 24584 | tf_op jit(solution)/shard_map/ppermute | solution.py:24
  189.0 0.8 collective-permute-done.37
  189.7 2.7 %collective-permute-start.38 = (f32[4,1,128]{2,1,0:T(1,128)S(1)}, f32[4,1,128]{2,1,0:T(1,128)S(1)}, u32[]{:S(2)}, u32[]{:S(2)}) collective-permute-start(f32[4,1,128]{2,1,0:T(1,128)S(1)} %get-tuple-element.59), channel_id=1, source_target_pairs={{0,1},{1,2},{2,3},{3,4},{4,5},{5,6},{6,7},{7,0},{8,9},{9,10},{10,1... | collective-permute-start | bytes 6152 | tf_op jit(solution)/shard_map/ppermute | solution.py:22
  192.4 1.2 collective-permute-start.39
  194.3 1.1 collective-permute-done.39
  196.4 1.9 collective-permute-start.41
  198.4 7.2 %collective-permute-start.40 = (f32[1,32,256]{2,1,0:T(8,128)S(1)}, f32[1,32,256]{2,1,0:T(8,128)S(1)}, u32[]{:S(2)}, u32[]{:S(2)}) collective-permute-start(f32[1,32,256]{2,1,0:T(8,128)S(1)} %get-tuple-element.28), channel_id=1, source_target_pairs={{8,0},{16,8},{24,16},{32,24},{40,32},{48,40},{56,48},{64,56},{72,6... | collective-permute-start | bytes 98312 | tf_op jit(solution)/shard_map/ppermute | solution.py:24
  205.7 0.9 collective-permute-done.40
  206.6 3.3 %collective-permute-start.42 = (f32[6,1,256]{2,1,0:T(1,128)S(1)}, f32[6,1,256]{2,1,0:T(1,128)S(1)}, u32[]{:S(2)}, u32[]{:S(2)}) collective-permute-start(f32[6,1,256]{2,1,0:T(1,128)S(1)} %get-tuple-element.9), channel_id=1, source_target_pairs={{1,0},{2,1},{3,2},{4,3},{5,4},{6,5},{7,6},{0,7},{9,8},{10,9},{11,1... | collective-permute-start | bytes 18440 | tf_op jit(solution)/shard_map/ppermute | solution.py:24
  210.0 0.7 collective-permute-done.42
  210.8 1.9 collective-permute-done.43
  212.9 1.9 collective-permute-start.45
  214.8 7.0 %collective-permute-start.44 = (f32[1,32,256]{2,1,0:T(8,128)S(1)}, f32[1,32,256]{2,1,0:T(8,128)S(1)}, u32[]{:S(2)}, u32[]{:S(2)}) collective-permute-start(f32[1,32,256]{2,1,0:T(8,128)S(1)} %get-tuple-element.22), channel_id=1, source_target_pairs={{8,0},{16,8},{24,16},{32,24},{40,32},{48,40},{56,48},{64,56},{72,6... | collective-permute-start | bytes 98312 | tf_op jit(solution)/shard_map/ppermute | solution.py:24
  221.9 0.9 collective-permute-done.44
  222.8 4.5 %collective-permute-start.46 = (f32[6,1,256]{2,1,0:T(1,128)S(1)}, f32[6,1,256]{2,1,0:T(1,128)S(1)}, u32[]{:S(2)}, u32[]{:S(2)}) collective-permute-start(f32[6,1,256]{2,1,0:T(1,128)S(1)} %get-tuple-element.7), channel_id=1, source_target_pairs={{1,0},{2,1},{3,2},{4,3},{5,4},{6,5},{7,6},{0,7},{9,8},{10,9},{11,1... | collective-permute-start | bytes 18440 | tf_op jit(solution)/shard_map/ppermute | solution.py:24
  227.3 0.7 collective-permute-done.46
  228.4 0.8 fusion.37
  (113 shorter events, 10.9 us)
Async XLA Ops:
  0.8 30.6 %collective-permute-start = (f32[1,32,256]{2,1,0:T(8,128)S(1)}, f32[1,32,256]{2,1,0:T(8,128)S(1)}, u32[]{:S(2)}, u32[]{:S(2)}) collective-permute-start(f32[1,32,256]{2,1,0:T(8,128)S(1)} %get-tuple-element.45), channel_id=1, source_target_pairs={{8,0},{16,8},{24,16},{32,24},{40,32},{48,40},{56,48},{64,56},{72,6... | collective-permute-start | bytes 98312 | tf_op jit(solution)/shard_map/ppermute | solution.py:24
  22.5 8.0 %collective-permute-start.1 = (f32[1,32,256]{2,1,0:T(8,128)S(1)}, f32[1,32,256]{2,1,0:T(8,128)S(1)}, u32[]{:S(2)}, u32[]{:S(2)}) collective-permute-start(f32[1,32,256]{2,1,0:T(8,128)S(1)} %get-tuple-element.46), channel_id=1, source_target_pairs={{0,8},{8,16},{16,24},{24,32},{32,40},{40,48},{48,56},{56,64},{64,7... | collective-permute-start | bytes 98312 | tf_op jit(solution)/shard_map/ppermute | solution.py:22
  31.4 4.5 %collective-permute-start.2 = (f32[6,1,256]{2,1,0:T(1,128)S(1)}, f32[6,1,256]{2,1,0:T(1,128)S(1)}, u32[]{:S(2)}, u32[]{:S(2)}) collective-permute-start(f32[6,1,256]{2,1,0:T(1,128)S(1)} %get-tuple-element.15), channel_id=1, source_target_pairs={{1,0},{2,1},{3,2},{4,3},{5,4},{6,5},{7,6},{0,7},{9,8},{10,9},{11,1... | collective-permute-start | bytes 18440 | tf_op jit(solution)/shard_map/ppermute | solution.py:24
  33.5 2.4 %collective-permute-start.3 = (f32[6,1,256]{2,1,0:T(1,128)S(1)}, f32[6,1,256]{2,1,0:T(1,128)S(1)}, u32[]{:S(2)}, u32[]{:S(2)}) collective-permute-start(f32[6,1,256]{2,1,0:T(1,128)S(1)} %get-tuple-element.16), channel_id=1, source_target_pairs={{0,1},{1,2},{2,3},{3,4},{4,5},{5,6},{6,7},{7,0},{8,9},{9,10},{10,1... | collective-permute-start | bytes 18440 | tf_op jit(solution)/shard_map/ppermute | solution.py:22
  37.2 8.7 %collective-permute-start.5 = (f32[1,32,256]{2,1,0:T(8,128)S(1)}, f32[1,32,256]{2,1,0:T(8,128)S(1)}, u32[]{:S(2)}, u32[]{:S(2)}) collective-permute-start(f32[1,32,256]{2,1,0:T(8,128)S(1)} %get-tuple-element.39), channel_id=1, source_target_pairs={{0,8},{8,16},{16,24},{24,32},{32,40},{40,48},{48,56},{56,64},{64,7... | collective-permute-start | bytes 98312 | tf_op jit(solution)/shard_map/ppermute | solution.py:22
  39.1 7.7 %collective-permute-start.4 = (f32[1,32,256]{2,1,0:T(8,128)S(1)}, f32[1,32,256]{2,1,0:T(8,128)S(1)}, u32[]{:S(2)}, u32[]{:S(2)}) collective-permute-start(f32[1,32,256]{2,1,0:T(8,128)S(1)} %get-tuple-element.40), channel_id=1, source_target_pairs={{8,0},{16,8},{24,16},{32,24},{40,32},{48,40},{56,48},{64,56},{72,6... | collective-permute-start | bytes 98312 | tf_op jit(solution)/shard_map/ppermute | solution.py:24
  46.8 4.6 %collective-permute-start.6 = (f32[6,1,256]{2,1,0:T(1,128)S(1)}, f32[6,1,256]{2,1,0:T(1,128)S(1)}, u32[]{:S(2)}, u32[]{:S(2)}) collective-permute-start(f32[6,1,256]{2,1,0:T(1,128)S(1)} %get-tuple-element.13), channel_id=1, source_target_pairs={{1,0},{2,1},{3,2},{4,3},{5,4},{6,5},{7,6},{0,7},{9,8},{10,9},{11,1... | collective-permute-start | bytes 18440 | tf_op jit(solution)/shard_map/ppermute | solution.py:24
  50.6 1.2 collective-permute-start.7
  53.0 37.6 %copy-start = (f32[4,32,256]{2,1,0:T(8,128)S(1)}, f32[4,32,256]{2,1,0:T(8,128)}, u32[]{:S(2)}) copy-start(f32[4,32,256]{2,1,0:T(8,128)} %param.2) | copy-start | bytes 393220
  67.0 17.8 %collective-permute-start.13 = (f32[1,32,256]{2,1,0:T(8,128)S(1)}, f32[1,32,256]{2,1,0:T(8,128)S(1)}, u32[]{:S(2)}, u32[]{:S(2)}) collective-permute-start(f32[1,32,256]{2,1,0:T(8,128)S(1)} %get-tuple-element.33), channel_id=1, source_target_pairs={{0,8},{8,16},{16,24},{24,32},{32,40},{40,48},{48,56},{56,64},{64,7... | collective-permute-start | bytes 98312 | tf_op jit(solution)/shard_map/ppermute | solution.py:22
  68.9 15.9 %collective-permute-start.12 = (f32[1,32,256]{2,1,0:T(8,128)S(1)}, f32[1,32,256]{2,1,0:T(8,128)S(1)}, u32[]{:S(2)}, u32[]{:S(2)}) collective-permute-start(f32[1,32,256]{2,1,0:T(8,128)S(1)} %get-tuple-element.34), channel_id=1, source_target_pairs={{8,0},{16,8},{24,16},{32,24},{40,32},{48,40},{56,48},{64,56},{72,6... | collective-permute-start | bytes 98312 | tf_op jit(solution)/shard_map/ppermute | solution.py:24
  76.2 12.6 %collective-permute-start.9 = (f32[1,16,128]{2,1,0:T(8,128)S(1)}, f32[1,16,128]{2,1,0:T(8,128)S(1)}, u32[]{:S(2)}, u32[]{:S(2)}) collective-permute-start(f32[1,16,128]{2,1,0:T(8,128)S(1)} %get-tuple-element.109), channel_id=1, source_target_pairs={{0,8},{8,16},{16,24},{24,32},{32,40},{40,48},{48,56},{56,64},{64,7... | collective-permute-start | bytes 24584 | tf_op jit(solution)/shard_map/ppermute | solution.py:22
  78.1 10.7 %collective-permute-start.8 = (f32[1,16,128]{2,1,0:T(8,128)S(1)}, f32[1,16,128]{2,1,0:T(8,128)S(1)}, u32[]{:S(2)}, u32[]{:S(2)}) collective-permute-start(f32[1,16,128]{2,1,0:T(8,128)S(1)} %get-tuple-element.110), channel_id=1, source_target_pairs={{8,0},{16,8},{24,16},{32,24},{40,32},{48,40},{56,48},{64,56},{72,6... | collective-permute-start | bytes 24584 | tf_op jit(solution)/shard_map/ppermute | solution.py:24
  84.8 5.8 %collective-permute-start.14 = (f32[6,1,256]{2,1,0:T(1,128)S(1)}, f32[6,1,256]{2,1,0:T(1,128)S(1)}, u32[]{:S(2)}, u32[]{:S(2)}) collective-permute-start(f32[6,1,256]{2,1,0:T(1,128)S(1)} %get-tuple-element.11), channel_id=1, source_target_pairs={{1,0},{2,1},{3,2},{4,3},{5,4},{6,5},{7,6},{0,7},{9,8},{10,9},{11,1... | collective-permute-start | bytes 18440 | tf_op jit(solution)/shard_map/ppermute | solution.py:24
  88.8 1.8 collective-permute-start.15
  88.8 15.7 %collective-permute-start.10 = (f32[4,1,128]{2,1,0:T(1,128)S(1)}, f32[4,1,128]{2,1,0:T(1,128)S(1)}, u32[]{:S(2)}, u32[]{:S(2)}) collective-permute-start(f32[4,1,128]{2,1,0:T(1,128)S(1)} %get-tuple-element.71), channel_id=1, source_target_pairs={{1,0},{2,1},{3,2},{4,3},{5,4},{6,5},{7,6},{0,7},{9,8},{10,9},{11,1... | collective-permute-start | bytes 6152 | tf_op jit(solution)/shard_map/ppermute | solution.py:24
  90.1 14.4 %collective-permute-start.11 = (f32[4,1,128]{2,1,0:T(1,128)S(1)}, f32[4,1,128]{2,1,0:T(1,128)S(1)}, u32[]{:S(2)}, u32[]{:S(2)}) collective-permute-start(f32[4,1,128]{2,1,0:T(1,128)S(1)} %get-tuple-element.72), channel_id=1, source_target_pairs={{0,1},{1,2},{2,3},{3,4},{4,5},{5,6},{6,7},{7,0},{8,9},{9,10},{10,1... | collective-permute-start | bytes 6152 | tf_op jit(solution)/shard_map/ppermute | solution.py:22
  104.7 8.8 %collective-permute-start.17 = (f32[1,16,128]{2,1,0:T(8,128)S(1)}, f32[1,16,128]{2,1,0:T(8,128)S(1)}, u32[]{:S(2)}, u32[]{:S(2)}) collective-permute-start(f32[1,16,128]{2,1,0:T(8,128)S(1)} %get-tuple-element.103), channel_id=1, source_target_pairs={{0,8},{8,16},{16,24},{24,32},{32,40},{40,48},{48,56},{56,64},{64,7... | collective-permute-start | bytes 24584 | tf_op jit(solution)/shard_map/ppermute | solution.py:22
  106.6 7.5 %collective-permute-start.16 = (f32[1,16,128]{2,1,0:T(8,128)S(1)}, f32[1,16,128]{2,1,0:T(8,128)S(1)}, u32[]{:S(2)}, u32[]{:S(2)}) collective-permute-start(f32[1,16,128]{2,1,0:T(8,128)S(1)} %get-tuple-element.104), channel_id=1, source_target_pairs={{8,0},{16,8},{24,16},{32,24},{40,32},{48,40},{56,48},{64,56},{72,6... | collective-permute-start | bytes 24584 | tf_op jit(solution)/shard_map/ppermute | solution.py:24
  114.2 4.4 %collective-permute-start.18 = (f32[4,1,128]{2,1,0:T(1,128)S(1)}, f32[4,1,128]{2,1,0:T(1,128)S(1)}, u32[]{:S(2)}, u32[]{:S(2)}) collective-permute-start(f32[4,1,128]{2,1,0:T(1,128)S(1)} %get-tuple-element.69), channel_id=1, source_target_pairs={{1,0},{2,1},{3,2},{4,3},{5,4},{6,5},{7,6},{0,7},{9,8},{10,9},{11,1... | collective-permute-start | bytes 6152 | tf_op jit(solution)/shard_map/ppermute | solution.py:24
  117.7 1.2 collective-permute-start.19
  119.0 9.2 %collective-permute-start.21 = (f32[1,16,128]{2,1,0:T(8,128)S(1)}, f32[1,16,128]{2,1,0:T(8,128)S(1)}, u32[]{:S(2)}, u32[]{:S(2)}) collective-permute-start(f32[1,16,128]{2,1,0:T(8,128)S(1)} %get-tuple-element.97), channel_id=1, source_target_pairs={{0,8},{8,16},{16,24},{24,32},{32,40},{40,48},{48,56},{56,64},{64,7... | collective-permute-start | bytes 24584 | tf_op jit(solution)/shard_map/ppermute | solution.py:22
  120.9 8.0 %collective-permute-start.20 = (f32[1,16,128]{2,1,0:T(8,128)S(1)}, f32[1,16,128]{2,1,0:T(8,128)S(1)}, u32[]{:S(2)}, u32[]{:S(2)}) collective-permute-start(f32[1,16,128]{2,1,0:T(8,128)S(1)} %get-tuple-element.98), channel_id=1, source_target_pairs={{8,0},{16,8},{24,16},{32,24},{40,32},{48,40},{56,48},{64,56},{72,6... | collective-permute-start | bytes 24584 | tf_op jit(solution)/shard_map/ppermute | solution.py:24
  128.9 5.0 %collective-permute-start.22 = (f32[4,1,128]{2,1,0:T(1,128)S(1)}, f32[4,1,128]{2,1,0:T(1,128)S(1)}, u32[]{:S(2)}, u32[]{:S(2)}) collective-permute-start(f32[4,1,128]{2,1,0:T(1,128)S(1)} %get-tuple-element.67), channel_id=1, source_target_pairs={{1,0},{2,1},{3,2},{4,3},{5,4},{6,5},{7,6},{0,7},{9,8},{10,9},{11,1... | collective-permute-start | bytes 6152 | tf_op jit(solution)/shard_map/ppermute | solution.py:24
  133.1 1.2 collective-permute-start.23
  134.4 9.2 %collective-permute-start.25 = (f32[1,16,128]{2,1,0:T(8,128)S(1)}, f32[1,16,128]{2,1,0:T(8,128)S(1)}, u32[]{:S(2)}, u32[]{:S(2)}) collective-permute-start(f32[1,16,128]{2,1,0:T(8,128)S(1)} %get-tuple-element.91), channel_id=1, source_target_pairs={{0,8},{8,16},{16,24},{24,32},{32,40},{40,48},{48,56},{56,64},{64,7... | collective-permute-start | bytes 24584 | tf_op jit(solution)/shard_map/ppermute | solution.py:22
  136.3 8.0 %collective-permute-start.24 = (f32[1,16,128]{2,1,0:T(8,128)S(1)}, f32[1,16,128]{2,1,0:T(8,128)S(1)}, u32[]{:S(2)}, u32[]{:S(2)}) collective-permute-start(f32[1,16,128]{2,1,0:T(8,128)S(1)} %get-tuple-element.92), channel_id=1, source_target_pairs={{8,0},{16,8},{24,16},{32,24},{40,32},{48,40},{56,48},{64,56},{72,6... | collective-permute-start | bytes 24584 | tf_op jit(solution)/shard_map/ppermute | solution.py:24
  144.3 4.8 %collective-permute-start.26 = (f32[4,1,128]{2,1,0:T(1,128)S(1)}, f32[4,1,128]{2,1,0:T(1,128)S(1)}, u32[]{:S(2)}, u32[]{:S(2)}) collective-permute-start(f32[4,1,128]{2,1,0:T(1,128)S(1)} %get-tuple-element.65), channel_id=1, source_target_pairs={{1,0},{2,1},{3,2},{4,3},{5,4},{6,5},{7,6},{0,7},{9,8},{10,9},{11,1... | collective-permute-start | bytes 6152 | tf_op jit(solution)/shard_map/ppermute | solution.py:24
  148.2 1.2 collective-permute-start.27
  149.5 9.2 %collective-permute-start.29 = (f32[1,16,128]{2,1,0:T(8,128)S(1)}, f32[1,16,128]{2,1,0:T(8,128)S(1)}, u32[]{:S(2)}, u32[]{:S(2)}) collective-permute-start(f32[1,16,128]{2,1,0:T(8,128)S(1)} %get-tuple-element.85), channel_id=1, source_target_pairs={{0,8},{8,16},{16,24},{24,32},{32,40},{40,48},{48,56},{56,64},{64,7... | collective-permute-start | bytes 24584 | tf_op jit(solution)/shard_map/ppermute | solution.py:22
  151.4 8.0 %collective-permute-start.28 = (f32[1,16,128]{2,1,0:T(8,128)S(1)}, f32[1,16,128]{2,1,0:T(8,128)S(1)}, u32[]{:S(2)}, u32[]{:S(2)}) collective-permute-start(f32[1,16,128]{2,1,0:T(8,128)S(1)} %get-tuple-element.86), channel_id=1, source_target_pairs={{8,0},{16,8},{24,16},{32,24},{40,32},{48,40},{56,48},{64,56},{72,6... | collective-permute-start | bytes 24584 | tf_op jit(solution)/shard_map/ppermute | solution.py:24
  159.5 4.8 %collective-permute-start.30 = (f32[4,1,128]{2,1,0:T(1,128)S(1)}, f32[4,1,128]{2,1,0:T(1,128)S(1)}, u32[]{:S(2)}, u32[]{:S(2)}) collective-permute-start(f32[4,1,128]{2,1,0:T(1,128)S(1)} %get-tuple-element.63), channel_id=1, source_target_pairs={{1,0},{2,1},{3,2},{4,3},{5,4},{6,5},{7,6},{0,7},{9,8},{10,9},{11,1... | collective-permute-start | bytes 6152 | tf_op jit(solution)/shard_map/ppermute | solution.py:24
  163.4 1.2 collective-permute-start.31
  164.6 9.2 %collective-permute-start.33 = (f32[1,16,128]{2,1,0:T(8,128)S(1)}, f32[1,16,128]{2,1,0:T(8,128)S(1)}, u32[]{:S(2)}, u32[]{:S(2)}) collective-permute-start(f32[1,16,128]{2,1,0:T(8,128)S(1)} %get-tuple-element.79), channel_id=1, source_target_pairs={{0,8},{8,16},{16,24},{24,32},{32,40},{40,48},{48,56},{56,64},{64,7... | collective-permute-start | bytes 24584 | tf_op jit(solution)/shard_map/ppermute | solution.py:22
  166.6 8.0 %collective-permute-start.32 = (f32[1,16,128]{2,1,0:T(8,128)S(1)}, f32[1,16,128]{2,1,0:T(8,128)S(1)}, u32[]{:S(2)}, u32[]{:S(2)}) collective-permute-start(f32[1,16,128]{2,1,0:T(8,128)S(1)} %get-tuple-element.80), channel_id=1, source_target_pairs={{8,0},{16,8},{24,16},{32,24},{40,32},{48,40},{56,48},{64,56},{72,6... | collective-permute-start | bytes 24584 | tf_op jit(solution)/shard_map/ppermute | solution.py:24
  174.6 4.8 %collective-permute-start.34 = (f32[4,1,128]{2,1,0:T(1,128)S(1)}, f32[4,1,128]{2,1,0:T(1,128)S(1)}, u32[]{:S(2)}, u32[]{:S(2)}) collective-permute-start(f32[4,1,128]{2,1,0:T(1,128)S(1)} %get-tuple-element.61), channel_id=1, source_target_pairs={{1,0},{2,1},{3,2},{4,3},{5,4},{6,5},{7,6},{0,7},{9,8},{10,9},{11,1... | collective-permute-start | bytes 6152 | tf_op jit(solution)/shard_map/ppermute | solution.py:24
  178.5 1.2 collective-permute-start.35
  179.8 9.2 %collective-permute-start.36 = (f32[1,16,128]{2,1,0:T(8,128)S(1)}, f32[1,16,128]{2,1,0:T(8,128)S(1)}, u32[]{:S(2)}, u32[]{:S(2)}) collective-permute-start(f32[1,16,128]{2,1,0:T(8,128)S(1)} %get-tuple-element.73), channel_id=1, source_target_pairs={{0,8},{8,16},{16,24},{24,32},{32,40},{40,48},{48,56},{56,64},{64,7... | collective-permute-start | bytes 24584 | tf_op jit(solution)/shard_map/ppermute | solution.py:22
  181.7 8.0 %collective-permute-start.37 = (f32[1,16,128]{2,1,0:T(8,128)S(1)}, f32[1,16,128]{2,1,0:T(8,128)S(1)}, u32[]{:S(2)}, u32[]{:S(2)}) collective-permute-start(f32[1,16,128]{2,1,0:T(8,128)S(1)} %get-tuple-element.74), channel_id=1, source_target_pairs={{8,0},{16,8},{24,16},{32,24},{40,32},{48,40},{56,48},{64,56},{72,6... | collective-permute-start | bytes 24584 | tf_op jit(solution)/shard_map/ppermute | solution.py:24
  189.7 4.6 %collective-permute-start.38 = (f32[4,1,128]{2,1,0:T(1,128)S(1)}, f32[4,1,128]{2,1,0:T(1,128)S(1)}, u32[]{:S(2)}, u32[]{:S(2)}) collective-permute-start(f32[4,1,128]{2,1,0:T(1,128)S(1)} %get-tuple-element.59), channel_id=1, source_target_pairs={{0,1},{1,2},{2,3},{3,4},{4,5},{5,6},{6,7},{7,0},{8,9},{9,10},{10,1... | collective-permute-start | bytes 6152 | tf_op jit(solution)/shard_map/ppermute | solution.py:22
  192.4 3.0 %collective-permute-start.39 = (f32[4,1,128]{2,1,0:T(1,128)S(1)}, f32[4,1,128]{2,1,0:T(1,128)S(1)}, u32[]{:S(2)}, u32[]{:S(2)}) collective-permute-start(f32[4,1,128]{2,1,0:T(1,128)S(1)} %get-tuple-element.60), channel_id=1, source_target_pairs={{1,0},{2,1},{3,2},{4,3},{5,4},{6,5},{7,6},{0,7},{9,8},{10,9},{11,1... | collective-permute-start | bytes 6152 | tf_op jit(solution)/shard_map/ppermute | solution.py:24
  196.4 9.3 %collective-permute-start.41 = (f32[1,32,256]{2,1,0:T(8,128)S(1)}, f32[1,32,256]{2,1,0:T(8,128)S(1)}, u32[]{:S(2)}, u32[]{:S(2)}) collective-permute-start(f32[1,32,256]{2,1,0:T(8,128)S(1)} %get-tuple-element.27), channel_id=1, source_target_pairs={{0,8},{8,16},{16,24},{24,32},{32,40},{40,48},{48,56},{56,64},{64,7... | collective-permute-start | bytes 98312 | tf_op jit(solution)/shard_map/ppermute | solution.py:22
  198.4 8.2 %collective-permute-start.40 = (f32[1,32,256]{2,1,0:T(8,128)S(1)}, f32[1,32,256]{2,1,0:T(8,128)S(1)}, u32[]{:S(2)}, u32[]{:S(2)}) collective-permute-start(f32[1,32,256]{2,1,0:T(8,128)S(1)} %get-tuple-element.28), channel_id=1, source_target_pairs={{8,0},{16,8},{24,16},{32,24},{40,32},{48,40},{56,48},{64,56},{72,6... | collective-permute-start | bytes 98312 | tf_op jit(solution)/shard_map/ppermute | solution.py:24
  206.6 4.2 %collective-permute-start.42 = (f32[6,1,256]{2,1,0:T(1,128)S(1)}, f32[6,1,256]{2,1,0:T(1,128)S(1)}, u32[]{:S(2)}, u32[]{:S(2)}) collective-permute-start(f32[6,1,256]{2,1,0:T(1,128)S(1)} %get-tuple-element.9), channel_id=1, source_target_pairs={{1,0},{2,1},{3,2},{4,3},{5,4},{6,5},{7,6},{0,7},{9,8},{10,9},{11,1... | collective-permute-start | bytes 18440 | tf_op jit(solution)/shard_map/ppermute | solution.py:24
  210.0 2.7 %collective-permute-start.43 = (f32[6,1,256]{2,1,0:T(1,128)S(1)}, f32[6,1,256]{2,1,0:T(1,128)S(1)}, u32[]{:S(2)}, u32[]{:S(2)}) collective-permute-start(f32[6,1,256]{2,1,0:T(1,128)S(1)} %get-tuple-element.10), channel_id=1, source_target_pairs={{0,1},{1,2},{2,3},{3,4},{4,5},{5,6},{6,7},{7,0},{8,9},{9,10},{10,1... | collective-permute-start | bytes 18440 | tf_op jit(solution)/shard_map/ppermute | solution.py:22
  212.9 9.0 %collective-permute-start.45 = (f32[1,32,256]{2,1,0:T(8,128)S(1)}, f32[1,32,256]{2,1,0:T(8,128)S(1)}, u32[]{:S(2)}, u32[]{:S(2)}) collective-permute-start(f32[1,32,256]{2,1,0:T(8,128)S(1)} %get-tuple-element.21), channel_id=1, source_target_pairs={{0,8},{8,16},{16,24},{24,32},{32,40},{40,48},{48,56},{56,64},{64,7... | collective-permute-start | bytes 98312 | tf_op jit(solution)/shard_map/ppermute | solution.py:22
  214.8 8.0 %collective-permute-start.44 = (f32[1,32,256]{2,1,0:T(8,128)S(1)}, f32[1,32,256]{2,1,0:T(8,128)S(1)}, u32[]{:S(2)}, u32[]{:S(2)}) collective-permute-start(f32[1,32,256]{2,1,0:T(8,128)S(1)} %get-tuple-element.22), channel_id=1, source_target_pairs={{8,0},{16,8},{24,16},{32,24},{40,32},{48,40},{56,48},{64,56},{72,6... | collective-permute-start | bytes 98312 | tf_op jit(solution)/shard_map/ppermute | solution.py:24
  222.8 5.3 %collective-permute-start.46 = (f32[6,1,256]{2,1,0:T(1,128)S(1)}, f32[6,1,256]{2,1,0:T(1,128)S(1)}, u32[]{:S(2)}, u32[]{:S(2)}) collective-permute-start(f32[6,1,256]{2,1,0:T(1,128)S(1)} %get-tuple-element.7), channel_id=1, source_target_pairs={{1,0},{2,1},{3,2},{4,3},{5,4},{6,5},{7,6},{0,7},{9,8},{10,9},{11,1... | collective-permute-start | bytes 18440 | tf_op jit(solution)/shard_map/ppermute | solution.py:24
  227.2 1.2 collective-permute-start.47
where the time goes:
time: 230 us; the launch traced here: 229 us
  starting transfers between devices  166 us (72%)
  local copies, waits for them, and re-layouts  25.6 us (11%)
  waiting for transfers between devices  24.3 us (11%)
  other arithmetic  12.3 us (5%)
    ppermute x24, starting transfers between devices, padded_2(): lax.ppermute(head, axis, [((i + 1) % count, i) for i in range(count)])  139 us
    ppermute x24, starting transfers between devices, padded_2(): lax.ppermute(tail, axis, [(i, (i + 1) % count) for i in range(count)])  27.4 us
    reshape x2, local copies, waits for them, and re-layouts, restrict(): values.reshape(first // 2, 2, second // 2, 2, third // 2, 2)  19.6 us
    ppermute x24, waiting for transfers between devices, padded_2(): lax.ppermute(head, axis, [((i + 1) % count, i) for i in range(count)])  14.3 us
    ppermute x24, waiting for transfers between devices, padded_2(): lax.ppermute(tail, axis, [(i, (i + 1) % count) for i in range(count)])  9.95 us
    reduce_sum x2, other arithmetic, restrict(): values.reshape(first // 2, 2, second // 2, 2, third // 2, 2)  8.04 us
  transfers between devices with their start and end apart: 48, of which 29 were waited for; matrix products, arithmetic and copies ran while one was open for 8% of the time, Pallas kernels for 0%

commit v1 on v0

v1 whole, which is shorter than its diff:
```python
import jax
import jax.numpy as jnp
from jax import lax
from jax.experimental import pallas as pl
from jax.experimental.pallas import tpu as pltpu
from jax.sharding import PartitionSpec as P

mass = 0.02
damping = 0.8


def jacobi(v, below, above, source, inv_step):
    around = below + above
    around = around + pltpu.roll(v, 1, 0) + pltpu.roll(v, v.shape[0] - 1, 0)
    around = around + pltpu.roll(v, 1, 1) + pltpu.roll(v, v.shape[1] - 1, 1)
    square = v * v
    top = inv_step * around - source - v * ((6.0 * inv_step + mass) + (mass / 3.0) * square)
    return v + top / ((6.0 * inv_step + mass) / damping + (mass / damping) * square)


def operator(v, below, above, inv_step):
    around = below + above
    around = around + pltpu.roll(v, 1, 0) + pltpu.roll(v, v.shape[0] - 1, 0)
    around = around + pltpu.roll(v, 1, 1) + pltpu.roll(v, v.shape[1] - 1, 1)
    return inv_step * around - v * ((6.0 * inv_step + mass) + (mass / 3.0) * (v * v))


def exact_dot(values, weights):
    high = values.astype(jnp.bfloat16)
    rest = values - high.astype(jnp.float32)
    middle = rest.astype(jnp.bfloat16)
    low = (rest - middle.astype(jnp.float32)).astype(jnp.bfloat16)
    total = jnp.dot(low, weights, preferred_element_type=jnp.float32)
    total = total + jnp.dot(middle, weights, preferred_element_type=jnp.float32)
    return total + jnp.dot(high, weights, preferred_element_type=jnp.float32)


def fine_kernel(field, density, xlo, xhi, ylo, yhi, clo, chi, smooth, dens, coarse, f, d, s1, pair, rows):
    f[0:4, 8:40] = xlo[0:4]
    f[4:8, 8:40] = field[...]
    f[8:12, 8:40] = xhi[0:4]
    d[0:3, 8:40] = xlo[4:7]
    d[3:7, 8:40] = density[...]
    d[7:10, 8:40] = xhi[4:7]
    for corner, side, at in ((clo, ylo, 4), (chi, yhi, 40)):
        f[0:4, at : at + 4] = corner[0:4]
        f[4:8, at : at + 4] = side[:, 0:4]
        f[8:12, at : at + 4] = corner[7:11]
        d[0:3, at : at + 4] = corner[4:7]
        d[3:7, at : at + 4] = side[:, 4:8]
        d[7:10, at : at + 4] = corner[11:14]
    for i in range(10):
        s1[i] = jacobi(f[i + 1], f[i], f[i + 2], d[i], 1.0)
    for i in range(8):
        smooth[i] = jacobi(s1[i + 1], s1[i], s1[i + 2], d[i + 1], 1.0)
    dens[...] = d[2:8]
    for j in range(2):
        total = smooth[2 * j + 2] + smooth[2 * j + 3]
        pair[j, 0], pair[j, 1] = total[:, 0:128], total[:, 128:256]
        defect = [
            d[i + 3] - operator(smooth[i + 2], smooth[i + 1], smooth[i + 3], 1.0) for i in (2 * j, 2 * j + 1)
        ]
        total = defect[0] + defect[1]
        pair[j + 2, 0], pair[j + 2, 1] = total[:, 0:128], total[:, 128:256]
    for j in range(4):
        for k in range(2):
            total = pair[j, k, pl.ds(8, 16, stride=2)] + pair[j, k, pl.ds(9, 16, stride=2)]
            rows[16 * j : 16 * j + 16, 128 * k : 128 * k + 128] = total
    third = lax.broadcasted_iota(jnp.int32, (256, 128), 0)
    half = lax.broadcasted_iota(jnp.int32, (256, 128), 1)
    weights = jnp.where(third // 2 == half, 0.125, 0.0).astype(jnp.bfloat16)
    coarse[...] = exact_dot(rows[...], weights).reshape(4, 16, 128)


def coarse_kernel(smooth, dens, own, xlo, xhi, flo, fhi, ylo, yhi, clo, chi, glo, ghi, out, a, r, g, c0, c1, wide, corrected, post):
    def place(rows, mine, low, high, far_low, far_high):
        for ref, at in ((a, 0), (r, 1)):
            ref[7:9, rows] = mine[2 * at : 2 * at + 2]
            ref[5:7, rows] = low[2 * at : 2 * at + 2]
            ref[9:11, rows] = high[2 * at : 2 * at + 2]
            ref[0:5, rows] = far_low[5 * at : 5 * at + 5]
            ref[11:16, rows] = far_high[5 * at : 5 * at + 5]

    place(slice(8, 24), own, xlo, xhi, flo, fhi)
    place(slice(0, 8), ylo, clo.at[0:4], clo.at[4:8], glo.at[0:10], glo.at[10:20])
    place(slice(24, 32), yhi, chi.at[0:4], chi.at[4:8], ghi.at[0:10], ghi.at[10:20])
    for i in range(16):
        v = a[i]
        c0[i] = v - r[i] / ((1.5 + mass) / damping + (mass / damping) * (v * v))
    for i in range(1, 15):
        g[i] = operator(a[i], a[i - 1], a[i + 1], 0.25) + r[i]
    now, later = c0, c1
    for sweep in range(1, 6):
        for i in range(sweep, 16 - sweep):
            later[i] = jacobi(now[i], now[i - 1], now[i + 1], g[i], 0.25)
        now, later = later, now
    change = (now[5:11] - a[5:11]).reshape(192, 128)
    half = lax.broadcasted_iota(jnp.int32, (128, 256), 0)
    third = lax.broadcasted_iota(jnp.int32, (128, 256), 1)
    beside = (third // 2 + 2 * (third % 2) - 1 + 128) % 128
    weights = jnp.where(third // 2 == half, 0.75, jnp.where(beside == half, 0.25, 0.0)).astype(jnp.bfloat16)
    spread = exact_dot(change, weights).reshape(6, 32, 256)
    for i in range(6):
        v = spread[i]
        even = 0.75 * v + 0.25 * pltpu.roll(v, 1, 0)
        odd = 0.75 * v + 0.25 * pltpu.roll(v, 31, 0)
        for k in range(2):
            wide[i, k, pl.ds(0, 32, stride=2)] = even[:, 128 * k : 128 * k + 128]
            wide[i, k, pl.ds(1, 32, stride=2)] = odd[:, 128 * k : 128 * k + 128]
    for i in range(8):
        near = i // 2 + 1
        beside_layer = near - 1 if i % 2 == 0 else near + 1
        for k in range(2):
            lanes = slice(128 * k, 128 * k + 128)
            change = 0.75 * wide[near, k, 8:56] + 0.25 * wide[beside_layer, k, 8:56]
            corrected[i, :, lanes] = smooth[i, :, lanes] + change
    for i in range(6):
        post[i] = jacobi(corrected[i + 1], corrected[i], corrected[i + 2], dens[i], 1.0)
    for i in range(4):
        out[i] = jacobi(post[i + 1], post[i], post[i + 2], dens[i + 1], 1.0)[8:40]


def call(kernel, outs, scratch, *args):
    vmem = pl.BlockSpec(memory_space=pltpu.VMEM)
    shapes = [jax.ShapeDtypeStruct(shape, jnp.float32) for shape in outs]
    return pl.pallas_call(
        kernel,
        out_shape=shapes,
        in_specs=[vmem] * len(args),
        out_specs=[vmem] * len(outs),
        scratch_shapes=[pltpu.VMEM(shape, jnp.float32) for shape in scratch],
        compiler_params=pltpu.CompilerParams(vmem_limit_bytes=32 * 1024 * 1024),
    )(*args)


def send(values, axis, step):
    count = lax.axis_size(axis)
    return lax.ppermute(values, axis, [(i, (i + step) % count) for i in range(count)])


def body(density, field):
    xlo = send(jnp.concatenate([field, density[1:4]], 0), "gx", 1)
    xhi = send(jnp.concatenate([field, density[0:3]], 0), "gx", -1)
    ylo = send(jnp.concatenate([field[:, 28:32], density[:, 28:32]], 1), "gy", 1)
    yhi = send(jnp.concatenate([field[:, 0:4], density[:, 0:4]], 1), "gy", -1)
    clo = send(jnp.concatenate([xlo[:, 28:32], xhi[:, 28:32]], 0), "gy", 1)
    chi = send(jnp.concatenate([xlo[:, 0:4], xhi[:, 0:4]], 0), "gy", -1)
    smooth, dens, own = call(
        fine_kernel,
        [(8, 48, 256), (6, 48, 256), (4, 16, 128)],
        [(12, 48, 256), (10, 48, 256), (10, 48, 256), (4, 2, 48, 128), (64, 256)],
        field, density, xlo, xhi, ylo, yhi, clo, chi,
    )
    xlo = send(own, "gx", 1)
    xhi = send(own, "gx", -1)
    ylo = send(own[:, 8:16], "gy", 1)
    yhi = send(own[:, 0:8], "gy", -1)
    flo = send(jnp.concatenate([xlo[1:2], own[0:2], xhi[0:2], xlo[3:4], own[2:4], xhi[2:4]], 0), "gx", 3)
    fhi = send(jnp.concatenate([xlo[0:2], own[0:2], xhi[0:1], xlo[2:4], own[2:4], xhi[2:3]], 0), "gx", -3)
    near = jnp.concatenate([xlo, xhi], 0)
    clo = send(near[:, 8:16], "gy", 1)
    chi = send(near[:, 0:8], "gy", -1)
    far = jnp.concatenate([flo, fhi], 0)
    glo = send(far[:, 8:16], "gy", 1)
    ghi = send(far[:, 0:8], "gy", -1)
    (out,) = call(
        coarse_kernel,
        [(4, 32, 256)],
        [(16, 32, 128), (16, 32, 128), (16, 32, 128), (16, 32, 128), (16, 32, 128), (6, 2, 64, 128), (8, 48, 256), (6, 48, 256)],
        smooth, dens, own, xlo, xhi, flo, fhi, ylo, yhi, clo, chi, glo, ghi,
    )
    return out


def solution(mesh):
    placed = (P("gx", "gy", None), P("gx", "gy", None))
    return jax.shard_map(body, mesh=mesh, in_specs=placed, out_specs=P("gx", "gy", None), check_vma=False)
```

time: 230 us -> 76.2 us (0.33)
  the two profiles are of different devices: /device:TPU:1 before, /device:TPU:71 now
where the time goes in v1:
time: 76.2 us; the launch traced here: 75.9 us
  starting transfers between devices  45.1 us (59%)
  waiting for transfers between devices  26.6 us (35%)
  Pallas kernels  2.86 us (4%)
  local copies, waits for them, and re-layouts  1.12 us (1%)
    ppermute x16, starting transfers between devices, send(): lax.ppermute(values, axis, [(i, (i + step) % count) for i in range(count)])  45.1 us
    ppermute x16, waiting for transfers between devices, send(): lax.ppermute(values, axis, [(i, (i + step) % count) for i in range(count)])  26.6 us
    pallas_call x2, Pallas kernels, call(): pl.pallas_call(kernel, out_shape=shapes, in_specs=[vmem] * len(args), out...  2.86 us
  transfers between devices with their start and end apart: 16, of which 6 were waited for; matrix products, arithmetic and copies ran while one was open for 0% of the time, Pallas kernels for 0%

profile of v1, /device:TPU:71, one launch (start us, length us, event | category | flops | bytes accessed | tf_op | source)
XLA Modules:
  0.0 75.9 jit_solution(7968052721451044507)
XLA Ops:
  0.0 0.0 copy-start.1
  0.0 1.0 %fusion.5 = (f32[3,32,256]{2,1,0:T(8,128)S(1)}, f32[3,32,256]{2,1,0:T(8,128)S(1)}) fusion(f32[4,32,256]{2,1,0:T(8,128)} %density.1), kind=kLoop, calls=%fused_computation.27 | loop fusion | bytes 393216 | tf_op jit(solution)/shard_map/slice | solution.py:143
  1.0 0.0 copy-done.1
  1.0 0.0 copy-start
  1.1 3.5 %collective-permute-start = (f32[7,32,256]{2,1,0:T(8,128)S(1)}, f32[7,32,256]{2,1,0:T(8,128)S(1)}, u32[]{:S(2)}, u32[]{:S(2)}) collective-permute-start(f32[7,32,256]{2,1,0:T(8,128)S(1)} %get-tuple-element.22), channel_id=1, source_target_pairs={{0,8},{8,16},{16,24},{24,32},{32,40},{40,48},{48,56},{56,64},{64,7... | collective-permute-start | bytes 688136 | tf_op jit(solution)/shard_map/ppermute | solution.py:138
  4.6 1.9 %collective-permute-start.1 = (f32[7,32,256]{2,1,0:T(8,128)S(1)}, f32[7,32,256]{2,1,0:T(8,128)S(1)}, u32[]{:S(2)}, u32[]{:S(2)}) collective-permute-start(f32[7,32,256]{2,1,0:T(8,128)S(1)} %get-tuple-element.21), channel_id=1, source_target_pairs={{0,1016},{8,0},{16,8},{24,16},{32,24},{40,32},{48,40},{56,48},{64,... | collective-permute-start | bytes 688136 | tf_op jit(solution)/shard_map/ppermute | solution.py:138
  6.6 0.0 copy-done
  6.6 1.1 %collective-permute-start.2 = (f32[4,8,256]{2,1,0:T(8,128)S(1)}, f32[4,8,256]{2,1,0:T(8,128)S(1)}, u32[]{:S(2)}, u32[]{:S(2)}) collective-permute-start(f32[4,8,256]{2,1,0:T(8,128)S(1)} %pad_maximum_fusion.4), channel_id=1, source_target_pairs={{0,1},{1,2},{2,3},{3,4},{4,5},{5,6},{6,7},{7,0},{8,9},{9,10},{10,1... | collective-permute-start | bytes 98312 | tf_op jit(solution)/shard_map/ppermute | solution.py:138
  7.8 1.7 %collective-permute-done.xlo = f32[7,32,256]{2,1,0:T(8,128)S(1)} collective-permute-done((f32[7,32,256]{2,1,0:T(8,128)S(1)}, f32[7,32,256]{2,1,0:T(8,128)S(1)}, u32[]{:S(2)}, u32[]{:S(2)}) %collective-permute-start) | collective-permute-done | bytes 229408 | tf_op jit(solution)/shard_map/ppermute | solution.py:138
  9.4 4.9 %collective-permute-done.1.xhi = f32[7,32,256]{2,1,0:T(8,128)S(1)} collective-permute-done((f32[7,32,256]{2,1,0:T(8,128)S(1)}, f32[7,32,256]{2,1,0:T(8,128)S(1)}, u32[]{:S(2)}, u32[]{:S(2)}) %collective-permute-start.1) | collective-permute-done | bytes 229408 | tf_op jit(solution)/shard_map/ppermute | solution.py:138
  14.4 1.6 %collective-permute-start.5 = (f32[14,4,256]{2,1,0:T(4,128)S(1)}, f32[14,4,256]{2,1,0:T(4,128)S(1)}, u32[]{:S(2)}, u32[]{:S(2)}) collective-permute-start(f32[14,4,256]{2,1,0:T(4,128)S(1)} %pad_maximum_fusion.3), channel_id=1, source_target_pairs={{0,7},{1,0},{2,1},{3,2},{4,3},{5,4},{6,5},{7,6},{8,15},{9,8},{10,9... | collective-permute-start | bytes 172040 | tf_op jit(solution)/shard_map/ppermute | solution.py:138
  16.0 1.4 %collective-permute-start.4 = (f32[14,4,256]{2,1,0:T(4,128)S(1)}, f32[14,4,256]{2,1,0:T(4,128)S(1)}, u32[]{:S(2)}, u32[]{:S(2)}) collective-permute-start(f32[14,4,256]{2,1,0:T(4,128)S(1)} %pad_maximum_fusion.2), channel_id=1, source_target_pairs={{0,1},{1,2},{2,3},{3,4},{4,5},{5,6},{6,7},{7,0},{8,9},{9,10},{10,1... | collective-permute-start | bytes 172040 | tf_op jit(solution)/shard_map/ppermute | solution.py:138
  17.4 0.0 collective-permute-start.3
  17.4 0.0 collective-permute-done.2.ylo
  17.5 4.5 %collective-permute-done.3.yhi = f32[4,8,256]{2,1,0:T(8,128)S(1)} collective-permute-done((f32[4,8,256]{2,1,0:T(8,128)S(1)}, f32[4,8,256]{2,1,0:T(8,128)S(1)}, u32[]{:S(2)}, u32[]{:S(2)}) %collective-permute-start.3) | collective-permute-done | bytes 32800 | tf_op jit(solution)/shard_map/ppermute | solution.py:138
  22.0 0.0 collective-permute-done.5.chi
  22.0 0.0 collective-permute-done.4.clo
  22.0 0.9 %shard_map.28 = (f32[8,48,256]{2,1,0:T(8,128)S(1)}, f32[6,48,256]{2,1,0:T(8,128)S(1)}, f32[4,16,128]{2,1,0:T(8,128)S(1)}) custom-call(f32[4,32,256]{2,1,0:T(8,128)S(1)} %copy-done.1, f32[4,32,256]{2,1,0:T(8,128)S(1)} %copy-done, f32[7,32,256]{2,1,0:T(8,128)S(1)} %collective-permute-done.xlo, f32[7,32,256]{2,1,0:T(8,128)S(1)} %collective-permute-done.1.xhi, ...), custom_call_target="tpu_custom_call" | custom-call | tf_op jit(solution)/shard_map/pallas_call | solution.py:126
  22.9 4.3 %collective-permute-start.6 = (f32[4,16,128]{2,1,0:T(8,128)S(1)}, f32[4,16,128]{2,1,0:T(8,128)S(1)}, u32[]{:S(2)}, u32[]{:S(2)}) collective-permute-start(f32[4,16,128]{2,1,0:T(8,128)S(1)} %get-tuple-element.10.own), channel_id=1, source_target_pairs={{0,8},{8,16},{16,24},{24,32},{32,40},{40,48},{48,56},{56,64},{64,7... | collective-permute-start | bytes 98312 | tf_op jit(solution)/shard_map/ppermute | solution.py:138
  27.2 4.0 %collective-permute-start.7 = (f32[4,16,128]{2,1,0:T(8,128)S(1)}, f32[4,16,128]{2,1,0:T(8,128)S(1)}, u32[]{:S(2)}, u32[]{:S(2)}) collective-permute-start(f32[4,16,128]{2,1,0:T(8,128)S(1)} %get-tuple-element.10.own), channel_id=1, source_target_pairs={{0,1016},{8,0},{16,8},{24,16},{32,24},{40,32},{48,40},{56,48},{64,... | collective-permute-start | bytes 98312 | tf_op jit(solution)/shard_map/ppermute | solution.py:138
  31.3 0.5 collective-permute-start.10
  31.8 0.0 collective-permute-done.6.xlo
  31.8 0.5 collective-permute-done.7.xhi
  32.3 20.8 %collective-permute-start.9 = (f32[10,16,128]{2,1,0:T(8,128)S(1)}, f32[10,16,128]{2,1,0:T(8,128)S(1)}, u32[]{:S(2)}, u32[]{:S(2)}) collective-permute-start(f32[10,16,128]{2,1,0:T(8,128)S(1)} %constant_dynamic-update-slice_fusion.6), channel_id=1, source_target_pairs={{0,1000},{8,1008},{16,1016},{24,0},{32,8},{40,16},{48,24},{56,32},... | collective-permute-start | bytes 245768 | tf_op jit(solution)/shard_map/ppermute | solution.py:138
  53.1 1.9 %collective-permute-start.8 = (f32[10,16,128]{2,1,0:T(8,128)S(1)}, f32[10,16,128]{2,1,0:T(8,128)S(1)}, u32[]{:S(2)}, u32[]{:S(2)}) collective-permute-start(f32[10,16,128]{2,1,0:T(8,128)S(1)} %constant_dynamic-update-slice_fusion), channel_id=1, source_target_pairs={{0,24},{8,32},{16,40},{24,48},{32,56},{40,64},{48,72},{56,80},{64,... | collective-permute-start | bytes 245768 | tf_op jit(solution)/shard_map/ppermute | solution.py:138
  55.1 11.0 %collective-permute-done.8.flo = f32[10,16,128]{2,1,0:T(8,128)S(1)} collective-permute-done((f32[10,16,128]{2,1,0:T(8,128)S(1)}, f32[10,16,128]{2,1,0:T(8,128)S(1)}, u32[]{:S(2)}, u32[]{:S(2)}) %collective-permute-start.8) | collective-permute-done | bytes 81952 | tf_op jit(solution)/shard_map/ppermute | solution.py:138
  66.1 0.0 collective-permute-done.9.fhi
  66.1 0.2 collective-permute-start.14
  66.3 0.3 collective-permute-start.15
  66.7 2.6 %collective-permute-start.12 = (f32[8,8,128]{2,1,0:T(8,128)S(1)}, f32[8,8,128]{2,1,0:T(8,128)S(1)}, u32[]{:S(2)}, u32[]{:S(2)}) collective-permute-start(f32[8,8,128]{2,1,0:T(8,128)S(1)} %get-tuple-element.26), channel_id=1, source_target_pairs={{0,1},{1,2},{2,3},{3,4},{4,5},{5,6},{6,7},{7,0},{8,9},{9,10},{10,1... | collective-permute-start | bytes 98312 | tf_op jit(solution)/shard_map/ppermute | solution.py:138
  69.3 0.0 collective-permute-start.13
  69.3 0.0 collective-permute-done.10.ylo
  69.3 0.7 collective-permute-start.11
  70.0 4.0 %collective-permute-done.11.yhi = f32[4,8,128]{2,1,0:T(8,128)S(1)} collective-permute-done((f32[4,8,128]{2,1,0:T(8,128)S(1)}, f32[4,8,128]{2,1,0:T(8,128)S(1)}, u32[]{:S(2)}, u32[]{:S(2)}) %collective-permute-start.11) | collective-permute-done | bytes 16416 | tf_op jit(solution)/shard_map/ppermute | solution.py:138
  74.0 0.0 collective-permute-done.12.clo
  74.0 0.0 collective-permute-done.13.chi
  74.0 0.0 collective-permute-done.14.glo
  74.0 0.0 collective-permute-done.15.ghi
  74.0 1.9 %shard_map.29 = f32[4,32,256]{2,1,0:T(8,128)} custom-call(f32[8,48,256]{2,1,0:T(8,128)S(1)} %get-tuple-element.8.smooth, f32[6,48,256]{2,1,0:T(8,128)S(1)} %get-tuple-element.9.dens, f32[4,16,128]{2,1,0:T(8,128)S(1)} %get-tuple-element.10.own, f32[4,16,128]{2,1,0:T(8,128)S(1)} %collective-permute-done.6.xlo, f32[4,16,128]{2,1,0:T(8,128)S(1)} %collective-permute-done.7.xhi, ...), custom_call_target="tpu_custom_call" | custom-call | tf_op jit(solution)/shard_map/pallas_call | solution.py:126
  (26 shorter events, 0.2 us)
Async XLA Ops:
  0.0 1.0 %copy-start.1 = (f32[4,32,256]{2,1,0:T(8,128)S(1)}, f32[4,32,256]{2,1,0:T(8,128)}, u32[]{:S(2)}) copy-start(f32[4,32,256]{2,1,0:T(8,128)} %field.1) | copy-start | bytes 393220
  1.0 5.6 %copy-start = (f32[4,32,256]{2,1,0:T(8,128)S(1)}, f32[4,32,256]{2,1,0:T(8,128)}, u32[]{:S(2)}) copy-start(f32[4,32,256]{2,1,0:T(8,128)} %density.1) | copy-start | bytes 393220
  1.1 8.4 %collective-permute-start = (f32[7,32,256]{2,1,0:T(8,128)S(1)}, f32[7,32,256]{2,1,0:T(8,128)S(1)}, u32[]{:S(2)}, u32[]{:S(2)}) collective-permute-start(f32[7,32,256]{2,1,0:T(8,128)S(1)} %get-tuple-element.22), channel_id=1, source_target_pairs={{0,8},{8,16},{16,24},{24,32},{32,40},{40,48},{48,56},{56,64},{64,7... | collective-permute-start | bytes 688136 | tf_op jit(solution)/shard_map/ppermute | solution.py:138
  4.6 9.8 %collective-permute-start.1 = (f32[7,32,256]{2,1,0:T(8,128)S(1)}, f32[7,32,256]{2,1,0:T(8,128)S(1)}, u32[]{:S(2)}, u32[]{:S(2)}) collective-permute-start(f32[7,32,256]{2,1,0:T(8,128)S(1)} %get-tuple-element.21), channel_id=1, source_target_pairs={{0,1016},{8,0},{16,8},{24,16},{32,24},{40,32},{48,40},{56,48},{64,... | collective-permute-start | bytes 688136 | tf_op jit(solution)/shard_map/ppermute | solution.py:138
  6.6 10.8 %collective-permute-start.2 = (f32[4,8,256]{2,1,0:T(8,128)S(1)}, f32[4,8,256]{2,1,0:T(8,128)S(1)}, u32[]{:S(2)}, u32[]{:S(2)}) collective-permute-start(f32[4,8,256]{2,1,0:T(8,128)S(1)} %pad_maximum_fusion.4), channel_id=1, source_target_pairs={{0,1},{1,2},{2,3},{3,4},{4,5},{5,6},{6,7},{7,0},{8,9},{9,10},{10,1... | collective-permute-start | bytes 98312 | tf_op jit(solution)/shard_map/ppermute | solution.py:138
  14.4 7.6 %collective-permute-start.5 = (f32[14,4,256]{2,1,0:T(4,128)S(1)}, f32[14,4,256]{2,1,0:T(4,128)S(1)}, u32[]{:S(2)}, u32[]{:S(2)}) collective-permute-start(f32[14,4,256]{2,1,0:T(4,128)S(1)} %pad_maximum_fusion.3), channel_id=1, source_target_pairs={{0,7},{1,0},{2,1},{3,2},{4,3},{5,4},{6,5},{7,6},{8,15},{9,8},{10,9... | collective-permute-start | bytes 172040 | tf_op jit(solution)/shard_map/ppermute | solution.py:138
  16.0 6.0 %collective-permute-start.4 = (f32[14,4,256]{2,1,0:T(4,128)S(1)}, f32[14,4,256]{2,1,0:T(4,128)S(1)}, u32[]{:S(2)}, u32[]{:S(2)}) collective-permute-start(f32[14,4,256]{2,1,0:T(4,128)S(1)} %pad_maximum_fusion.2), channel_id=1, source_target_pairs={{0,1},{1,2},{2,3},{3,4},{4,5},{5,6},{6,7},{7,0},{8,9},{9,10},{10,1... | collective-permute-start | bytes 172040 | tf_op jit(solution)/shard_map/ppermute | solution.py:138
  17.4 4.6 %collective-permute-start.3 = (f32[4,8,256]{2,1,0:T(8,128)S(1)}, f32[4,8,256]{2,1,0:T(8,128)S(1)}, u32[]{:S(2)}, u32[]{:S(2)}) collective-permute-start(f32[4,8,256]{2,1,0:T(8,128)S(1)} %pad_maximum_fusion.5), channel_id=1, source_target_pairs={{0,7},{1,0},{2,1},{3,2},{4,3},{5,4},{6,5},{7,6},{8,15},{9,8},{10,9... | collective-permute-start | bytes 98312 | tf_op jit(solution)/shard_map/ppermute | solution.py:138
  22.9 8.8 %collective-permute-start.6 = (f32[4,16,128]{2,1,0:T(8,128)S(1)}, f32[4,16,128]{2,1,0:T(8,128)S(1)}, u32[]{:S(2)}, u32[]{:S(2)}) collective-permute-start(f32[4,16,128]{2,1,0:T(8,128)S(1)} %get-tuple-element.10.own), channel_id=1, source_target_pairs={{0,8},{8,16},{16,24},{24,32},{32,40},{40,48},{48,56},{56,64},{64,7... | collective-permute-start | bytes 98312 | tf_op jit(solution)/shard_map/ppermute | solution.py:138
  27.2 5.0 %collective-permute-start.7 = (f32[4,16,128]{2,1,0:T(8,128)S(1)}, f32[4,16,128]{2,1,0:T(8,128)S(1)}, u32[]{:S(2)}, u32[]{:S(2)}) collective-permute-start(f32[4,16,128]{2,1,0:T(8,128)S(1)} %get-tuple-element.10.own), channel_id=1, source_target_pairs={{0,1016},{8,0},{16,8},{24,16},{32,24},{40,32},{48,40},{56,48},{64,... | collective-permute-start | bytes 98312 | tf_op jit(solution)/shard_map/ppermute | solution.py:138
  31.3 38.0 %collective-permute-start.10 = (f32[4,8,128]{2,1,0:T(8,128)S(1)}, f32[4,8,128]{2,1,0:T(8,128)S(1)}, u32[]{:S(2)}, u32[]{:S(2)}) collective-permute-start(f32[4,8,128]{2,1,0:T(8,128)S(1)} %get-tuple-element.28), channel_id=1, source_target_pairs={{0,1},{1,2},{2,3},{3,4},{4,5},{5,6},{6,7},{7,0},{8,9},{9,10},{10,1... | collective-permute-start | bytes 49160 | tf_op jit(solution)/shard_map/ppermute | solution.py:138
  32.3 33.8 %collective-permute-start.9 = (f32[10,16,128]{2,1,0:T(8,128)S(1)}, f32[10,16,128]{2,1,0:T(8,128)S(1)}, u32[]{:S(2)}, u32[]{:S(2)}) collective-permute-start(f32[10,16,128]{2,1,0:T(8,128)S(1)} %constant_dynamic-update-slice_fusion.6), channel_id=1, source_target_pairs={{0,1000},{8,1008},{16,1016},{24,0},{32,8},{40,16},{48,24},{56,32},... | collective-permute-start | bytes 245768 | tf_op jit(solution)/shard_map/ppermute | solution.py:138
  53.1 12.9 %collective-permute-start.8 = (f32[10,16,128]{2,1,0:T(8,128)S(1)}, f32[10,16,128]{2,1,0:T(8,128)S(1)}, u32[]{:S(2)}, u32[]{:S(2)}) collective-permute-start(f32[10,16,128]{2,1,0:T(8,128)S(1)} %constant_dynamic-update-slice_fusion), channel_id=1, source_target_pairs={{0,24},{8,32},{16,40},{24,48},{32,56},{40,64},{48,72},{56,80},{64,... | collective-permute-start | bytes 245768 | tf_op jit(solution)/shard_map/ppermute | solution.py:138
  66.1 7.9 %collective-permute-start.14 = (f32[20,8,128]{2,1,0:T(8,128)S(1)}, f32[20,8,128]{2,1,0:T(8,128)S(1)}, u32[]{:S(2)}, u32[]{:S(2)}) collective-permute-start(f32[20,8,128]{2,1,0:T(8,128)S(1)} %get-tuple-element.16), channel_id=1, source_target_pairs={{0,1},{1,2},{2,3},{3,4},{4,5},{5,6},{6,7},{7,0},{8,9},{9,10},{10,1... | collective-permute-start | bytes 245768 | tf_op jit(solution)/shard_map/ppermute | solution.py:138
  66.3 7.7 %collective-permute-start.15 = (f32[20,8,128]{2,1,0:T(8,128)S(1)}, f32[20,8,128]{2,1,0:T(8,128)S(1)}, u32[]{:S(2)}, u32[]{:S(2)}) collective-permute-start(f32[20,8,128]{2,1,0:T(8,128)S(1)} %get-tuple-element.15), channel_id=1, source_target_pairs={{0,7},{1,0},{2,1},{3,2},{4,3},{5,4},{6,5},{7,6},{8,15},{9,8},{10,9... | collective-permute-start | bytes 245768 | tf_op jit(solution)/shard_map/ppermute | solution.py:138
  66.7 7.4 %collective-permute-start.12 = (f32[8,8,128]{2,1,0:T(8,128)S(1)}, f32[8,8,128]{2,1,0:T(8,128)S(1)}, u32[]{:S(2)}, u32[]{:S(2)}) collective-permute-start(f32[8,8,128]{2,1,0:T(8,128)S(1)} %get-tuple-element.26), channel_id=1, source_target_pairs={{0,1},{1,2},{2,3},{3,4},{4,5},{5,6},{6,7},{7,0},{8,9},{9,10},{10,1... | collective-permute-start | bytes 98312 | tf_op jit(solution)/shard_map/ppermute | solution.py:138
  69.3 4.7 %collective-permute-start.13 = (f32[8,8,128]{2,1,0:T(8,128)S(1)}, f32[8,8,128]{2,1,0:T(8,128)S(1)}, u32[]{:S(2)}, u32[]{:S(2)}) collective-permute-start(f32[8,8,128]{2,1,0:T(8,128)S(1)} %get-tuple-element.25), channel_id=1, source_target_pairs={{0,7},{1,0},{2,1},{3,2},{4,3},{5,4},{6,5},{7,6},{8,15},{9,8},{10,9... | collective-permute-start | bytes 98312 | tf_op jit(solution)/shard_map/ppermute | solution.py:138
  69.3 4.7 %collective-permute-start.11 = (f32[4,8,128]{2,1,0:T(8,128)S(1)}, f32[4,8,128]{2,1,0:T(8,128)S(1)}, u32[]{:S(2)}, u32[]{:S(2)}) collective-permute-start(f32[4,8,128]{2,1,0:T(8,128)S(1)} %get-tuple-element.27), channel_id=1, source_target_pairs={{0,7},{1,0},{2,1},{3,2},{4,3},{5,4},{6,5},{7,6},{8,15},{9,8},{10,9... | collective-permute-start | bytes 49160 | tf_op jit(solution)/shard_map/ppermute | solution.py:138

commit v2 on v1

--- a/solution.py
+++ b/solution.py
@@ -35,30 +35,30 @@
     return total + jnp.dot(high, weights, preferred_element_type=jnp.float32)
 
 
-def fine_kernel(field, density, xlo, xhi, ylo, yhi, clo, chi, smooth, dens, coarse, f, d, s1, pair, rows):
-    f[0:4, 8:40] = xlo[0:4]
-    f[4:8, 8:40] = field[...]
-    f[8:12, 8:40] = xhi[0:4]
-    d[0:3, 8:40] = xlo[4:7]
-    d[3:7, 8:40] = density[...]
-    d[7:10, 8:40] = xhi[4:7]
+def fine_kernel(field, density, xlo, xhi, ylo, yhi, clo, chi, smooth, dens, coarse, up, down, f, d, s1, pair, rows):
+    f[0:3, 8:40] = xlo[0:3]
+    f[3:7, 8:40] = field[...]
+    f[7:10, 8:40] = xhi[0:3]
+    d[0:2, 8:40] = xlo[3:5]
+    d[2:6, 8:40] = density[...]
+    d[6:8, 8:40] = xhi[3:5]
     for corner, side, at in ((clo, ylo, 4), (chi, yhi, 40)):
-        f[0:4, at : at + 4] = corner[0:4]
-        f[4:8, at : at + 4] = side[:, 0:4]
-        f[8:12, at : at + 4] = corner[7:11]
-        d[0:3, at : at + 4] = corner[4:7]
-        d[3:7, at : at + 4] = side[:, 4:8]
-        d[7:10, at : at + 4] = corner[11:14]
-    for i in range(10):
+        f[0:3, at : at + 4] = corner[0:3]
+        f[3:7, at : at + 4] = side[:, 0:4]
+        f[7:10, at : at + 4] = corner[5:8]
+        d[0:2, at : at + 4] = corner[3:5]
+        d[2:6, at : at + 4] = side[:, 4:8]
+        d[6:8, at : at + 4] = corner[8:10]
+    for i in range(8):
         s1[i] = jacobi(f[i + 1], f[i], f[i + 2], d[i], 1.0)
-    for i in range(8):
+    for i in range(6):
         smooth[i] = jacobi(s1[i + 1], s1[i], s1[i + 2], d[i + 1], 1.0)
-    dens[...] = d[2:8]
+    dens[...] = d[1:7]
     for j in range(2):
-        total = smooth[2 * j + 2] + smooth[2 * j + 3]
+        total = smooth[2 * j + 1] + smooth[2 * j + 2]
         pair[j, 0], pair[j, 1] = total[:, 0:128], total[:, 128:256]
         defect = [
-            d[i + 3] - operator(smooth[i + 2], smooth[i + 1], smooth[i + 3], 1.0) for i in (2 * j, 2 * j + 1)
+            d[i + 2] - operator(smooth[i + 1], smooth[i], smooth[i + 2], 1.0) for i in (2 * j, 2 * j + 1)
         ]
         total = defect[0] + defect[1]
         pair[j + 2, 0], pair[j + 2, 1] = total[:, 0:128], total[:, 128:256]
@@ -70,20 +70,31 @@
     half = lax.broadcasted_iota(jnp.int32, (256, 128), 1)
     weights = jnp.where(third // 2 == half, 0.125, 0.0).astype(jnp.bfloat16)
     coarse[...] = exact_dot(rows[...], weights).reshape(4, 16, 128)
+    for face, layer in ((up, 3), (down, 2)):
+        for j in range(4):
+            at, lane = 8 + 16 * (j // 2), 128 * (j % 2)
+            face[j] = smooth[layer, at : at + 16, lane : lane + 128]
 
 
-def coarse_kernel(smooth, dens, own, xlo, xhi, flo, fhi, ylo, yhi, clo, chi, glo, ghi, out, a, r, g, c0, c1, wide, corrected, post):
-    def place(rows, mine, low, high, far_low, far_high):
+def coarse_kernel(
+    smooth, dens, own, flo, fhi, nlo, nhi, yown, yfar, ynear, zown, zfar, znear,
+    out, a, r, g, c0, c1, wide, corrected, post,
+):
+    def place(rows, mine, far_low, far_high, low, high):
         for ref, at in ((a, 0), (r, 1)):
+            ref[0:1, rows] = low[at : at + 1]
+            ref[1:3, rows] = far_low[2 * at : 2 * at + 2]
+            ref[3:5, rows] = high[2 * at + 6 : 2 * at + 8]
+            ref[5:7, rows] = low[2 * at + 2 : 2 * at + 4]
             ref[7:9, rows] = mine[2 * at : 2 * at + 2]
-            ref[5:7, rows] = low[2 * at : 2 * at + 2]
-            ref[9:11, rows] = high[2 * at : 2 * at + 2]
-            ref[0:5, rows] = far_low[5 * at : 5 * at + 5]
-            ref[11:16, rows] = far_high[5 * at : 5 * at + 5]
+            ref[9:11, rows] = high[2 * at + 2 : 2 * at + 4]
+            ref[11:13, rows] = low[2 * at + 6 : 2 * at + 8]
+            ref[13:15, rows] = far_high[2 * at : 2 * at + 2]
+            ref[15:16, rows] = high[at : at + 1]
 
-    place(slice(8, 24), own, xlo, xhi, flo, fhi)
-    place(slice(0, 8), ylo, clo.at[0:4], clo.at[4:8], glo.at[0:10], glo.at[10:20])
-    place(slice(24, 32), yhi, chi.at[0:4], chi.at[4:8], ghi.at[0:10], ghi.at[10:20])
+    place(slice(8, 24), own, flo, fhi, nlo, nhi)
+    place(slice(0, 8), yown, yfar.at[0:4], yfar.at[4:8], ynear.at[0:10], ynear.at[10:20])
+    place(slice(24, 32), zown, zfar.at[0:4], zfar.at[4:8], znear.at[0:10], znear.at[10:20])
     for i in range(16):
         v = a[i]
         c0[i] = v - r[i] / ((1.5 + mass) / damping + (mass / damping) * (v * v))
@@ -107,13 +118,18 @@
         for k in range(2):
             wide[i, k, pl.ds(0, 32, stride=2)] = even[:, 128 * k : 128 * k + 128]
             wide[i, k, pl.ds(1, 32, stride=2)] = odd[:, 128 * k : 128 * k + 128]
+    for j in range(4):
+        at, lane = 8 + 16 * (j // 2), 128 * (j % 2)
+        corrected[0, at : at + 16, lane : lane + 128] = nlo[10 + j]
+        corrected[7, at : at + 16, lane : lane + 128] = nhi[10 + j]
     for i in range(8):
         near = i // 2 + 1
         beside_layer = near - 1 if i % 2 == 0 else near + 1
+        before = corrected.at[i] if i in (0, 7) else smooth.at[i - 1]
         for k in range(2):
             lanes = slice(128 * k, 128 * k + 128)
             change = 0.75 * wide[near, k, 8:56] + 0.25 * wide[beside_layer, k, 8:56]
-            corrected[i, :, lanes] = smooth[i, :, lanes] + change
+            corrected[i, :, lanes] = before[:, lanes] + change
     for i in range(6):
         post[i] = jacobi(corrected[i + 1], corrected[i], corrected[i + 2], dens[i], 1.0)
     for i in range(4):
@@ -138,36 +154,38 @@
     return lax.ppermute(values, axis, [(i, (i + step) % count) for i in range(count)])
 
 
+def rows_from_sides(values):
+    height = values.shape[1]
+    return send(values[:, height - 8 :], "gy", 1), send(values[:, :8], "gy", -1)
+
+
 def body(density, field):
-    xlo = send(jnp.concatenate([field, density[1:4]], 0), "gx", 1)
-    xhi = send(jnp.concatenate([field, density[0:3]], 0), "gx", -1)
+    xlo = send(jnp.concatenate([field[1:4], density[2:4]], 0), "gx", 1)
+    xhi = send(jnp.concatenate([field[0:3], density[0:2]], 0), "gx", -1)
     ylo = send(jnp.concatenate([field[:, 28:32], density[:, 28:32]], 1), "gy", 1)
     yhi = send(jnp.concatenate([field[:, 0:4], density[:, 0:4]], 1), "gy", -1)
+    xlo, xhi, ylo, yhi = lax.optimization_barrier((xlo, xhi, ylo, yhi))
     clo = send(jnp.concatenate([xlo[:, 28:32], xhi[:, 28:32]], 0), "gy", 1)
     chi = send(jnp.concatenate([xlo[:, 0:4], xhi[:, 0:4]], 0), "gy", -1)
-    smooth, dens, own = call(
+    smooth, dens, own, up, down = call(
         fine_kernel,
-        [(8, 48, 256), (6, 48, 256), (4, 16, 128)],
-        [(12, 48, 256), (10, 48, 256), (10, 48, 256), (4, 2, 48, 128), (64, 256)],
+        [(6, 48, 256), (6, 48, 256), (4, 16, 128), (4, 16, 128), (4, 16, 128)],
+        [(10, 48, 256), (8, 48, 256), (8, 48, 256), (4, 2, 48, 128), (64, 256)],
         field, density, xlo, xhi, ylo, yhi, clo, chi,
     )
-    xlo = send(own, "gx", 1)
-    xhi = send(own, "gx", -1)
-    ylo = send(own[:, 8:16], "gy", 1)
-    yhi = send(own[:, 0:8], "gy", -1)
-    flo = send(jnp.concatenate([xlo[1:2], own[0:2], xhi[0:2], xlo[3:4], own[2:4], xhi[2:4]], 0), "gx", 3)
-    fhi = send(jnp.concatenate([xlo[0:2], own[0:2], xhi[0:1], xlo[2:4], own[2:4], xhi[2:3]], 0), "gx", -3)
-    near = jnp.concatenate([xlo, xhi], 0)
-    clo = send(near[:, 8:16], "gy", 1)
-    chi = send(near[:, 0:8], "gy", -1)
-    far = jnp.concatenate([flo, fhi], 0)
-    glo = send(far[:, 8:16], "gy", 1)
-    ghi = send(far[:, 0:8], "gy", -1)
+    flo, fhi = send(own, "gx", 3), send(own, "gx", -3)
+    yown, zown = rows_from_sides(own)
+    flo, fhi, yown, zown = lax.optimization_barrier((flo, fhi, yown, zown))
+    nlo = send(jnp.concatenate([flo[1:2], flo[3:4], own, fhi, up], 0), "gx", 1)
+    nhi = send(jnp.concatenate([fhi[0:1], fhi[2:3], own, flo, down], 0), "gx", -1)
+    yfar, zfar = rows_from_sides(jnp.concatenate([flo, fhi], 0))
+    nlo, nhi, yfar, zfar = lax.optimization_barrier((nlo, nhi, yfar, zfar))
+    ynear, znear = rows_from_sides(jnp.concatenate([nlo[0:10], nhi[0:10]], 0))
     (out,) = call(
         coarse_kernel,
         [(4, 32, 256)],
-        [(16, 32, 128), (16, 32, 128), (16, 32, 128), (16, 32, 128), (16, 32, 128), (6, 2, 64, 128), (8, 48, 256), (6, 48, 256)],
-        smooth, dens, own, xlo, xhi, flo, fhi, ylo, yhi, clo, chi, glo, ghi,
+        [(16, 32, 128)] * 5 + [(6, 2, 64, 128), (8, 48, 256), (6, 48, 256)],
+        smooth, dens, own, flo, fhi, nlo, nhi, yown, yfar, ynear, zown, zfar, znear,
     )
     return out
 

time: 76.2 us -> 74.1 us (0.972)
  the two profiles are of different devices: /device:TPU:71 before, /device:TPU:1 now
where the time goes in v2:
time: 74.1 us; the launch traced here: 73.8 us
  starting transfers between devices  52.6 us (71%)
  waiting for transfers between devices  17 us (23%)
  Pallas kernels  2.78 us (4%)
  local copies, waits for them, and re-layouts  1.08 us (1%)
    ppermute x16, starting transfers between devices, send(): lax.ppermute(values, axis, [(i, (i + step) % count) for i in range(count)])  52.6 us
    ppermute x16, waiting for transfers between devices, send(): lax.ppermute(values, axis, [(i, (i + step) % count) for i in range(count)])  17 us
    pallas_call x2, Pallas kernels, call(): pl.pallas_call(kernel, out_shape=shapes, in_specs=[vmem] * len(args), out...  2.78 us
  transfers between devices with their start and end apart: 16, of which 12 were waited for; matrix products, arithmetic and copies ran while one was open for 0% of the time, Pallas kernels for 0%

profile of v2, /device:TPU:1, one launch (start us, length us, event | category | flops | bytes accessed | tf_op | source)
XLA Modules:
  0.0 73.8 jit_solution(16969942511261873812)
XLA Ops:
  0.0 0.0 copy-start
  0.0 0.9 %fusion.6 = (f32[2,32,256]{2,1,0:T(8,128)S(1)}, f32[2,32,256]{2,1,0:T(8,128)S(1)}) fusion(f32[4,32,256]{2,1,0:T(8,128)} %density.1), kind=kLoop, calls=%fused_computation.27 | loop fusion | bytes 262144 | tf_op jit(solution)/shard_map/slice | solution.py:164
  0.9 0.0 copy-done
  1.0 4.4 %collective-permute-start = (f32[5,32,256]{2,1,0:T(8,128)S(1)}, f32[5,32,256]{2,1,0:T(8,128)S(1)}, u32[]{:S(2)}, u32[]{:S(2)}) collective-permute-start(f32[5,32,256]{2,1,0:T(8,128)S(1)} %pad_maximum_fusion), channel_id=1, source_target_pairs={{0,8},{8,16},{16,24},{24,32},{32,40},{40,48},{48,56},{56,64},{64,7... | collective-permute-start | bytes 491528 | tf_op jit(solution)/shard_map/ppermute | solution.py:154
  5.4 0.0 copy-start.1
  5.4 19.4 %collective-permute-start.1 = (f32[5,32,256]{2,1,0:T(8,128)S(1)}, f32[5,32,256]{2,1,0:T(8,128)S(1)}, u32[]{:S(2)}, u32[]{:S(2)}) collective-permute-start(f32[5,32,256]{2,1,0:T(8,128)S(1)} %pad_maximum_fusion.1), channel_id=1, source_target_pairs={{0,1016},{8,0},{16,8},{24,16},{32,24},{40,32},{48,40},{56,48},{64,... | collective-permute-start | bytes 491528 | tf_op jit(solution)/shard_map/ppermute | solution.py:154
  24.8 0.0 copy-done.1
  24.8 2.1 %collective-permute-start.2 = (f32[4,8,256]{2,1,0:T(8,128)S(1)}, f32[4,8,256]{2,1,0:T(8,128)S(1)}, u32[]{:S(2)}, u32[]{:S(2)}) collective-permute-start(f32[4,8,256]{2,1,0:T(8,128)S(1)} %pad_maximum_fusion.5), channel_id=1, source_target_pairs={{0,1},{1,2},{2,3},{3,4},{4,5},{5,6},{6,7},{7,0},{8,9},{9,10},{10,1... | collective-permute-start | bytes 98312 | tf_op jit(solution)/shard_map/ppermute | solution.py:154
  26.9 0.0 collective-permute-start.3
  26.9 1.0 %collective-permute-done.2.ylo = f32[4,8,256]{2,1,0:T(8,128)S(1)} collective-permute-done((f32[4,8,256]{2,1,0:T(8,128)S(1)}, f32[4,8,256]{2,1,0:T(8,128)S(1)}, u32[]{:S(2)}, u32[]{:S(2)}) %collective-permute-start.2) | collective-permute-done | bytes 32800 | tf_op jit(solution)/shard_map/ppermute | solution.py:154
  27.9 2.3 %collective-permute-done.3.yhi = f32[4,8,256]{2,1,0:T(8,128)S(1)} collective-permute-done((f32[4,8,256]{2,1,0:T(8,128)S(1)}, f32[4,8,256]{2,1,0:T(8,128)S(1)}, u32[]{:S(2)}, u32[]{:S(2)}) %collective-permute-start.3) | collective-permute-done | bytes 32800 | tf_op jit(solution)/shard_map/ppermute | solution.py:154
  30.3 0.0 collective-permute-done.xlo
  30.3 0.0 collective-permute-done.1.xhi
  30.3 0.0 collective-permute-start.4
  30.4 0.5 collective-permute-start.5
  30.9 0.7 collective-permute-done.4.clo
  31.6 2.5 %collective-permute-done.5.chi = f32[10,4,256]{2,1,0:T(4,128)S(1)} collective-permute-done((f32[10,4,256]{2,1,0:T(4,128)S(1)}, f32[10,4,256]{2,1,0:T(4,128)S(1)}, u32[]{:S(2)}, u32[]{:S(2)}) %collective-permute-start.5) | collective-permute-done | bytes 40992 | tf_op jit(solution)/shard_map/ppermute | solution.py:154
  34.1 0.8 %shard_map.28 = (f32[6,48,256]{2,1,0:T(8,128)S(1)}, f32[6,48,256]{2,1,0:T(8,128)S(1)}, f32[4,16,128]{2,1,0:T(8,128)S(1)}, f32[4,16,128]{2,1,0:T(8,128)S(1)}, f32[4,16,128]{2,1,0:T(8,128)S(1)}) custom-call(f32[4,32,256]{2,1,0:T(8,128)S(1)} %copy-done, f32[4,32,256]{2,1,0:T(8,128)S(1)} %copy-done.1, f32[5,32,256]{2,1,0:T(8,128)S(1)} %collective-permute-done.xlo, ...), custom_call_target="tpu_custom_call" | custom-call | tf_op jit(solution)/shard_map/pallas_call | solution.py:142
  34.9 5.4 %collective-permute-start.7 = (f32[4,16,128]{2,1,0:T(8,128)S(1)}, f32[4,16,128]{2,1,0:T(8,128)S(1)}, u32[]{:S(2)}, u32[]{:S(2)}) collective-permute-start(f32[4,16,128]{2,1,0:T(8,128)S(1)} %get-tuple-element.28.own), channel_id=1, source_target_pairs={{0,1000},{8,1008},{16,1016},{24,0},{32,8},{40,16},{48,24},{56,32},... | collective-permute-start | bytes 98312 | tf_op jit(solution)/shard_map/ppermute | solution.py:154
  40.4 1.9 %collective-permute-start.6 = (f32[4,16,128]{2,1,0:T(8,128)S(1)}, f32[4,16,128]{2,1,0:T(8,128)S(1)}, u32[]{:S(2)}, u32[]{:S(2)}) collective-permute-start(f32[4,16,128]{2,1,0:T(8,128)S(1)} %get-tuple-element.28.own), channel_id=1, source_target_pairs={{0,24},{8,32},{16,40},{24,48},{32,56},{40,64},{48,72},{56,80},{64,... | collective-permute-start | bytes 98312 | tf_op jit(solution)/shard_map/ppermute | solution.py:154
  42.3 1.3 %collective-permute-start.9 = (f32[4,8,128]{2,1,0:T(8,128)S(1)}, f32[4,8,128]{2,1,0:T(8,128)S(1)}, u32[]{:S(2)}, u32[]{:S(2)}) collective-permute-start(f32[4,8,128]{2,1,0:T(8,128)S(1)} %get-tuple-element.61), channel_id=1, source_target_pairs={{0,7},{1,0},{2,1},{3,2},{4,3},{5,4},{6,5},{7,6},{8,15},{9,8},{10,9... | collective-permute-start | bytes 49160 | tf_op jit(solution)/shard_map/ppermute | solution.py:154
  43.6 0.4 collective-permute-start.8
  44.1 1.4 %collective-permute-done.9.zown = f32[4,8,128]{2,1,0:T(8,128)S(1)} collective-permute-done((f32[4,8,128]{2,1,0:T(8,128)S(1)}, f32[4,8,128]{2,1,0:T(8,128)S(1)}, u32[]{:S(2)}, u32[]{:S(2)}) %collective-permute-start.9) | collective-permute-done | bytes 16416 | tf_op jit(solution)/shard_map/ppermute | solution.py:154
  45.5 1.2 %collective-permute-done.8.yown = f32[4,8,128]{2,1,0:T(8,128)S(1)} collective-permute-done((f32[4,8,128]{2,1,0:T(8,128)S(1)}, f32[4,8,128]{2,1,0:T(8,128)S(1)}, u32[]{:S(2)}, u32[]{:S(2)}) %collective-permute-start.8) | collective-permute-done | bytes 16416 | tf_op jit(solution)/shard_map/ppermute | solution.py:154
  46.7 0.0 collective-permute-done.7.fhi
  46.7 3.4 %collective-permute-done.6.flo = f32[4,16,128]{2,1,0:T(8,128)S(1)} collective-permute-done((f32[4,16,128]{2,1,0:T(8,128)S(1)}, f32[4,16,128]{2,1,0:T(8,128)S(1)}, u32[]{:S(2)}, u32[]{:S(2)}) %collective-permute-start.6) | collective-permute-done | bytes 32800 | tf_op jit(solution)/shard_map/ppermute | solution.py:154
  50.2 6.1 %collective-permute-start.11 = (f32[14,16,128]{2,1,0:T(8,128)S(1)}, f32[14,16,128]{2,1,0:T(8,128)S(1)}, u32[]{:S(2)}, u32[]{:S(2)}) collective-permute-start(f32[14,16,128]{2,1,0:T(8,128)S(1)} %constant_dynamic-update-slice_fusion.5), channel_id=1, source_target_pairs={{0,1016},{8,0},{16,8},{24,16},{32,24},{40,32},{48,40},{56,48},{64,... | collective-permute-start | bytes 344072 | tf_op jit(solution)/shard_map/ppermute | solution.py:154
  56.4 1.9 %collective-permute-start.10 = (f32[14,16,128]{2,1,0:T(8,128)S(1)}, f32[14,16,128]{2,1,0:T(8,128)S(1)}, u32[]{:S(2)}, u32[]{:S(2)}) collective-permute-start(f32[14,16,128]{2,1,0:T(8,128)S(1)} %constant_dynamic-update-slice_fusion), channel_id=1, source_target_pairs={{0,8},{8,16},{16,24},{24,32},{32,40},{40,48},{48,56},{56,64},{64,7... | collective-permute-start | bytes 344072 | tf_op jit(solution)/shard_map/ppermute | solution.py:154
  58.3 4.0 %collective-permute-start.13 = (f32[8,8,128]{2,1,0:T(8,128)S(1)}, f32[8,8,128]{2,1,0:T(8,128)S(1)}, u32[]{:S(2)}, u32[]{:S(2)}) collective-permute-start(f32[8,8,128]{2,1,0:T(8,128)S(1)} %get-tuple-element.53), channel_id=1, source_target_pairs={{0,7},{1,0},{2,1},{3,2},{4,3},{5,4},{6,5},{7,6},{8,15},{9,8},{10,9... | collective-permute-start | bytes 98312 | tf_op jit(solution)/shard_map/ppermute | solution.py:154
  62.3 0.0 collective-permute-start.12
  62.3 0.9 %collective-permute-done.13.zfar = f32[8,8,128]{2,1,0:T(8,128)S(1)} collective-permute-done((f32[8,8,128]{2,1,0:T(8,128)S(1)}, f32[8,8,128]{2,1,0:T(8,128)S(1)}, u32[]{:S(2)}, u32[]{:S(2)}) %collective-permute-start.13) | collective-permute-done | bytes 32800 | tf_op jit(solution)/shard_map/ppermute | solution.py:154
  63.2 0.3 collective-permute-done.12.yfar
  63.5 0.0 collective-permute-done.11.nhi
  63.5 1.7 %collective-permute-done.10.nlo = f32[14,16,128]{2,1,0:T(8,128)S(1)} collective-permute-done((f32[14,16,128]{2,1,0:T(8,128)S(1)}, f32[14,16,128]{2,1,0:T(8,128)S(1)}, u32[]{:S(2)}, u32[]{:S(2)}) %collective-permute-start.10) | collective-permute-done | bytes 114720 | tf_op jit(solution)/shard_map/ppermute | solution.py:154
  65.3 5.1 %collective-permute-start.15 = (f32[20,8,128]{2,1,0:T(8,128)S(1)}, f32[20,8,128]{2,1,0:T(8,128)S(1)}, u32[]{:S(2)}, u32[]{:S(2)}) collective-permute-start(f32[20,8,128]{2,1,0:T(8,128)S(1)} %get-tuple-element.39), channel_id=1, source_target_pairs={{0,7},{1,0},{2,1},{3,2},{4,3},{5,4},{6,5},{7,6},{8,15},{9,8},{10,9... | collective-permute-start | bytes 245768 | tf_op jit(solution)/shard_map/ppermute | solution.py:154
  70.4 0.0 collective-permute-start.14
  70.4 0.9 %collective-permute-done.15.znear = f32[20,8,128]{2,1,0:T(8,128)S(1)} collective-permute-done((f32[20,8,128]{2,1,0:T(8,128)S(1)}, f32[20,8,128]{2,1,0:T(8,128)S(1)}, u32[]{:S(2)}, u32[]{:S(2)}) %collective-permute-start.15) | collective-permute-done | bytes 81952 | tf_op jit(solution)/shard_map/ppermute | solution.py:154
  71.3 0.6 collective-permute-done.14.ynear
  71.9 1.9 %shard_map.29 = f32[4,32,256]{2,1,0:T(8,128)} custom-call(f32[6,48,256]{2,1,0:T(8,128)S(1)} %get-tuple-element.26.smooth, f32[6,48,256]{2,1,0:T(8,128)S(1)} %get-tuple-element.27.dens, f32[4,16,128]{2,1,0:T(8,128)S(1)} %get-tuple-element.28.own, f32[4,16,128]{2,1,0:T(8,128)S(1)} %collective-permute-done.6.flo, f32[4,16,128]{2,1,0:T(8,128)S(1)} %collective-permute-done.7.fhi, ...), custom_call_target="tpu_custom_call" | custom-call | tf_op jit(solution)/shard_map/pallas_call | solution.py:142
  (24 shorter events, 0.2 us)
Async XLA Ops:
  0.0 1.0 %copy-start = (f32[4,32,256]{2,1,0:T(8,128)S(1)}, f32[4,32,256]{2,1,0:T(8,128)}, u32[]{:S(2)}) copy-start(f32[4,32,256]{2,1,0:T(8,128)} %field.1) | copy-start | bytes 393220
  1.0 29.3 %collective-permute-start = (f32[5,32,256]{2,1,0:T(8,128)S(1)}, f32[5,32,256]{2,1,0:T(8,128)S(1)}, u32[]{:S(2)}, u32[]{:S(2)}) collective-permute-start(f32[5,32,256]{2,1,0:T(8,128)S(1)} %pad_maximum_fusion), channel_id=1, source_target_pairs={{0,8},{8,16},{16,24},{24,32},{32,40},{40,48},{48,56},{56,64},{64,7... | collective-permute-start | bytes 491528 | tf_op jit(solution)/shard_map/ppermute | solution.py:154
  5.4 19.4 %copy-start.1 = (f32[4,32,256]{2,1,0:T(8,128)S(1)}, f32[4,32,256]{2,1,0:T(8,128)}, u32[]{:S(2)}) copy-start(f32[4,32,256]{2,1,0:T(8,128)} %density.1) | copy-start | bytes 393220
  5.4 24.8 %collective-permute-start.1 = (f32[5,32,256]{2,1,0:T(8,128)S(1)}, f32[5,32,256]{2,1,0:T(8,128)S(1)}, u32[]{:S(2)}, u32[]{:S(2)}) collective-permute-start(f32[5,32,256]{2,1,0:T(8,128)S(1)} %pad_maximum_fusion.1), channel_id=1, source_target_pairs={{0,1016},{8,0},{16,8},{24,16},{32,24},{40,32},{48,40},{56,48},{64,... | collective-permute-start | bytes 491528 | tf_op jit(solution)/shard_map/ppermute | solution.py:154
  24.8 3.1 %collective-permute-start.2 = (f32[4,8,256]{2,1,0:T(8,128)S(1)}, f32[4,8,256]{2,1,0:T(8,128)S(1)}, u32[]{:S(2)}, u32[]{:S(2)}) collective-permute-start(f32[4,8,256]{2,1,0:T(8,128)S(1)} %pad_maximum_fusion.5), channel_id=1, source_target_pairs={{0,1},{1,2},{2,3},{3,4},{4,5},{5,6},{6,7},{7,0},{8,9},{9,10},{10,1... | collective-permute-start | bytes 98312 | tf_op jit(solution)/shard_map/ppermute | solution.py:154
  26.9 3.4 %collective-permute-start.3 = (f32[4,8,256]{2,1,0:T(8,128)S(1)}, f32[4,8,256]{2,1,0:T(8,128)S(1)}, u32[]{:S(2)}, u32[]{:S(2)}) collective-permute-start(f32[4,8,256]{2,1,0:T(8,128)S(1)} %pad_maximum_fusion.6), channel_id=1, source_target_pairs={{0,7},{1,0},{2,1},{3,2},{4,3},{5,4},{6,5},{7,6},{8,15},{9,8},{10,9... | collective-permute-start | bytes 98312 | tf_op jit(solution)/shard_map/ppermute | solution.py:154
  30.3 1.2 %collective-permute-start.4 = (f32[10,4,256]{2,1,0:T(4,128)S(1)}, f32[10,4,256]{2,1,0:T(4,128)S(1)}, u32[]{:S(2)}, u32[]{:S(2)}) collective-permute-start(f32[10,4,256]{2,1,0:T(4,128)S(1)} %pad_maximum_fusion.3), channel_id=1, source_target_pairs={{0,1},{1,2},{2,3},{3,4},{4,5},{5,6},{6,7},{7,0},{8,9},{9,10},{10,1... | collective-permute-start | bytes 122888 | tf_op jit(solution)/shard_map/ppermute | solution.py:154
  30.4 3.7 %collective-permute-start.5 = (f32[10,4,256]{2,1,0:T(4,128)S(1)}, f32[10,4,256]{2,1,0:T(4,128)S(1)}, u32[]{:S(2)}, u32[]{:S(2)}) collective-permute-start(f32[10,4,256]{2,1,0:T(4,128)S(1)} %pad_maximum_fusion.4), channel_id=1, source_target_pairs={{0,7},{1,0},{2,1},{3,2},{4,3},{5,4},{6,5},{7,6},{8,15},{9,8},{10,9... | collective-permute-start | bytes 122888 | tf_op jit(solution)/shard_map/ppermute | solution.py:154
  34.9 11.8 %collective-permute-start.7 = (f32[4,16,128]{2,1,0:T(8,128)S(1)}, f32[4,16,128]{2,1,0:T(8,128)S(1)}, u32[]{:S(2)}, u32[]{:S(2)}) collective-permute-start(f32[4,16,128]{2,1,0:T(8,128)S(1)} %get-tuple-element.28.own), channel_id=1, source_target_pairs={{0,1000},{8,1008},{16,1016},{24,0},{32,8},{40,16},{48,24},{56,32},... | collective-permute-start | bytes 98312 | tf_op jit(solution)/shard_map/ppermute | solution.py:154
  40.4 9.8 %collective-permute-start.6 = (f32[4,16,128]{2,1,0:T(8,128)S(1)}, f32[4,16,128]{2,1,0:T(8,128)S(1)}, u32[]{:S(2)}, u32[]{:S(2)}) collective-permute-start(f32[4,16,128]{2,1,0:T(8,128)S(1)} %get-tuple-element.28.own), channel_id=1, source_target_pairs={{0,24},{8,32},{16,40},{24,48},{32,56},{40,64},{48,72},{56,80},{64,... | collective-permute-start | bytes 98312 | tf_op jit(solution)/shard_map/ppermute | solution.py:154
  42.3 3.2 %collective-permute-start.9 = (f32[4,8,128]{2,1,0:T(8,128)S(1)}, f32[4,8,128]{2,1,0:T(8,128)S(1)}, u32[]{:S(2)}, u32[]{:S(2)}) collective-permute-start(f32[4,8,128]{2,1,0:T(8,128)S(1)} %get-tuple-element.61), channel_id=1, source_target_pairs={{0,7},{1,0},{2,1},{3,2},{4,3},{5,4},{6,5},{7,6},{8,15},{9,8},{10,9... | collective-permute-start | bytes 49160 | tf_op jit(solution)/shard_map/ppermute | solution.py:154
  43.6 3.1 %collective-permute-start.8 = (f32[4,8,128]{2,1,0:T(8,128)S(1)}, f32[4,8,128]{2,1,0:T(8,128)S(1)}, u32[]{:S(2)}, u32[]{:S(2)}) collective-permute-start(f32[4,8,128]{2,1,0:T(8,128)S(1)} %get-tuple-element.62), channel_id=1, source_target_pairs={{0,1},{1,2},{2,3},{3,4},{4,5},{5,6},{6,7},{7,0},{8,9},{9,10},{10,1... | collective-permute-start | bytes 49160 | tf_op jit(solution)/shard_map/ppermute | solution.py:154
  50.2 13.3 %collective-permute-start.11 = (f32[14,16,128]{2,1,0:T(8,128)S(1)}, f32[14,16,128]{2,1,0:T(8,128)S(1)}, u32[]{:S(2)}, u32[]{:S(2)}) collective-permute-start(f32[14,16,128]{2,1,0:T(8,128)S(1)} %constant_dynamic-update-slice_fusion.5), channel_id=1, source_target_pairs={{0,1016},{8,0},{16,8},{24,16},{32,24},{40,32},{48,40},{56,48},{64,... | collective-permute-start | bytes 344072 | tf_op jit(solution)/shard_map/ppermute | solution.py:154
  56.4 8.9 %collective-permute-start.10 = (f32[14,16,128]{2,1,0:T(8,128)S(1)}, f32[14,16,128]{2,1,0:T(8,128)S(1)}, u32[]{:S(2)}, u32[]{:S(2)}) collective-permute-start(f32[14,16,128]{2,1,0:T(8,128)S(1)} %constant_dynamic-update-slice_fusion), channel_id=1, source_target_pairs={{0,8},{8,16},{16,24},{24,32},{32,40},{40,48},{48,56},{56,64},{64,7... | collective-permute-start | bytes 344072 | tf_op jit(solution)/shard_map/ppermute | solution.py:154
  58.3 4.8 %collective-permute-start.13 = (f32[8,8,128]{2,1,0:T(8,128)S(1)}, f32[8,8,128]{2,1,0:T(8,128)S(1)}, u32[]{:S(2)}, u32[]{:S(2)}) collective-permute-start(f32[8,8,128]{2,1,0:T(8,128)S(1)} %get-tuple-element.53), channel_id=1, source_target_pairs={{0,7},{1,0},{2,1},{3,2},{4,3},{5,4},{6,5},{7,6},{8,15},{9,8},{10,9... | collective-permute-start | bytes 98312 | tf_op jit(solution)/shard_map/ppermute | solution.py:154
  62.3 1.2 %collective-permute-start.12 = (f32[8,8,128]{2,1,0:T(8,128)S(1)}, f32[8,8,128]{2,1,0:T(8,128)S(1)}, u32[]{:S(2)}, u32[]{:S(2)}) collective-permute-start(f32[8,8,128]{2,1,0:T(8,128)S(1)} %get-tuple-element.54), channel_id=1, source_target_pairs={{0,1},{1,2},{2,3},{3,4},{4,5},{5,6},{6,7},{7,0},{8,9},{9,10},{10,1... | collective-permute-start | bytes 98312 | tf_op jit(solution)/shard_map/ppermute | solution.py:154
  65.3 6.1 %collective-permute-start.15 = (f32[20,8,128]{2,1,0:T(8,128)S(1)}, f32[20,8,128]{2,1,0:T(8,128)S(1)}, u32[]{:S(2)}, u32[]{:S(2)}) collective-permute-start(f32[20,8,128]{2,1,0:T(8,128)S(1)} %get-tuple-element.39), channel_id=1, source_target_pairs={{0,7},{1,0},{2,1},{3,2},{4,3},{5,4},{6,5},{7,6},{8,15},{9,8},{10,9... | collective-permute-start | bytes 245768 | tf_op jit(solution)/shard_map/ppermute | solution.py:154
  70.4 1.5 %collective-permute-start.14 = (f32[20,8,128]{2,1,0:T(8,128)S(1)}, f32[20,8,128]{2,1,0:T(8,128)S(1)}, u32[]{:S(2)}, u32[]{:S(2)}) collective-permute-start(f32[20,8,128]{2,1,0:T(8,128)S(1)} %get-tuple-element.40), channel_id=1, source_target_pairs={{0,1},{1,2},{2,3},{3,4},{4,5},{5,6},{6,7},{7,0},{8,9},{9,10},{10,1... | collective-permute-start | bytes 245768 | tf_op jit(solution)/shard_map/ppermute | solution.py:154

commit v3 on v2

--- a/solution.py
+++ b/solution.py
@@ -35,20 +35,20 @@
     return total + jnp.dot(high, weights, preferred_element_type=jnp.float32)
 
 
-def fine_kernel(field, density, xlo, xhi, ylo, yhi, clo, chi, smooth, dens, coarse, up, down, f, d, s1, pair, rows):
+def fine_kernel(field, density, xlo, xhi, clo, chi, smooth, dens, coarse, up, down, f, d, s1, pair, rows):
     f[0:3, 8:40] = xlo[0:3]
     f[3:7, 8:40] = field[...]
     f[7:10, 8:40] = xhi[0:3]
     d[0:2, 8:40] = xlo[3:5]
     d[2:6, 8:40] = density[...]
     d[6:8, 8:40] = xhi[3:5]
-    for corner, side, at in ((clo, ylo, 4), (chi, yhi, 40)):
-        f[0:3, at : at + 4] = corner[0:3]
-        f[3:7, at : at + 4] = side[:, 0:4]
-        f[7:10, at : at + 4] = corner[5:8]
-        d[0:2, at : at + 4] = corner[3:5]
-        d[2:6, at : at + 4] = side[:, 4:8]
-        d[6:8, at : at + 4] = corner[8:10]
+    for side, at in ((clo, 4), (chi, 40)):
+        f[0:3, at : at + 4] = side[0:3]
+        f[3:7, at : at + 4] = side[10:14]
+        f[7:10, at : at + 4] = side[5:8]
+        d[0:2, at : at + 4] = side[3:5]
+        d[2:6, at : at + 4] = side[14:18]
+        d[6:8, at : at + 4] = side[8:10]
     for i in range(8):
         s1[i] = jacobi(f[i + 1], f[i], f[i + 2], d[i], 1.0)
     for i in range(6):
@@ -77,7 +77,7 @@
 
 
 def coarse_kernel(
-    smooth, dens, own, flo, fhi, nlo, nhi, yown, yfar, ynear, zown, zfar, znear,
+    smooth, dens, own, flo, fhi, nlo, nhi, yrows, zrows,
     out, a, r, g, c0, c1, wide, corrected, post,
 ):
     def place(rows, mine, far_low, far_high, low, high):
@@ -93,8 +93,8 @@
             ref[15:16, rows] = high[at : at + 1]
 
     place(slice(8, 24), own, flo, fhi, nlo, nhi)
-    place(slice(0, 8), yown, yfar.at[0:4], yfar.at[4:8], ynear.at[0:10], ynear.at[10:20])
-    place(slice(24, 32), zown, zfar.at[0:4], zfar.at[4:8], znear.at[0:10], znear.at[10:20])
+    for rows, side in ((slice(0, 8), yrows), (slice(24, 32), zrows)):
+        place(rows, side.at[0:4], side.at[4:8], side.at[8:12], side.at[12:22], side.at[22:32])
     for i in range(16):
         v = a[i]
         c0[i] = v - r[i] / ((1.5 + mass) / damping + (mass / damping) * (v * v))
@@ -154,38 +154,32 @@
     return lax.ppermute(values, axis, [(i, (i + step) % count) for i in range(count)])
 
 
-def rows_from_sides(values):
-    height = values.shape[1]
-    return send(values[:, height - 8 :], "gy", 1), send(values[:, :8], "gy", -1)
+def rows_from_sides(pieces):
+    last = jnp.concatenate([piece[:, 8:16] for piece in pieces], 0)
+    first = jnp.concatenate([piece[:, 0:8] for piece in pieces], 0)
+    return send(last, "gy", 1), send(first, "gy", -1)
 
 
 def body(density, field):
     xlo = send(jnp.concatenate([field[1:4], density[2:4]], 0), "gx", 1)
     xhi = send(jnp.concatenate([field[0:3], density[0:2]], 0), "gx", -1)
-    ylo = send(jnp.concatenate([field[:, 28:32], density[:, 28:32]], 1), "gy", 1)
-    yhi = send(jnp.concatenate([field[:, 0:4], density[:, 0:4]], 1), "gy", -1)
-    xlo, xhi, ylo, yhi = lax.optimization_barrier((xlo, xhi, ylo, yhi))
-    clo = send(jnp.concatenate([xlo[:, 28:32], xhi[:, 28:32]], 0), "gy", 1)
-    chi = send(jnp.concatenate([xlo[:, 0:4], xhi[:, 0:4]], 0), "gy", -1)
+    clo = send(jnp.concatenate([xlo[:, 28:32], xhi[:, 28:32], field[:, 28:32], density[:, 28:32]], 0), "gy", 1)
+    chi = send(jnp.concatenate([xlo[:, 0:4], xhi[:, 0:4], field[:, 0:4], density[:, 0:4]], 0), "gy", -1)
     smooth, dens, own, up, down = call(
         fine_kernel,
         [(6, 48, 256), (6, 48, 256), (4, 16, 128), (4, 16, 128), (4, 16, 128)],
         [(10, 48, 256), (8, 48, 256), (8, 48, 256), (4, 2, 48, 128), (64, 256)],
-        field, density, xlo, xhi, ylo, yhi, clo, chi,
+        field, density, xlo, xhi, clo, chi,
     )
     flo, fhi = send(own, "gx", 3), send(own, "gx", -3)
-    yown, zown = rows_from_sides(own)
-    flo, fhi, yown, zown = lax.optimization_barrier((flo, fhi, yown, zown))
     nlo = send(jnp.concatenate([flo[1:2], flo[3:4], own, fhi, up], 0), "gx", 1)
     nhi = send(jnp.concatenate([fhi[0:1], fhi[2:3], own, flo, down], 0), "gx", -1)
-    yfar, zfar = rows_from_sides(jnp.concatenate([flo, fhi], 0))
-    nlo, nhi, yfar, zfar = lax.optimization_barrier((nlo, nhi, yfar, zfar))
-    ynear, znear = rows_from_sides(jnp.concatenate([nlo[0:10], nhi[0:10]], 0))
+    yrows, zrows = rows_from_sides([own, flo, fhi, nlo[0:10], nhi[0:10]])
     (out,) = call(
         coarse_kernel,
         [(4, 32, 256)],
         [(16, 32, 128)] * 5 + [(6, 2, 64, 128), (8, 48, 256), (6, 48, 256)],
-        smooth, dens, own, flo, fhi, nlo, nhi, yown, yfar, ynear, zown, zfar, znear,
+        smooth, dens, own, flo, fhi, nlo, nhi, yrows, zrows,
     )
     return out
 

time: 74.1 us -> 70.6 us (0.953)
  the two profiles are of different devices: /device:TPU:1 before, /device:TPU:32 now
where the time goes in v3:
time: 70.6 us; the launch traced here: 70.3 us
  starting transfers between devices  42.1 us (60%)
  waiting for transfers between devices  24.1 us (34%)
  Pallas kernels  2.78 us (4%)
  local copies, waits for them, and re-layouts  1.08 us (2%)
    ppermute x10, starting transfers between devices, send(): lax.ppermute(values, axis, [(i, (i + step) % count) for i in range(count)])  42.1 us
    ppermute x10, waiting for transfers between devices, send(): lax.ppermute(values, axis, [(i, (i + step) % count) for i in range(count)])  24.1 us
    pallas_call x2, Pallas kernels, call(): pl.pallas_call(kernel, out_shape=shapes, in_specs=[vmem] * len(args), out...  2.78 us
  transfers between devices with their start and end apart: 10, of which 8 were waited for; matrix products, arithmetic and copies ran while one was open for 0% of the time, Pallas kernels for 0%

profile of v3, /device:TPU:32, one launch (start us, length us, event | category | flops | bytes accessed | tf_op | source)
XLA Modules:
  0.0 70.3 jit_solution(15181725942184040317)
XLA Ops:
  0.0 0.0 copy-start
  0.0 0.9 %fusion.5 = (f32[2,32,256]{2,1,0:T(8,128)S(1)}, f32[2,32,256]{2,1,0:T(8,128)S(1)}) fusion(f32[4,32,256]{2,1,0:T(8,128)} %density.1), kind=kLoop, calls=%fused_computation.29 | loop fusion | bytes 262144 | tf_op jit(solution)/shard_map/slice | solution.py:165
  0.9 0.0 copy-done
  1.0 3.8 %collective-permute-start = (f32[5,32,256]{2,1,0:T(8,128)S(1)}, f32[5,32,256]{2,1,0:T(8,128)S(1)}, u32[]{:S(2)}, u32[]{:S(2)}) collective-permute-start(f32[5,32,256]{2,1,0:T(8,128)S(1)} %pad_maximum_fusion), channel_id=1, source_target_pairs={{0,8},{8,16},{16,24},{24,32},{32,40},{40,48},{48,56},{56,64},{64,7... | collective-permute-start | bytes 491528 | tf_op jit(solution)/shard_map/ppermute | solution.py:154
  4.8 0.0 copy-start.1
  4.9 12.9 %collective-permute-start.1 = (f32[5,32,256]{2,1,0:T(8,128)S(1)}, f32[5,32,256]{2,1,0:T(8,128)S(1)}, u32[]{:S(2)}, u32[]{:S(2)}) collective-permute-start(f32[5,32,256]{2,1,0:T(8,128)S(1)} %pad_maximum_fusion.1), channel_id=1, source_target_pairs={{0,1016},{8,0},{16,8},{24,16},{32,24},{40,32},{48,40},{56,48},{64,... | collective-permute-start | bytes 491528 | tf_op jit(solution)/shard_map/ppermute | solution.py:154
  17.8 0.0 copy-done.1
  17.8 1.2 %collective-permute-done.xlo = f32[5,32,256]{2,1,0:T(8,128)S(1)} collective-permute-done((f32[5,32,256]{2,1,0:T(8,128)S(1)}, f32[5,32,256]{2,1,0:T(8,128)S(1)}, u32[]{:S(2)}, u32[]{:S(2)}) %collective-permute-start) | collective-permute-done | bytes 163872 | tf_op jit(solution)/shard_map/ppermute | solution.py:154
  19.0 1.6 %collective-permute-done.1.xhi = f32[5,32,256]{2,1,0:T(8,128)S(1)} collective-permute-done((f32[5,32,256]{2,1,0:T(8,128)S(1)}, f32[5,32,256]{2,1,0:T(8,128)S(1)}, u32[]{:S(2)}, u32[]{:S(2)}) %collective-permute-start.1) | collective-permute-done | bytes 163872 | tf_op jit(solution)/shard_map/ppermute | solution.py:154
  20.6 0.0 collective-permute-start.2
  20.7 2.9 %collective-permute-start.3 = (f32[18,4,256]{2,1,0:T(4,128)S(1)}, f32[18,4,256]{2,1,0:T(4,128)S(1)}, u32[]{:S(2)}, u32[]{:S(2)}) collective-permute-start(f32[18,4,256]{2,1,0:T(4,128)S(1)} %pad_maximum_fusion.3), channel_id=1, source_target_pairs={{0,7},{1,0},{2,1},{3,2},{4,3},{5,4},{6,5},{7,6},{8,15},{9,8},{10,9... | collective-permute-start | bytes 221192 | tf_op jit(solution)/shard_map/ppermute | solution.py:154
  23.6 2.0 %collective-permute-done.2.clo = f32[18,4,256]{2,1,0:T(4,128)S(1)} collective-permute-done((f32[18,4,256]{2,1,0:T(4,128)S(1)}, f32[18,4,256]{2,1,0:T(4,128)S(1)}, u32[]{:S(2)}, u32[]{:S(2)}) %collective-permute-start.2) | collective-permute-done | bytes 73760 | tf_op jit(solution)/shard_map/ppermute | solution.py:154
  25.6 0.0 collective-permute-done.3.chi
  25.6 0.8 %shard_map.28 = (f32[6,48,256]{2,1,0:T(8,128)S(1)}, f32[6,48,256]{2,1,0:T(8,128)S(1)}, f32[4,16,128]{2,1,0:T(8,128)S(1)}, f32[4,16,128]{2,1,0:T(8,128)S(1)}, f32[4,16,128]{2,1,0:T(8,128)S(1)}) custom-call(f32[4,32,256]{2,1,0:T(8,128)S(1)} %copy-done, f32[4,32,256]{2,1,0:T(8,128)S(1)} %copy-done.1, f32[5,32,256]{2,1,0:T(8,128)S(1)} %collective-permute-done.xlo, ...), custom_call_target="tpu_custom_call" | custom-call | tf_op jit(solution)/shard_map/pallas_call | solution.py:142
  26.5 12.2 %collective-permute-start.5 = (f32[4,16,128]{2,1,0:T(8,128)S(1)}, f32[4,16,128]{2,1,0:T(8,128)S(1)}, u32[]{:S(2)}, u32[]{:S(2)}) collective-permute-start(f32[4,16,128]{2,1,0:T(8,128)S(1)} %get-tuple-element.12.own), channel_id=1, source_target_pairs={{0,1000},{8,1008},{16,1016},{24,0},{32,8},{40,16},{48,24},{56,32},... | collective-permute-start | bytes 98312 | tf_op jit(solution)/shard_map/ppermute | solution.py:154
  38.7 1.9 %collective-permute-start.4 = (f32[4,16,128]{2,1,0:T(8,128)S(1)}, f32[4,16,128]{2,1,0:T(8,128)S(1)}, u32[]{:S(2)}, u32[]{:S(2)}) collective-permute-start(f32[4,16,128]{2,1,0:T(8,128)S(1)} %get-tuple-element.12.own), channel_id=1, source_target_pairs={{0,24},{8,32},{16,40},{24,48},{32,56},{40,64},{48,72},{56,80},{64,... | collective-permute-start | bytes 98312 | tf_op jit(solution)/shard_map/ppermute | solution.py:154
  40.6 9.0 %collective-permute-done.4.flo = f32[4,16,128]{2,1,0:T(8,128)S(1)} collective-permute-done((f32[4,16,128]{2,1,0:T(8,128)S(1)}, f32[4,16,128]{2,1,0:T(8,128)S(1)}, u32[]{:S(2)}, u32[]{:S(2)}) %collective-permute-start.4) | collective-permute-done | bytes 32800 | tf_op jit(solution)/shard_map/ppermute | solution.py:154
  49.6 0.0 collective-permute-done.5.fhi
  49.7 5.5 %collective-permute-start.6 = (f32[14,16,128]{2,1,0:T(8,128)S(1)}, f32[14,16,128]{2,1,0:T(8,128)S(1)}, u32[]{:S(2)}, u32[]{:S(2)}) collective-permute-start(f32[14,16,128]{2,1,0:T(8,128)S(1)} %constant_dynamic-update-slice_fusion), channel_id=1, source_target_pairs={{0,8},{8,16},{16,24},{24,32},{32,40},{40,48},{48,56},{56,64},{64,7... | collective-permute-start | bytes 344072 | tf_op jit(solution)/shard_map/ppermute | solution.py:154
  55.2 1.9 %collective-permute-start.7 = (f32[14,16,128]{2,1,0:T(8,128)S(1)}, f32[14,16,128]{2,1,0:T(8,128)S(1)}, u32[]{:S(2)}, u32[]{:S(2)}) collective-permute-start(f32[14,16,128]{2,1,0:T(8,128)S(1)} %constant_dynamic-update-slice_fusion.5), channel_id=1, source_target_pairs={{0,1016},{8,0},{16,8},{24,16},{32,24},{40,32},{48,40},{56,48},{64,... | collective-permute-start | bytes 344072 | tf_op jit(solution)/shard_map/ppermute | solution.py:154
  57.2 0.4 collective-permute-done.6.nlo
  57.5 4.4 %collective-permute-done.7.nhi = f32[14,16,128]{2,1,0:T(8,128)S(1)} collective-permute-done((f32[14,16,128]{2,1,0:T(8,128)S(1)}, f32[14,16,128]{2,1,0:T(8,128)S(1)}, u32[]{:S(2)}, u32[]{:S(2)}) %collective-permute-start.7) | collective-permute-done | bytes 114720 | tf_op jit(solution)/shard_map/ppermute | solution.py:154
  61.9 0.9 %collective-permute-start.9 = (f32[32,8,128]{2,1,0:T(8,128)S(1)}, f32[32,8,128]{2,1,0:T(8,128)S(1)}, u32[]{:S(2)}, u32[]{:S(2)}) collective-permute-start(f32[32,8,128]{2,1,0:T(8,128)S(1)} %get-tuple-element.27), channel_id=1, source_target_pairs={{0,7},{1,0},{2,1},{3,2},{4,3},{5,4},{6,5},{7,6},{8,15},{9,8},{10,9... | collective-permute-start | bytes 393224 | tf_op jit(solution)/shard_map/ppermute | solution.py:154
  62.8 0.0 collective-permute-start.8
  62.8 2.5 %collective-permute-done.9.zrows = f32[32,8,128]{2,1,0:T(8,128)S(1)} collective-permute-done((f32[32,8,128]{2,1,0:T(8,128)S(1)}, f32[32,8,128]{2,1,0:T(8,128)S(1)}, u32[]{:S(2)}, u32[]{:S(2)}) %collective-permute-start.9) | collective-permute-done | bytes 131104 | tf_op jit(solution)/shard_map/ppermute | solution.py:154
  65.3 3.1 %collective-permute-done.8.yrows = f32[32,8,128]{2,1,0:T(8,128)S(1)} collective-permute-done((f32[32,8,128]{2,1,0:T(8,128)S(1)}, f32[32,8,128]{2,1,0:T(8,128)S(1)}, u32[]{:S(2)}, u32[]{:S(2)}) %collective-permute-start.8) | collective-permute-done | bytes 131104 | tf_op jit(solution)/shard_map/ppermute | solution.py:154
  68.4 1.9 %shard_map.29 = f32[4,32,256]{2,1,0:T(8,128)} custom-call(f32[6,48,256]{2,1,0:T(8,128)S(1)} %get-tuple-element.10.smooth, f32[6,48,256]{2,1,0:T(8,128)S(1)} %get-tuple-element.11.dens, f32[4,16,128]{2,1,0:T(8,128)S(1)} %get-tuple-element.12.own, f32[4,16,128]{2,1,0:T(8,128)S(1)} %collective-permute-done.4.flo, f32[4,16,128]{2,1,0:T(8,128)S(1)} %collective-permute-done.5.fhi, ...), custom_call_target="tpu_custom_call" | custom-call | tf_op jit(solution)/shard_map/pallas_call | solution.py:142
  (22 shorter events, 0.2 us)
Async XLA Ops:
  0.0 1.0 %copy-start = (f32[4,32,256]{2,1,0:T(8,128)S(1)}, f32[4,32,256]{2,1,0:T(8,128)}, u32[]{:S(2)}) copy-start(f32[4,32,256]{2,1,0:T(8,128)} %field.1) | copy-start | bytes 393220
  1.0 18.0 %collective-permute-start = (f32[5,32,256]{2,1,0:T(8,128)S(1)}, f32[5,32,256]{2,1,0:T(8,128)S(1)}, u32[]{:S(2)}, u32[]{:S(2)}) collective-permute-start(f32[5,32,256]{2,1,0:T(8,128)S(1)} %pad_maximum_fusion), channel_id=1, source_target_pairs={{0,8},{8,16},{16,24},{24,32},{32,40},{40,48},{48,56},{56,64},{64,7... | collective-permute-start | bytes 491528 | tf_op jit(solution)/shard_map/ppermute | solution.py:154
  4.8 12.9 %copy-start.1 = (f32[4,32,256]{2,1,0:T(8,128)S(1)}, f32[4,32,256]{2,1,0:T(8,128)}, u32[]{:S(2)}) copy-start(f32[4,32,256]{2,1,0:T(8,128)} %density.1) | copy-start | bytes 393220
  4.9 15.7 %collective-permute-start.1 = (f32[5,32,256]{2,1,0:T(8,128)S(1)}, f32[5,32,256]{2,1,0:T(8,128)S(1)}, u32[]{:S(2)}, u32[]{:S(2)}) collective-permute-start(f32[5,32,256]{2,1,0:T(8,128)S(1)} %pad_maximum_fusion.1), channel_id=1, source_target_pairs={{0,1016},{8,0},{16,8},{24,16},{32,24},{40,32},{48,40},{56,48},{64,... | collective-permute-start | bytes 491528 | tf_op jit(solution)/shard_map/ppermute | solution.py:154
  20.6 5.0 %collective-permute-start.2 = (f32[18,4,256]{2,1,0:T(4,128)S(1)}, f32[18,4,256]{2,1,0:T(4,128)S(1)}, u32[]{:S(2)}, u32[]{:S(2)}) collective-permute-start(f32[18,4,256]{2,1,0:T(4,128)S(1)} %pad_maximum_fusion.2), channel_id=1, source_target_pairs={{0,1},{1,2},{2,3},{3,4},{4,5},{5,6},{6,7},{7,0},{8,9},{9,10},{10,1... | collective-permute-start | bytes 221192 | tf_op jit(solution)/shard_map/ppermute | solution.py:154
  20.7 5.0 %collective-permute-start.3 = (f32[18,4,256]{2,1,0:T(4,128)S(1)}, f32[18,4,256]{2,1,0:T(4,128)S(1)}, u32[]{:S(2)}, u32[]{:S(2)}) collective-permute-start(f32[18,4,256]{2,1,0:T(4,128)S(1)} %pad_maximum_fusion.3), channel_id=1, source_target_pairs={{0,7},{1,0},{2,1},{3,2},{4,3},{5,4},{6,5},{7,6},{8,15},{9,8},{10,9... | collective-permute-start | bytes 221192 | tf_op jit(solution)/shard_map/ppermute | solution.py:154
  26.5 23.1 %collective-permute-start.5 = (f32[4,16,128]{2,1,0:T(8,128)S(1)}, f32[4,16,128]{2,1,0:T(8,128)S(1)}, u32[]{:S(2)}, u32[]{:S(2)}) collective-permute-start(f32[4,16,128]{2,1,0:T(8,128)S(1)} %get-tuple-element.12.own), channel_id=1, source_target_pairs={{0,1000},{8,1008},{16,1016},{24,0},{32,8},{40,16},{48,24},{56,32},... | collective-permute-start | bytes 98312 | tf_op jit(solution)/shard_map/ppermute | solution.py:154
  38.7 10.9 %collective-permute-start.4 = (f32[4,16,128]{2,1,0:T(8,128)S(1)}, f32[4,16,128]{2,1,0:T(8,128)S(1)}, u32[]{:S(2)}, u32[]{:S(2)}) collective-permute-start(f32[4,16,128]{2,1,0:T(8,128)S(1)} %get-tuple-element.12.own), channel_id=1, source_target_pairs={{0,24},{8,32},{16,40},{24,48},{32,56},{40,64},{48,72},{56,80},{64,... | collective-permute-start | bytes 98312 | tf_op jit(solution)/shard_map/ppermute | solution.py:154
  49.7 7.9 %collective-permute-start.6 = (f32[14,16,128]{2,1,0:T(8,128)S(1)}, f32[14,16,128]{2,1,0:T(8,128)S(1)}, u32[]{:S(2)}, u32[]{:S(2)}) collective-permute-start(f32[14,16,128]{2,1,0:T(8,128)S(1)} %constant_dynamic-update-slice_fusion), channel_id=1, source_target_pairs={{0,8},{8,16},{16,24},{24,32},{32,40},{40,48},{48,56},{56,64},{64,7... | collective-permute-start | bytes 344072 | tf_op jit(solution)/shard_map/ppermute | solution.py:154
  55.2 6.7 %collective-permute-start.7 = (f32[14,16,128]{2,1,0:T(8,128)S(1)}, f32[14,16,128]{2,1,0:T(8,128)S(1)}, u32[]{:S(2)}, u32[]{:S(2)}) collective-permute-start(f32[14,16,128]{2,1,0:T(8,128)S(1)} %constant_dynamic-update-slice_fusion.5), channel_id=1, source_target_pairs={{0,1016},{8,0},{16,8},{24,16},{32,24},{40,32},{48,40},{56,48},{64,... | collective-permute-start | bytes 344072 | tf_op jit(solution)/shard_map/ppermute | solution.py:154
  61.9 3.4 %collective-permute-start.9 = (f32[32,8,128]{2,1,0:T(8,128)S(1)}, f32[32,8,128]{2,1,0:T(8,128)S(1)}, u32[]{:S(2)}, u32[]{:S(2)}) collective-permute-start(f32[32,8,128]{2,1,0:T(8,128)S(1)} %get-tuple-element.27), channel_id=1, source_target_pairs={{0,7},{1,0},{2,1},{3,2},{4,3},{5,4},{6,5},{7,6},{8,15},{9,8},{10,9... | collective-permute-start | bytes 393224 | tf_op jit(solution)/shard_map/ppermute | solution.py:154
  62.8 5.6 %collective-permute-start.8 = (f32[32,8,128]{2,1,0:T(8,128)S(1)}, f32[32,8,128]{2,1,0:T(8,128)S(1)}, u32[]{:S(2)}, u32[]{:S(2)}) collective-permute-start(f32[32,8,128]{2,1,0:T(8,128)S(1)} %get-tuple-element.28), channel_id=1, source_target_pairs={{0,1},{1,2},{2,3},{3,4},{4,5},{5,6},{6,7},{7,0},{8,9},{9,10},{10,1... | collective-permute-start | bytes 393224 | tf_op jit(solution)/shard_map/ppermute | solution.py:154

commit v4 on v3

--- a/solution.py
+++ b/solution.py
@@ -35,7 +35,7 @@
     return total + jnp.dot(high, weights, preferred_element_type=jnp.float32)
 
 
-def fine_kernel(field, density, xlo, xhi, clo, chi, smooth, dens, coarse, up, down, f, d, s1, pair, rows):
+def fine_kernel(field, density, xlo, xhi, clo, chi, smooth, dens, coarse, coarse2, up, down, f, d, s1, pair, rows):
     f[0:3, 8:40] = xlo[0:3]
     f[3:7, 8:40] = field[...]
     f[7:10, 8:40] = xhi[0:3]
@@ -70,6 +70,7 @@
     half = lax.broadcasted_iota(jnp.int32, (256, 128), 1)
     weights = jnp.where(third // 2 == half, 0.125, 0.0).astype(jnp.bfloat16)
     coarse[...] = exact_dot(rows[...], weights).reshape(4, 16, 128)
+    coarse2[...] = coarse[...]
     for face, layer in ((up, 3), (down, 2)):
         for j in range(4):
             at, lane = 8 + 16 * (j // 2), 128 * (j % 2)
@@ -165,13 +166,13 @@
     xhi = send(jnp.concatenate([field[0:3], density[0:2]], 0), "gx", -1)
     clo = send(jnp.concatenate([xlo[:, 28:32], xhi[:, 28:32], field[:, 28:32], density[:, 28:32]], 0), "gy", 1)
     chi = send(jnp.concatenate([xlo[:, 0:4], xhi[:, 0:4], field[:, 0:4], density[:, 0:4]], 0), "gy", -1)
-    smooth, dens, own, up, down = call(
+    smooth, dens, own, own2, up, down = call(
         fine_kernel,
-        [(6, 48, 256), (6, 48, 256), (4, 16, 128), (4, 16, 128), (4, 16, 128)],
+        [(6, 48, 256), (6, 48, 256), (4, 16, 128), (4, 16, 128), (4, 16, 128), (4, 16, 128)],
         [(10, 48, 256), (8, 48, 256), (8, 48, 256), (4, 2, 48, 128), (64, 256)],
         field, density, xlo, xhi, clo, chi,
     )
-    flo, fhi = send(own, "gx", 3), send(own, "gx", -3)
+    flo, fhi = send(own, "gx", 3), send(own2, "gx", -3)
     nlo = send(jnp.concatenate([flo[1:2], flo[3:4], own, fhi, up], 0), "gx", 1)
     nhi = send(jnp.concatenate([fhi[0:1], fhi[2:3], own, flo, down], 0), "gx", -1)
     yrows, zrows = rows_from_sides([own, flo, fhi, nlo[0:10], nhi[0:10]])

time: 70.6 us -> 66 us (0.935)
  the two profiles are of different devices: /device:TPU:32 before, /device:TPU:1 now
where the time goes in v4:
time: 66 us; the launch traced here: 65.2 us
  starting transfers between devices  49.1 us (74%)
  waiting for transfers between devices  11.9 us (18%)
  Pallas kernels  2.79 us (4%)
  local copies, waits for them, and re-layouts  1.08 us (2%)
    ppermute x10, starting transfers between devices, send(): lax.ppermute(values, axis, [(i, (i + step) % count) for i in range(count)])  49.1 us
    ppermute x10, waiting for transfers between devices, send(): lax.ppermute(values, axis, [(i, (i + step) % count) for i in range(count)])  11.9 us
    pallas_call x2, Pallas kernels, call(): pl.pallas_call(kernel, out_shape=shapes, in_specs=[vmem] * len(args), out...  2.79 us
  transfers between devices with their start and end apart: 10, of which 8 were waited for; matrix products, arithmetic and copies ran while one was open for 0% of the time, Pallas kernels for 0%

profile of v4, /device:TPU:1, one launch (start us, length us, event | category | flops | bytes accessed | tf_op | source)
XLA Modules:
  0.0 65.2 jit_solution(509250266677261086)
XLA Ops:
  0.0 0.0 copy-start
  0.0 0.9 %fusion.5 = (f32[2,32,256]{2,1,0:T(8,128)S(1)}, f32[2,32,256]{2,1,0:T(8,128)S(1)}) fusion(f32[4,32,256]{2,1,0:T(8,128)} %density.1), kind=kLoop, calls=%fused_computation.29 | loop fusion | bytes 262144 | tf_op jit(solution)/shard_map/slice | solution.py:166
  0.9 0.0 copy-done
  1.0 4.4 %collective-permute-start = (f32[5,32,256]{2,1,0:T(8,128)S(1)}, f32[5,32,256]{2,1,0:T(8,128)S(1)}, u32[]{:S(2)}, u32[]{:S(2)}) collective-permute-start(f32[5,32,256]{2,1,0:T(8,128)S(1)} %pad_maximum_fusion), channel_id=1, source_target_pairs={{0,8},{8,16},{16,24},{24,32},{32,40},{40,48},{48,56},{56,64},{64,7... | collective-permute-start | bytes 491528 | tf_op jit(solution)/shard_map/ppermute | solution.py:155
  5.4 0.0 copy-start.1
  5.4 19.4 %collective-permute-start.1 = (f32[5,32,256]{2,1,0:T(8,128)S(1)}, f32[5,32,256]{2,1,0:T(8,128)S(1)}, u32[]{:S(2)}, u32[]{:S(2)}) collective-permute-start(f32[5,32,256]{2,1,0:T(8,128)S(1)} %pad_maximum_fusion.1), channel_id=1, source_target_pairs={{0,1016},{8,0},{16,8},{24,16},{32,24},{40,32},{48,40},{56,48},{64,... | collective-permute-start | bytes 491528 | tf_op jit(solution)/shard_map/ppermute | solution.py:155
  24.8 0.0 copy-done.1
  24.8 1.8 %collective-permute-done.xlo = f32[5,32,256]{2,1,0:T(8,128)S(1)} collective-permute-done((f32[5,32,256]{2,1,0:T(8,128)S(1)}, f32[5,32,256]{2,1,0:T(8,128)S(1)}, u32[]{:S(2)}, u32[]{:S(2)}) %collective-permute-start) | collective-permute-done | bytes 163872 | tf_op jit(solution)/shard_map/ppermute | solution.py:155
  26.6 1.0 %collective-permute-done.1.xhi = f32[5,32,256]{2,1,0:T(8,128)S(1)} collective-permute-done((f32[5,32,256]{2,1,0:T(8,128)S(1)}, f32[5,32,256]{2,1,0:T(8,128)S(1)}, u32[]{:S(2)}, u32[]{:S(2)}) %collective-permute-start.1) | collective-permute-done | bytes 163872 | tf_op jit(solution)/shard_map/ppermute | solution.py:155
  27.7 2.7 %collective-permute-start.2 = (f32[18,4,256]{2,1,0:T(4,128)S(1)}, f32[18,4,256]{2,1,0:T(4,128)S(1)}, u32[]{:S(2)}, u32[]{:S(2)}) collective-permute-start(f32[18,4,256]{2,1,0:T(4,128)S(1)} %pad_maximum_fusion.2), channel_id=1, source_target_pairs={{0,1},{1,2},{2,3},{3,4},{4,5},{5,6},{6,7},{7,0},{8,9},{9,10},{10,1... | collective-permute-start | bytes 221192 | tf_op jit(solution)/shard_map/ppermute | solution.py:155
  30.3 0.0 collective-permute-start.3
  30.4 1.4 %collective-permute-done.2.clo = f32[18,4,256]{2,1,0:T(4,128)S(1)} collective-permute-done((f32[18,4,256]{2,1,0:T(4,128)S(1)}, f32[18,4,256]{2,1,0:T(4,128)S(1)}, u32[]{:S(2)}, u32[]{:S(2)}) %collective-permute-start.2) | collective-permute-done | bytes 73760 | tf_op jit(solution)/shard_map/ppermute | solution.py:155
  31.7 2.4 %collective-permute-done.3.chi = f32[18,4,256]{2,1,0:T(4,128)S(1)} collective-permute-done((f32[18,4,256]{2,1,0:T(4,128)S(1)}, f32[18,4,256]{2,1,0:T(4,128)S(1)}, u32[]{:S(2)}, u32[]{:S(2)}) %collective-permute-start.3) | collective-permute-done | bytes 73760 | tf_op jit(solution)/shard_map/ppermute | solution.py:155
  34.1 0.8 %shard_map.28 = (f32[6,48,256]{2,1,0:T(8,128)S(1)}, f32[6,48,256]{2,1,0:T(8,128)S(1)}, f32[4,16,128]{2,1,0:T(8,128)S(1)}, f32[4,16,128]{2,1,0:T(8,128)S(1)}, f32...) custom-call(f32[4,32,256]{2,1,0:T(8,128)S(1)} %copy-done, f32[4,32,256]{2,1,0:T(8,128)S(1)} %copy-done.1, ...), custom_call_target="tpu_custom_call" | custom-call | tf_op jit(solution)/shard_map/pallas_call | solution.py:143
  35.0 1.9 %collective-permute-start.4 = (f32[4,16,128]{2,1,0:T(8,128)S(1)}, f32[4,16,128]{2,1,0:T(8,128)S(1)}, u32[]{:S(2)}, u32[]{:S(2)}) collective-permute-start(f32[4,16,128]{2,1,0:T(8,128)S(1)} %get-tuple-element.13.own), channel_id=1, source_target_pairs={{0,24},{8,32},{16,40},{24,48},{32,56},{40,64},{48,72},{56,80},{64,... | collective-permute-start | bytes 98312 | tf_op jit(solution)/shard_map/ppermute | solution.py:155
  36.9 8.5 %collective-permute-start.5 = (f32[4,16,128]{2,1,0:T(8,128)S(1)}, f32[4,16,128]{2,1,0:T(8,128)S(1)}, u32[]{:S(2)}, u32[]{:S(2)}) collective-permute-start(f32[4,16,128]{2,1,0:T(8,128)S(1)} %get-tuple-element.14), channel_id=1, source_target_pairs={{0,1000},{8,1008},{16,1016},{24,0},{32,8},{40,16},{48,24},{56,32},... | collective-permute-start | bytes 98312 | tf_op jit(solution)/shard_map/ppermute | solution.py:155
  45.4 0.0 collective-permute-done.4.flo
  45.5 1.0 %collective-permute-done.5.fhi = f32[4,16,128]{2,1,0:T(8,128)S(1)} collective-permute-done((f32[4,16,128]{2,1,0:T(8,128)S(1)}, f32[4,16,128]{2,1,0:T(8,128)S(1)}, u32[]{:S(2)}, u32[]{:S(2)}) %collective-permute-start.5) | collective-permute-done | bytes 32800 | tf_op jit(solution)/shard_map/ppermute | solution.py:155
  46.5 1.9 %collective-permute-start.6 = (f32[14,16,128]{2,1,0:T(8,128)S(1)}, f32[14,16,128]{2,1,0:T(8,128)S(1)}, u32[]{:S(2)}, u32[]{:S(2)}) collective-permute-start(f32[14,16,128]{2,1,0:T(8,128)S(1)} %constant_dynamic-update-slice_fusion), channel_id=1, source_target_pairs={{0,8},{8,16},{16,24},{24,32},{32,40},{40,48},{48,56},{56,64},{64,7... | collective-permute-start | bytes 344072 | tf_op jit(solution)/shard_map/ppermute | solution.py:155
  48.4 7.7 %collective-permute-start.7 = (f32[14,16,128]{2,1,0:T(8,128)S(1)}, f32[14,16,128]{2,1,0:T(8,128)S(1)}, u32[]{:S(2)}, u32[]{:S(2)}) collective-permute-start(f32[14,16,128]{2,1,0:T(8,128)S(1)} %constant_dynamic-update-slice_fusion.5), channel_id=1, source_target_pairs={{0,1016},{8,0},{16,8},{24,16},{32,24},{40,32},{48,40},{56,48},{64,... | collective-permute-start | bytes 344072 | tf_op jit(solution)/shard_map/ppermute | solution.py:155
  56.2 0.2 collective-permute-done.6.nlo
  56.4 1.6 %collective-permute-done.7.nhi = f32[14,16,128]{2,1,0:T(8,128)S(1)} collective-permute-done((f32[14,16,128]{2,1,0:T(8,128)S(1)}, f32[14,16,128]{2,1,0:T(8,128)S(1)}, u32[]{:S(2)}, u32[]{:S(2)}) %collective-permute-start.7) | collective-permute-done | bytes 114720 | tf_op jit(solution)/shard_map/ppermute | solution.py:155
  58.0 2.0 %collective-permute-start.9 = (f32[32,8,128]{2,1,0:T(8,128)S(1)}, f32[32,8,128]{2,1,0:T(8,128)S(1)}, u32[]{:S(2)}, u32[]{:S(2)}) collective-permute-start(f32[32,8,128]{2,1,0:T(8,128)S(1)} %get-tuple-element.29), channel_id=1, source_target_pairs={{0,7},{1,0},{2,1},{3,2},{4,3},{5,4},{6,5},{7,6},{8,15},{9,8},{10,9... | collective-permute-start | bytes 393224 | tf_op jit(solution)/shard_map/ppermute | solution.py:155
  60.0 0.6 collective-permute-start.8
  60.6 2.6 %collective-permute-done.9.zrows = f32[32,8,128]{2,1,0:T(8,128)S(1)} collective-permute-done((f32[32,8,128]{2,1,0:T(8,128)S(1)}, f32[32,8,128]{2,1,0:T(8,128)S(1)}, u32[]{:S(2)}, u32[]{:S(2)}) %collective-permute-start.9) | collective-permute-done | bytes 131104 | tf_op jit(solution)/shard_map/ppermute | solution.py:155
  63.2 0.0 collective-permute-done.8.yrows
  63.2 1.9 %shard_map.29 = f32[4,32,256]{2,1,0:T(8,128)} custom-call(f32[6,48,256]{2,1,0:T(8,128)S(1)} %get-tuple-element.11.smooth, f32[6,48,256]{2,1,0:T(8,128)S(1)} %get-tuple-element.12.dens, f32[4,16,128]{2,1,0:T(8,128)S(1)} %get-tuple-element.13.own, f32[4,16,128]{2,1,0:T(8,128)S(1)} %collective-permute-done.4.flo, f32[4,16,128]{2,1,0:T(8,128)S(1)} %collective-permute-done.5.fhi, ...), custom_call_target="tpu_custom_call" | custom-call | tf_op jit(solution)/shard_map/pallas_call | solution.py:143
  (22 shorter events, 0.2 us)
Async XLA Ops:
  0.0 1.0 %copy-start = (f32[4,32,256]{2,1,0:T(8,128)S(1)}, f32[4,32,256]{2,1,0:T(8,128)}, u32[]{:S(2)}) copy-start(f32[4,32,256]{2,1,0:T(8,128)} %field.1) | copy-start | bytes 393220
  1.0 25.6 %collective-permute-start = (f32[5,32,256]{2,1,0:T(8,128)S(1)}, f32[5,32,256]{2,1,0:T(8,128)S(1)}, u32[]{:S(2)}, u32[]{:S(2)}) collective-permute-start(f32[5,32,256]{2,1,0:T(8,128)S(1)} %pad_maximum_fusion), channel_id=1, source_target_pairs={{0,8},{8,16},{16,24},{24,32},{32,40},{40,48},{48,56},{56,64},{64,7... | collective-permute-start | bytes 491528 | tf_op jit(solution)/shard_map/ppermute | solution.py:155
  5.4 19.4 %copy-start.1 = (f32[4,32,256]{2,1,0:T(8,128)S(1)}, f32[4,32,256]{2,1,0:T(8,128)}, u32[]{:S(2)}) copy-start(f32[4,32,256]{2,1,0:T(8,128)} %density.1) | copy-start | bytes 393220
  5.4 22.2 %collective-permute-start.1 = (f32[5,32,256]{2,1,0:T(8,128)S(1)}, f32[5,32,256]{2,1,0:T(8,128)S(1)}, u32[]{:S(2)}, u32[]{:S(2)}) collective-permute-start(f32[5,32,256]{2,1,0:T(8,128)S(1)} %pad_maximum_fusion.1), channel_id=1, source_target_pairs={{0,1016},{8,0},{16,8},{24,16},{32,24},{40,32},{48,40},{56,48},{64,... | collective-permute-start | bytes 491528 | tf_op jit(solution)/shard_map/ppermute | solution.py:155
  27.7 4.1 %collective-permute-start.2 = (f32[18,4,256]{2,1,0:T(4,128)S(1)}, f32[18,4,256]{2,1,0:T(4,128)S(1)}, u32[]{:S(2)}, u32[]{:S(2)}) collective-permute-start(f32[18,4,256]{2,1,0:T(4,128)S(1)} %pad_maximum_fusion.2), channel_id=1, source_target_pairs={{0,1},{1,2},{2,3},{3,4},{4,5},{5,6},{6,7},{7,0},{8,9},{9,10},{10,1... | collective-permute-start | bytes 221192 | tf_op jit(solution)/shard_map/ppermute | solution.py:155
  30.3 3.8 %collective-permute-start.3 = (f32[18,4,256]{2,1,0:T(4,128)S(1)}, f32[18,4,256]{2,1,0:T(4,128)S(1)}, u32[]{:S(2)}, u32[]{:S(2)}) collective-permute-start(f32[18,4,256]{2,1,0:T(4,128)S(1)} %pad_maximum_fusion.3), channel_id=1, source_target_pairs={{0,7},{1,0},{2,1},{3,2},{4,3},{5,4},{6,5},{7,6},{8,15},{9,8},{10,9... | collective-permute-start | bytes 221192 | tf_op jit(solution)/shard_map/ppermute | solution.py:155
  35.0 10.4 %collective-permute-start.4 = (f32[4,16,128]{2,1,0:T(8,128)S(1)}, f32[4,16,128]{2,1,0:T(8,128)S(1)}, u32[]{:S(2)}, u32[]{:S(2)}) collective-permute-start(f32[4,16,128]{2,1,0:T(8,128)S(1)} %get-tuple-element.13.own), channel_id=1, source_target_pairs={{0,24},{8,32},{16,40},{24,48},{32,56},{40,64},{48,72},{56,80},{64,... | collective-permute-start | bytes 98312 | tf_op jit(solution)/shard_map/ppermute | solution.py:155
  36.9 9.5 %collective-permute-start.5 = (f32[4,16,128]{2,1,0:T(8,128)S(1)}, f32[4,16,128]{2,1,0:T(8,128)S(1)}, u32[]{:S(2)}, u32[]{:S(2)}) collective-permute-start(f32[4,16,128]{2,1,0:T(8,128)S(1)} %get-tuple-element.14), channel_id=1, source_target_pairs={{0,1000},{8,1008},{16,1016},{24,0},{32,8},{40,16},{48,24},{56,32},... | collective-permute-start | bytes 98312 | tf_op jit(solution)/shard_map/ppermute | solution.py:155
  46.5 9.9 %collective-permute-start.6 = (f32[14,16,128]{2,1,0:T(8,128)S(1)}, f32[14,16,128]{2,1,0:T(8,128)S(1)}, u32[]{:S(2)}, u32[]{:S(2)}) collective-permute-start(f32[14,16,128]{2,1,0:T(8,128)S(1)} %constant_dynamic-update-slice_fusion), channel_id=1, source_target_pairs={{0,8},{8,16},{16,24},{24,32},{32,40},{40,48},{48,56},{56,64},{64,7... | collective-permute-start | bytes 344072 | tf_op jit(solution)/shard_map/ppermute | solution.py:155
  48.4 9.5 %collective-permute-start.7 = (f32[14,16,128]{2,1,0:T(8,128)S(1)}, f32[14,16,128]{2,1,0:T(8,128)S(1)}, u32[]{:S(2)}, u32[]{:S(2)}) collective-permute-start(f32[14,16,128]{2,1,0:T(8,128)S(1)} %constant_dynamic-update-slice_fusion.5), channel_id=1, source_target_pairs={{0,1016},{8,0},{16,8},{24,16},{32,24},{40,32},{48,40},{56,48},{64,... | collective-permute-start | bytes 344072 | tf_op jit(solution)/shard_map/ppermute | solution.py:155
  58.0 5.3 %collective-permute-start.9 = (f32[32,8,128]{2,1,0:T(8,128)S(1)}, f32[32,8,128]{2,1,0:T(8,128)S(1)}, u32[]{:S(2)}, u32[]{:S(2)}) collective-permute-start(f32[32,8,128]{2,1,0:T(8,128)S(1)} %get-tuple-element.29), channel_id=1, source_target_pairs={{0,7},{1,0},{2,1},{3,2},{4,3},{5,4},{6,5},{7,6},{8,15},{9,8},{10,9... | collective-permute-start | bytes 393224 | tf_op jit(solution)/shard_map/ppermute | solution.py:155
  60.0 3.2 %collective-permute-start.8 = (f32[32,8,128]{2,1,0:T(8,128)S(1)}, f32[32,8,128]{2,1,0:T(8,128)S(1)}, u32[]{:S(2)}, u32[]{:S(2)}) collective-permute-start(f32[32,8,128]{2,1,0:T(8,128)S(1)} %get-tuple-element.30), channel_id=1, source_target_pairs={{0,1},{1,2},{2,3},{3,4},{4,5},{5,6},{6,7},{7,0},{8,9},{9,10},{10,1... | collective-permute-start | bytes 393224 | tf_op jit(solution)/shard_map/ppermute | solution.py:155

commit v5 on v4

--- a/solution.py
+++ b/solution.py
@@ -35,7 +35,7 @@
     return total + jnp.dot(high, weights, preferred_element_type=jnp.float32)
 
 
-def fine_kernel(field, density, xlo, xhi, clo, chi, smooth, dens, coarse, coarse2, up, down, f, d, s1, pair, rows):
+def fine_kernel(field, density, xhi, xlo, clo, chi, smooth, dens, coarse, coarse2, up, down, f, d, s1, pair, rows):
     f[0:3, 8:40] = xlo[0:3]
     f[3:7, 8:40] = field[...]
     f[7:10, 8:40] = xhi[0:3]
@@ -68,7 +68,7 @@
             rows[16 * j : 16 * j + 16, 128 * k : 128 * k + 128] = total
     third = lax.broadcasted_iota(jnp.int32, (256, 128), 0)
     half = lax.broadcasted_iota(jnp.int32, (256, 128), 1)
-    weights = jnp.where(third // 2 == half, 0.125, 0.0).astype(jnp.bfloat16)
+    weights = jnp.where(third >> 1 == half, 0.125, 0.0).astype(jnp.bfloat16)
     coarse[...] = exact_dot(rows[...], weights).reshape(4, 16, 128)
     coarse2[...] = coarse[...]
     for face, layer in ((up, 3), (down, 2)):
@@ -109,8 +109,8 @@
     change = (now[5:11] - a[5:11]).reshape(192, 128)
     half = lax.broadcasted_iota(jnp.int32, (128, 256), 0)
     third = lax.broadcasted_iota(jnp.int32, (128, 256), 1)
-    beside = (third // 2 + 2 * (third % 2) - 1 + 128) % 128
-    weights = jnp.where(third // 2 == half, 0.75, jnp.where(beside == half, 0.25, 0.0)).astype(jnp.bfloat16)
+    beside = ((third >> 1) + 2 * (third & 1) - 1) & 127
+    weights = jnp.where(third >> 1 == half, 0.75, jnp.where(beside == half, 0.25, 0.0)).astype(jnp.bfloat16)
     spread = exact_dot(change, weights).reshape(6, 32, 256)
     for i in range(6):
         v = spread[i]
@@ -170,7 +170,7 @@
         fine_kernel,
         [(6, 48, 256), (6, 48, 256), (4, 16, 128), (4, 16, 128), (4, 16, 128), (4, 16, 128)],
         [(10, 48, 256), (8, 48, 256), (8, 48, 256), (4, 2, 48, 128), (64, 256)],
-        field, density, xlo, xhi, clo, chi,
+        field, density, xhi, xlo, clo, chi,
     )
     flo, fhi = send(own, "gx", 3), send(own2, "gx", -3)
     nlo = send(jnp.concatenate([flo[1:2], flo[3:4], own, fhi, up], 0), "gx", 1)

time: 66 us -> 70.3 us (1.065)
  waiting for transfers between devices: 11.9 us -> 17.1 us
    ppermute x10, waiting for transfers between devices: 11.9 us -> 17.1 us  [send(): lax.ppermute(values, axis, [(i, (i + step) % count) for i in range(count)])]
    ppermute x10, starting transfers between devices: 49.1 us -> 48.4 us  [send(): lax.ppermute(values, axis, [(i, (i + step) % count) for i in range(count)])]
where the time goes in v5:
time: 70.3 us; the launch traced here: 69.6 us
  starting transfers between devices  48.4 us (69%)
  waiting for transfers between devices  17.1 us (24%)
  Pallas kernels  2.78 us (4%)
  local copies, waits for them, and re-layouts  1.08 us (2%)
    ppermute x10, starting transfers between devices, send(): lax.ppermute(values, axis, [(i, (i + step) % count) for i in range(count)])  48.4 us
    ppermute x10, waiting for transfers between devices, send(): lax.ppermute(values, axis, [(i, (i + step) % count) for i in range(count)])  17.1 us
    pallas_call x2, Pallas kernels, call(): pl.pallas_call(kernel, out_shape=shapes, in_specs=[vmem] * len(args), out...  2.78 us
  transfers between devices with their start and end apart: 10, of which 8 were waited for; matrix products, arithmetic and copies ran while one was open for 0% of the time, Pallas kernels for 0%

profile of v5, /device:TPU:1, one launch (start us, length us, event | category | flops | bytes accessed | tf_op | source)
XLA Modules:
  0.0 69.6 jit_solution(6451681117317423544)
XLA Ops:
  0.0 0.0 copy-start
  0.0 0.9 %fusion.5 = (f32[2,32,256]{2,1,0:T(8,128)S(1)}, f32[2,32,256]{2,1,0:T(8,128)S(1)}) fusion(f32[4,32,256]{2,1,0:T(8,128)} %density.1), kind=kLoop, calls=%fused_computation.29 | loop fusion | bytes 262144 | tf_op jit(solution)/shard_map/slice | solution.py:165
  0.9 0.0 copy-done
  1.0 21.7 %collective-permute-start = (f32[5,32,256]{2,1,0:T(8,128)S(1)}, f32[5,32,256]{2,1,0:T(8,128)S(1)}, u32[]{:S(2)}, u32[]{:S(2)}) collective-permute-start(f32[5,32,256]{2,1,0:T(8,128)S(1)} %pad_maximum_fusion), channel_id=1, source_target_pairs={{0,1016},{8,0},{16,8},{24,16},{32,24},{40,32},{48,40},{56,48},{64,... | collective-permute-start | bytes 491528 | tf_op jit(solution)/shard_map/ppermute | solution.py:155
  22.7 0.0 copy-start.1
  22.7 2.1 %collective-permute-start.1 = (f32[5,32,256]{2,1,0:T(8,128)S(1)}, f32[5,32,256]{2,1,0:T(8,128)S(1)}, u32[]{:S(2)}, u32[]{:S(2)}) collective-permute-start(f32[5,32,256]{2,1,0:T(8,128)S(1)} %pad_maximum_fusion.1), channel_id=1, source_target_pairs={{0,8},{8,16},{16,24},{24,32},{32,40},{40,48},{48,56},{56,64},{64,7... | collective-permute-start | bytes 491528 | tf_op jit(solution)/shard_map/ppermute | solution.py:155
  24.8 0.0 copy-done.1
  24.8 0.7 %collective-permute-done.xhi = f32[5,32,256]{2,1,0:T(8,128)S(1)} collective-permute-done((f32[5,32,256]{2,1,0:T(8,128)S(1)}, f32[5,32,256]{2,1,0:T(8,128)S(1)}, u32[]{:S(2)}, u32[]{:S(2)}) %collective-permute-start) | collective-permute-done | bytes 163872 | tf_op jit(solution)/shard_map/ppermute | solution.py:155
  25.5 7.3 %collective-permute-done.1.xlo = f32[5,32,256]{2,1,0:T(8,128)S(1)} collective-permute-done((f32[5,32,256]{2,1,0:T(8,128)S(1)}, f32[5,32,256]{2,1,0:T(8,128)S(1)}, u32[]{:S(2)}, u32[]{:S(2)}) %collective-permute-start.1) | collective-permute-done | bytes 163872 | tf_op jit(solution)/shard_map/ppermute | solution.py:155
  32.9 3.0 %collective-permute-start.2 = (f32[18,4,256]{2,1,0:T(4,128)S(1)}, f32[18,4,256]{2,1,0:T(4,128)S(1)}, u32[]{:S(2)}, u32[]{:S(2)}) collective-permute-start(f32[18,4,256]{2,1,0:T(4,128)S(1)} %pad_maximum_fusion.2), channel_id=1, source_target_pairs={{0,1},{1,2},{2,3},{3,4},{4,5},{5,6},{6,7},{7,0},{8,9},{9,10},{10,1... | collective-permute-start | bytes 221192 | tf_op jit(solution)/shard_map/ppermute | solution.py:155
  35.9 0.0 collective-permute-start.3
  35.9 1.4 %collective-permute-done.2.clo = f32[18,4,256]{2,1,0:T(4,128)S(1)} collective-permute-done((f32[18,4,256]{2,1,0:T(4,128)S(1)}, f32[18,4,256]{2,1,0:T(4,128)S(1)}, u32[]{:S(2)}, u32[]{:S(2)}) %collective-permute-start.2) | collective-permute-done | bytes 73760 | tf_op jit(solution)/shard_map/ppermute | solution.py:155
  37.2 2.4 %collective-permute-done.3.chi = f32[18,4,256]{2,1,0:T(4,128)S(1)} collective-permute-done((f32[18,4,256]{2,1,0:T(4,128)S(1)}, f32[18,4,256]{2,1,0:T(4,128)S(1)}, u32[]{:S(2)}, u32[]{:S(2)}) %collective-permute-start.3) | collective-permute-done | bytes 73760 | tf_op jit(solution)/shard_map/ppermute | solution.py:155
  39.6 0.8 %shard_map.28 = (f32[6,48,256]{2,1,0:T(8,128)S(1)}, f32[6,48,256]{2,1,0:T(8,128)S(1)}, f32[4,16,128]{2,1,0:T(8,128)S(1)}, f32[4,16,128]{2,1,0:T(8,128)S(1)}, f32...) custom-call(f32[4,32,256]{2,1,0:T(8,128)S(1)} %copy-done, f32[4,32,256]{2,1,0:T(8,128)S(1)} %copy-done.1, ...), custom_call_target="tpu_custom_call" | custom-call | tf_op jit(solution)/shard_map/pallas_call | solution.py:143
  40.5 1.9 %collective-permute-start.4 = (f32[4,16,128]{2,1,0:T(8,128)S(1)}, f32[4,16,128]{2,1,0:T(8,128)S(1)}, u32[]{:S(2)}, u32[]{:S(2)}) collective-permute-start(f32[4,16,128]{2,1,0:T(8,128)S(1)} %get-tuple-element.13.own), channel_id=1, source_target_pairs={{0,24},{8,32},{16,40},{24,48},{32,56},{40,64},{48,72},{56,80},{64,... | collective-permute-start | bytes 98312 | tf_op jit(solution)/shard_map/ppermute | solution.py:155
  42.4 8.5 %collective-permute-start.5 = (f32[4,16,128]{2,1,0:T(8,128)S(1)}, f32[4,16,128]{2,1,0:T(8,128)S(1)}, u32[]{:S(2)}, u32[]{:S(2)}) collective-permute-start(f32[4,16,128]{2,1,0:T(8,128)S(1)} %get-tuple-element.14), channel_id=1, source_target_pairs={{0,1000},{8,1008},{16,1016},{24,0},{32,8},{40,16},{48,24},{56,32},... | collective-permute-start | bytes 98312 | tf_op jit(solution)/shard_map/ppermute | solution.py:155
  50.9 0.0 collective-permute-done.4.flo
  51.0 1.0 %collective-permute-done.5.fhi = f32[4,16,128]{2,1,0:T(8,128)S(1)} collective-permute-done((f32[4,16,128]{2,1,0:T(8,128)S(1)}, f32[4,16,128]{2,1,0:T(8,128)S(1)}, u32[]{:S(2)}, u32[]{:S(2)}) %collective-permute-start.5) | collective-permute-done | bytes 32800 | tf_op jit(solution)/shard_map/ppermute | solution.py:155
  52.0 1.9 %collective-permute-start.6 = (f32[14,16,128]{2,1,0:T(8,128)S(1)}, f32[14,16,128]{2,1,0:T(8,128)S(1)}, u32[]{:S(2)}, u32[]{:S(2)}) collective-permute-start(f32[14,16,128]{2,1,0:T(8,128)S(1)} %constant_dynamic-update-slice_fusion), channel_id=1, source_target_pairs={{0,8},{8,16},{16,24},{24,32},{32,40},{40,48},{48,56},{56,64},{64,7... | collective-permute-start | bytes 344072 | tf_op jit(solution)/shard_map/ppermute | solution.py:155
  53.9 6.7 %collective-permute-start.7 = (f32[14,16,128]{2,1,0:T(8,128)S(1)}, f32[14,16,128]{2,1,0:T(8,128)S(1)}, u32[]{:S(2)}, u32[]{:S(2)}) collective-permute-start(f32[14,16,128]{2,1,0:T(8,128)S(1)} %constant_dynamic-update-slice_fusion.5), channel_id=1, source_target_pairs={{0,1016},{8,0},{16,8},{24,16},{32,24},{40,32},{48,40},{56,48},{64,... | collective-permute-start | bytes 344072 | tf_op jit(solution)/shard_map/ppermute | solution.py:155
  60.6 0.2 collective-permute-done.6.nlo
  60.8 1.6 %collective-permute-done.7.nhi = f32[14,16,128]{2,1,0:T(8,128)S(1)} collective-permute-done((f32[14,16,128]{2,1,0:T(8,128)S(1)}, f32[14,16,128]{2,1,0:T(8,128)S(1)}, u32[]{:S(2)}, u32[]{:S(2)}) %collective-permute-start.7) | collective-permute-done | bytes 114720 | tf_op jit(solution)/shard_map/ppermute | solution.py:155
  62.4 2.3 %collective-permute-start.9 = (f32[32,8,128]{2,1,0:T(8,128)S(1)}, f32[32,8,128]{2,1,0:T(8,128)S(1)}, u32[]{:S(2)}, u32[]{:S(2)}) collective-permute-start(f32[32,8,128]{2,1,0:T(8,128)S(1)} %get-tuple-element.29), channel_id=1, source_target_pairs={{0,7},{1,0},{2,1},{3,2},{4,3},{5,4},{6,5},{7,6},{8,15},{9,8},{10,9... | collective-permute-start | bytes 393224 | tf_op jit(solution)/shard_map/ppermute | solution.py:155
  64.7 0.3 collective-permute-start.8
  65.1 2.6 %collective-permute-done.9.zrows = f32[32,8,128]{2,1,0:T(8,128)S(1)} collective-permute-done((f32[32,8,128]{2,1,0:T(8,128)S(1)}, f32[32,8,128]{2,1,0:T(8,128)S(1)}, u32[]{:S(2)}, u32[]{:S(2)}) %collective-permute-start.9) | collective-permute-done | bytes 131104 | tf_op jit(solution)/shard_map/ppermute | solution.py:155
  67.7 0.0 collective-permute-done.8.yrows
  67.7 1.9 %shard_map.29 = f32[4,32,256]{2,1,0:T(8,128)} custom-call(f32[6,48,256]{2,1,0:T(8,128)S(1)} %get-tuple-element.11.smooth, f32[6,48,256]{2,1,0:T(8,128)S(1)} %get-tuple-element.12.dens, f32[4,16,128]{2,1,0:T(8,128)S(1)} %get-tuple-element.13.own, f32[4,16,128]{2,1,0:T(8,128)S(1)} %collective-permute-done.4.flo, f32[4,16,128]{2,1,0:T(8,128)S(1)} %collective-permute-done.5.fhi, ...), custom_call_target="tpu_custom_call" | custom-call | tf_op jit(solution)/shard_map/pallas_call | solution.py:143
  (22 shorter events, 0.2 us)
Async XLA Ops:
  0.0 1.0 %copy-start = (f32[4,32,256]{2,1,0:T(8,128)S(1)}, f32[4,32,256]{2,1,0:T(8,128)}, u32[]{:S(2)}) copy-start(f32[4,32,256]{2,1,0:T(8,128)} %field.1) | copy-start | bytes 393220
  1.0 24.5 %collective-permute-start = (f32[5,32,256]{2,1,0:T(8,128)S(1)}, f32[5,32,256]{2,1,0:T(8,128)S(1)}, u32[]{:S(2)}, u32[]{:S(2)}) collective-permute-start(f32[5,32,256]{2,1,0:T(8,128)S(1)} %pad_maximum_fusion), channel_id=1, source_target_pairs={{0,1016},{8,0},{16,8},{24,16},{32,24},{40,32},{48,40},{56,48},{64,... | collective-permute-start | bytes 491528 | tf_op jit(solution)/shard_map/ppermute | solution.py:155
  22.7 2.1 %copy-start.1 = (f32[4,32,256]{2,1,0:T(8,128)S(1)}, f32[4,32,256]{2,1,0:T(8,128)}, u32[]{:S(2)}) copy-start(f32[4,32,256]{2,1,0:T(8,128)} %density.1) | copy-start | bytes 393220
  22.7 10.1 %collective-permute-start.1 = (f32[5,32,256]{2,1,0:T(8,128)S(1)}, f32[5,32,256]{2,1,0:T(8,128)S(1)}, u32[]{:S(2)}, u32[]{:S(2)}) collective-permute-start(f32[5,32,256]{2,1,0:T(8,128)S(1)} %pad_maximum_fusion.1), channel_id=1, source_target_pairs={{0,8},{8,16},{16,24},{24,32},{32,40},{40,48},{48,56},{56,64},{64,7... | collective-permute-start | bytes 491528 | tf_op jit(solution)/shard_map/ppermute | solution.py:155
  32.9 4.4 %collective-permute-start.2 = (f32[18,4,256]{2,1,0:T(4,128)S(1)}, f32[18,4,256]{2,1,0:T(4,128)S(1)}, u32[]{:S(2)}, u32[]{:S(2)}) collective-permute-start(f32[18,4,256]{2,1,0:T(4,128)S(1)} %pad_maximum_fusion.2), channel_id=1, source_target_pairs={{0,1},{1,2},{2,3},{3,4},{4,5},{5,6},{6,7},{7,0},{8,9},{9,10},{10,1... | collective-permute-start | bytes 221192 | tf_op jit(solution)/shard_map/ppermute | solution.py:155
  35.9 3.8 %collective-permute-start.3 = (f32[18,4,256]{2,1,0:T(4,128)S(1)}, f32[18,4,256]{2,1,0:T(4,128)S(1)}, u32[]{:S(2)}, u32[]{:S(2)}) collective-permute-start(f32[18,4,256]{2,1,0:T(4,128)S(1)} %pad_maximum_fusion.3), channel_id=1, source_target_pairs={{0,7},{1,0},{2,1},{3,2},{4,3},{5,4},{6,5},{7,6},{8,15},{9,8},{10,9... | collective-permute-start | bytes 221192 | tf_op jit(solution)/shard_map/ppermute | solution.py:155
  40.5 10.4 %collective-permute-start.4 = (f32[4,16,128]{2,1,0:T(8,128)S(1)}, f32[4,16,128]{2,1,0:T(8,128)S(1)}, u32[]{:S(2)}, u32[]{:S(2)}) collective-permute-start(f32[4,16,128]{2,1,0:T(8,128)S(1)} %get-tuple-element.13.own), channel_id=1, source_target_pairs={{0,24},{8,32},{16,40},{24,48},{32,56},{40,64},{48,72},{56,80},{64,... | collective-permute-start | bytes 98312 | tf_op jit(solution)/shard_map/ppermute | solution.py:155
  42.4 9.5 %collective-permute-start.5 = (f32[4,16,128]{2,1,0:T(8,128)S(1)}, f32[4,16,128]{2,1,0:T(8,128)S(1)}, u32[]{:S(2)}, u32[]{:S(2)}) collective-permute-start(f32[4,16,128]{2,1,0:T(8,128)S(1)} %get-tuple-element.14), channel_id=1, source_target_pairs={{0,1000},{8,1008},{16,1016},{24,0},{32,8},{40,16},{48,24},{56,32},... | collective-permute-start | bytes 98312 | tf_op jit(solution)/shard_map/ppermute | solution.py:155
  52.0 8.9 %collective-permute-start.6 = (f32[14,16,128]{2,1,0:T(8,128)S(1)}, f32[14,16,128]{2,1,0:T(8,128)S(1)}, u32[]{:S(2)}, u32[]{:S(2)}) collective-permute-start(f32[14,16,128]{2,1,0:T(8,128)S(1)} %constant_dynamic-update-slice_fusion), channel_id=1, source_target_pairs={{0,8},{8,16},{16,24},{24,32},{32,40},{40,48},{48,56},{56,64},{64,7... | collective-permute-start | bytes 344072 | tf_op jit(solution)/shard_map/ppermute | solution.py:155
  53.9 8.5 %collective-permute-start.7 = (f32[14,16,128]{2,1,0:T(8,128)S(1)}, f32[14,16,128]{2,1,0:T(8,128)S(1)}, u32[]{:S(2)}, u32[]{:S(2)}) collective-permute-start(f32[14,16,128]{2,1,0:T(8,128)S(1)} %constant_dynamic-update-slice_fusion.5), channel_id=1, source_target_pairs={{0,1016},{8,0},{16,8},{24,16},{32,24},{40,32},{48,40},{56,48},{64,... | collective-permute-start | bytes 344072 | tf_op jit(solution)/shard_map/ppermute | solution.py:155
  62.4 5.3 %collective-permute-start.9 = (f32[32,8,128]{2,1,0:T(8,128)S(1)}, f32[32,8,128]{2,1,0:T(8,128)S(1)}, u32[]{:S(2)}, u32[]{:S(2)}) collective-permute-start(f32[32,8,128]{2,1,0:T(8,128)S(1)} %get-tuple-element.29), channel_id=1, source_target_pairs={{0,7},{1,0},{2,1},{3,2},{4,3},{5,4},{6,5},{7,6},{8,15},{9,8},{10,9... | collective-permute-start | bytes 393224 | tf_op jit(solution)/shard_map/ppermute | solution.py:155
  64.7 3.0 %collective-permute-start.8 = (f32[32,8,128]{2,1,0:T(8,128)S(1)}, f32[32,8,128]{2,1,0:T(8,128)S(1)}, u32[]{:S(2)}, u32[]{:S(2)}) collective-permute-start(f32[32,8,128]{2,1,0:T(8,128)S(1)} %get-tuple-element.30), channel_id=1, source_target_pairs={{0,1},{1,2},{2,3},{3,4},{4,5},{5,6},{6,7},{7,0},{8,9},{9,10},{10,1... | collective-permute-start | bytes 393224 | tf_op jit(solution)/shard_map/ppermute | solution.py:155

commit v6 on v5

--- a/solution.py
+++ b/solution.py
@@ -7,6 +7,18 @@
 
 mass = 0.02
 damping = 0.8
+
+
+def pair_of(ref, i, start, rows):
+    return ref[i, start - 1 : start - 1 + rows] + ref[i, start + 1 : start + 1 + rows]
+
+
+def jacobi_rows(v, rows, below, above, source, inv_step):
+    around = below + above + rows
+    around = around + pltpu.roll(v, 1, 1) + pltpu.roll(v, v.shape[1] - 1, 1)
+    square = v * v
+    top = inv_step * around - source - v * ((6.0 * inv_step + mass) + (mass / 3.0) * square)
+    return v + top / ((6.0 * inv_step + mass) / damping + (mass / damping) * square)
 
 
 def jacobi(v, below, above, source, inv_step):
@@ -35,20 +47,26 @@
     return total + jnp.dot(high, weights, preferred_element_type=jnp.float32)
 
 
-def fine_kernel(field, density, xhi, xlo, clo, chi, smooth, dens, coarse, coarse2, up, down, f, d, s1, pair, rows):
+def edge_kernel(field, density, backward, first, last):
+    backward[0:3] = field[0:3]
+    backward[3:5] = density[0:2]
+    for target, at in ((first, 0), (last, 28)):
+        target[0:3] = field[0:3, at : at + 4]
+        target[3:5] = density[0:2, at : at + 4]
+
+
+def fine_kernel(field, density, xlo, xhi, clo, chi, smooth, dens, coarse, coarse2, up, down, f, d, s1, pair, rows):
     f[0:3, 8:40] = xlo[0:3]
     f[3:7, 8:40] = field[...]
-    f[7:10, 8:40] = xhi[0:3]
+    f[7:10, 4:44] = xhi[0:3]
     d[0:2, 8:40] = xlo[3:5]
     d[2:6, 8:40] = density[...]
-    d[6:8, 8:40] = xhi[3:5]
+    d[6:8, 4:44] = xhi[3:5]
     for side, at in ((clo, 4), (chi, 40)):
         f[0:3, at : at + 4] = side[0:3]
-        f[3:7, at : at + 4] = side[10:14]
-        f[7:10, at : at + 4] = side[5:8]
+        f[3:7, at : at + 4] = side[5:9]
         d[0:2, at : at + 4] = side[3:5]
-        d[2:6, at : at + 4] = side[14:18]
-        d[6:8, at : at + 4] = side[8:10]
+        d[2:6, at : at + 4] = side[9:13]
     for i in range(8):
         s1[i] = jacobi(f[i + 1], f[i], f[i + 2], d[i], 1.0)
     for i in range(6):
@@ -98,15 +116,15 @@
         place(rows, side.at[0:4], side.at[4:8], side.at[8:12], side.at[12:22], side.at[22:32])
     for i in range(16):
         v = a[i]
-        c0[i] = v - r[i] / ((1.5 + mass) / damping + (mass / damping) * (v * v))
+        c0[i, 8:40] = v - r[i] / ((1.5 + mass) / damping + (mass / damping) * (v * v))
     for i in range(1, 15):
         g[i] = operator(a[i], a[i - 1], a[i + 1], 0.25) + r[i]
     now, later = c0, c1
     for sweep in range(1, 6):
         for i in range(sweep, 16 - sweep):
-            later[i] = jacobi(now[i], now[i - 1], now[i + 1], g[i], 0.25)
+            later[i, 8:40] = jacobi_rows(now[i, 8:40], pair_of(now, i, 8, 32), now[i - 1, 8:40], now[i + 1, 8:40], g[i], 0.25)
         now, later = later, now
-    change = (now[5:11] - a[5:11]).reshape(192, 128)
+    change = (now[5:11, 8:40] - a[5:11]).reshape(192, 128)
     half = lax.broadcasted_iota(jnp.int32, (128, 256), 0)
     third = lax.broadcasted_iota(jnp.int32, (128, 256), 1)
     beside = ((third >> 1) + 2 * (third & 1) - 1) & 127
@@ -155,6 +173,14 @@
     return lax.ppermute(values, axis, [(i, (i + step) % count) for i in range(count)])
 
 
+def send_both(values, step, side_step):
+    count, sides = lax.axis_size("gx"), lax.axis_size("gy")
+    pairs = [
+        (i * sides + j, (i + step) % count * sides + (j + side_step) % sides) for i in range(count) for j in range(sides)
+    ]
+    return lax.ppermute(values, ("gx", "gy"), pairs)
+
+
 def rows_from_sides(pieces):
     last = jnp.concatenate([piece[:, 8:16] for piece in pieces], 0)
     first = jnp.concatenate([piece[:, 0:8] for piece in pieces], 0)
@@ -163,14 +189,23 @@
 
 def body(density, field):
     xlo = send(jnp.concatenate([field[1:4], density[2:4]], 0), "gx", 1)
-    xhi = send(jnp.concatenate([field[0:3], density[0:2]], 0), "gx", -1)
-    clo = send(jnp.concatenate([xlo[:, 28:32], xhi[:, 28:32], field[:, 28:32], density[:, 28:32]], 0), "gy", 1)
-    chi = send(jnp.concatenate([xlo[:, 0:4], xhi[:, 0:4], field[:, 0:4], density[:, 0:4]], 0), "gy", -1)
+    backward, first, last = pl.pallas_call(
+        edge_kernel,
+        out_shape=[jax.ShapeDtypeStruct((5, rows, 256), jnp.float32) for rows in (32, 4, 4)],
+        in_specs=[pl.BlockSpec(memory_space=pltpu.VMEM)] * 2,
+        out_specs=[pl.BlockSpec(memory_space=pltpu.VMEM)] * 3,
+    )(field, density)
+    dlo = send_both(last, -1, 1)
+    dhi = send_both(first, -1, -1)
+    xhi = send(backward, "gx", -1)
+    xhi = jnp.concatenate([dlo, xhi, dhi], 1)
+    clo = send(jnp.concatenate([xlo[:, 28:32], field[:, 28:32], density[:, 28:32]], 0), "gy", 1)
+    chi = send(jnp.concatenate([xlo[:, 0:4], field[:, 0:4], density[:, 0:4]], 0), "gy", -1)
     smooth, dens, own, own2, up, down = call(
         fine_kernel,
         [(6, 48, 256), (6, 48, 256), (4, 16, 128), (4, 16, 128), (4, 16, 128), (4, 16, 128)],
         [(10, 48, 256), (8, 48, 256), (8, 48, 256), (4, 2, 48, 128), (64, 256)],
-        field, density, xhi, xlo, clo, chi,
+        field, density, xlo, xhi, clo, chi,
     )
     flo, fhi = send(own, "gx", 3), send(own2, "gx", -3)
     nlo = send(jnp.concatenate([flo[1:2], flo[3:4], own, fhi, up], 0), "gx", 1)
@@ -179,7 +214,7 @@
     (out,) = call(
         coarse_kernel,
         [(4, 32, 256)],
-        [(16, 32, 128)] * 5 + [(6, 2, 64, 128), (8, 48, 256), (6, 48, 256)],
+        [(16, 32, 128)] * 3 + [(16, 48, 128)] * 2 + [(6, 2, 64, 128), (8, 48, 256), (6, 48, 256)],
         smooth, dens, own, flo, fhi, nlo, nhi, yrows, zrows,
     )
     return out

time: 70.3 us -> 72 us (1.024)
  waiting for transfers between devices: 17.1 us -> 9.46 us
  starting transfers between devices: 48.4 us -> 55.6 us
  Pallas kernels: 2.78 us -> 4.38 us
    ppermute x0 -> x2, starting transfers between devices: none -> 22.9 us  [send_both(): return lax.ppermute(values, ('gx', 'gy'), pairs)]
    ppermute x10, starting transfers between devices: 48.4 us -> 32.8 us  [send(): lax.ppermute(values, axis, [(i, (i + step) % count) for i in range(count)])]
    ppermute x10, waiting for transfers between devices: 17.1 us -> 9.45 us  [send(): lax.ppermute(values, axis, [(i, (i + step) % count) for i in range(count)])]
    pallas_call x0 -> x1, Pallas kernels: none -> 1.65 us  [body(): pl.pallas_call(edge_kernel, out_shape=[jax.ShapeDtypeStruct((5, rows, 256...]
  transfers between devices with their start and end apart: 10 -> 12, of which waited for: 8 -> 7; matrix products, arithmetic and copies ran while one was open for 0% -> 0% of each run, Pallas kernels for 0% -> 2%
where the time goes in v6:
time: 72 us; the launch traced here: 70.8 us
  starting transfers between devices  55.6 us (77%)
  waiting for transfers between devices  9.46 us (13%)
  Pallas kernels  4.38 us (6%)
  local copies, waits for them, and re-layouts  1 us (1%)
    ppermute x10, starting transfers between devices, send(): lax.ppermute(values, axis, [(i, (i + step) % count) for i in range(count)])  32.8 us
    ppermute x2, starting transfers between devices, send_both(): return lax.ppermute(values, ('gx', 'gy'), pairs)  22.9 us
    ppermute x10, waiting for transfers between devices, send(): lax.ppermute(values, axis, [(i, (i + step) % count) for i in range(count)])  9.45 us
    pallas_call x2, Pallas kernels, call(): pl.pallas_call(kernel, out_shape=shapes, in_specs=[vmem] * len(args), out...  2.73 us
    pallas_call x1, Pallas kernels, body(): pl.pallas_call(edge_kernel, out_shape=[jax.ShapeDtypeStruct((5, rows, 256...  1.65 us
  transfers between devices with their start and end apart: 12, of which 7 were waited for; matrix products, arithmetic and copies ran while one was open for 0% of the time, Pallas kernels for 2%

profile of v6, /device:TPU:1, one launch (start us, length us, event | category | flops | bytes accessed | tf_op | source)
XLA Modules:
  0.0 70.8 jit_solution(18413706344637102708)
XLA Ops:
  0.0 0.0 slice-start
  0.0 0.0 slice-start.1
  0.0 0.9 %slice-done = f32[3,32,256]{2,1,0:T(8,128)S(1)} async-done(((f32[4,32,256]{2,1,0:T(8,128)}), f32[3,32,256]{2,1,0:T(8,128)S(1)}, s32[]{:S(2)}) %slice-start) | async-done | bytes 98328 | tf_op jit(solution)/shard_map/slice | solution.py:191
  0.9 0.0 slice-done.1
  0.9 0.0 copy-start
  0.9 0.0 copy-start.1
  0.9 4.5 %collective-permute-start = (f32[5,32,256]{2,1,0:T(8,128)S(1)}, f32[5,32,256]{2,1,0:T(8,128)S(1)}, u32[]{:S(2)}, u32[]{:S(2)}) collective-permute-start(f32[5,32,256]{2,1,0:T(8,128)S(1)} %pad_maximum_fusion.1), channel_id=1, source_target_pairs={{0,8},{8,16},{16,24},{24,32},{32,40},{40,48},{48,56},{56,64},{64,7... | collective-permute-start | bytes 491528 | tf_op jit(solution)/shard_map/ppermute | solution.py:173
  5.5 1.7 %shard_map.28 = (f32[5,32,256]{2,1,0:T(8,128)}, f32[5,4,256]{2,1,0:T(4,128)}, f32[5,4,256]{2,1,0:T(4,128)}) custom-call(f32[4,32,256]{2,1,0:T(8,128)} %field.3, f32[4,32,256]{2,1,0:T(8,128)} %density.3), custom_call_target="tpu_custom_call" | custom-call | tf_op jit(solution)/shard_map/pallas_call | solution.py:192
  7.1 20.7 %collective-permute-start.1 = (f32[5,4,256]{2,1,0:T(4,128)}, f32[5,4,256]{2,1,0:T(4,128)S(1)}, u32[]{:S(2)}, u32[]{:S(2)}) collective-permute-start(f32[5,4,256]{2,1,0:T(4,128)} %get-tuple-element.14), channel_id=1, source_target_pairs={{0,1017},{1,1018},{2,1019},{3,1020},{4,1021},{5,1022},{6,1023},{7,... | collective-permute-start | bytes 61448 | tf_op jit(solution)/shard_map/ppermute | solution.py:181
  27.8 2.2 %collective-permute-start.3 = (f32[5,4,256]{2,1,0:T(4,128)}, f32[5,4,256]{2,1,0:T(4,128)S(1)}, u32[]{:S(2)}, u32[]{:S(2)}) collective-permute-start(f32[5,4,256]{2,1,0:T(4,128)} %get-tuple-element.16), channel_id=1, source_target_pairs={{0,1023},{1,1016},{2,1017},{3,1018},{4,1019},{5,1020},{6,1021},{7,... | collective-permute-start | bytes 61448 | tf_op jit(solution)/shard_map/ppermute | solution.py:181
  30.0 3.4 %collective-permute-start.2 = (f32[5,32,256]{2,1,0:T(8,128)}, f32[5,32,256]{2,1,0:T(8,128)S(1)}, u32[]{:S(2)}, u32[]{:S(2)}) collective-permute-start(f32[5,32,256]{2,1,0:T(8,128)} %get-tuple-element.15), channel_id=1, source_target_pairs={{0,1016},{8,0},{16,8},{24,16},{32,24},{40,32},{48,40},{56,48},{64,... | collective-permute-start | bytes 491528 | tf_op jit(solution)/shard_map/ppermute | solution.py:173
  33.4 0.0 copy-done
  33.4 0.0 copy-done.1
  33.4 0.0 collective-permute-done.xlo
  33.5 2.5 %collective-permute-start.4 = (f32[13,4,256]{2,1,0:T(4,128)S(1)}, f32[13,4,256]{2,1,0:T(4,128)S(1)}, u32[]{:S(2)}, u32[]{:S(2)}) collective-permute-start(f32[13,4,256]{2,1,0:T(4,128)S(1)} %pad_maximum_fusion.2), channel_id=1, source_target_pairs={{0,1},{1,2},{2,3},{3,4},{4,5},{5,6},{6,7},{7,0},{8,9},{9,10},{10,1... | collective-permute-start | bytes 159752 | tf_op jit(solution)/shard_map/ppermute | solution.py:173
  36.0 0.1 collective-permute-start.5
  36.1 0.0 collective-permute-done.1
  36.1 0.0 collective-permute-done.3
  36.1 0.1 collective-permute-done.2
  36.3 0.9 %collective-permute-done.4.clo = f32[13,4,256]{2,1,0:T(4,128)S(1)} collective-permute-done((f32[13,4,256]{2,1,0:T(4,128)S(1)}, f32[13,4,256]{2,1,0:T(4,128)S(1)}, u32[]{:S(2)}, u32[]{:S(2)}) %collective-permute-start.4) | collective-permute-done | bytes 53280 | tf_op jit(solution)/shard_map/ppermute | solution.py:173
  37.2 2.7 %collective-permute-done.5.chi = f32[13,4,256]{2,1,0:T(4,128)S(1)} collective-permute-done((f32[13,4,256]{2,1,0:T(4,128)S(1)}, f32[13,4,256]{2,1,0:T(4,128)S(1)}, u32[]{:S(2)}, u32[]{:S(2)}) %collective-permute-start.5) | collective-permute-done | bytes 53280 | tf_op jit(solution)/shard_map/ppermute | solution.py:173
  39.8 0.8 %shard_map.29 = (f32[6,48,256]{2,1,0:T(8,128)S(1)}, f32[6,48,256]{2,1,0:T(8,128)S(1)}, f32[4,16,128]{2,1,0:T(8,128)S(1)}, f32[4,16,128]{2,1,0:T(8,128)S(1)}, f32...) custom-call(f32[4,32,256]{2,1,0:T(8,128)S(1)} %copy-done, f32[4,32,256]{2,1,0:T(8,128)S(1)} %copy-done.1, ...), custom_call_target="tpu_custom_call" | custom-call | tf_op jit(solution)/shard_map/pallas_call | solution.py:161
  40.7 1.9 %collective-permute-start.6 = (f32[4,16,128]{2,1,0:T(8,128)S(1)}, f32[4,16,128]{2,1,0:T(8,128)S(1)}, u32[]{:S(2)}, u32[]{:S(2)}) collective-permute-start(f32[4,16,128]{2,1,0:T(8,128)S(1)} %get-tuple-element.19.own), channel_id=1, source_target_pairs={{0,24},{8,32},{16,40},{24,48},{32,56},{40,64},{48,72},{56,80},{64,... | collective-permute-start | bytes 98312 | tf_op jit(solution)/shard_map/ppermute | solution.py:173
  42.6 8.5 %collective-permute-start.7 = (f32[4,16,128]{2,1,0:T(8,128)S(1)}, f32[4,16,128]{2,1,0:T(8,128)S(1)}, u32[]{:S(2)}, u32[]{:S(2)}) collective-permute-start(f32[4,16,128]{2,1,0:T(8,128)S(1)} %get-tuple-element.20), channel_id=1, source_target_pairs={{0,1000},{8,1008},{16,1016},{24,0},{32,8},{40,16},{48,24},{56,32},... | collective-permute-start | bytes 98312 | tf_op jit(solution)/shard_map/ppermute | solution.py:173
  51.1 0.0 collective-permute-done.6.flo
  51.1 1.4 %collective-permute-done.7.fhi = f32[4,16,128]{2,1,0:T(8,128)S(1)} collective-permute-done((f32[4,16,128]{2,1,0:T(8,128)S(1)}, f32[4,16,128]{2,1,0:T(8,128)S(1)}, u32[]{:S(2)}, u32[]{:S(2)}) %collective-permute-start.7) | collective-permute-done | bytes 32800 | tf_op jit(solution)/shard_map/ppermute | solution.py:173
  52.6 1.9 %collective-permute-start.8 = (f32[14,16,128]{2,1,0:T(8,128)S(1)}, f32[14,16,128]{2,1,0:T(8,128)S(1)}, u32[]{:S(2)}, u32[]{:S(2)}) collective-permute-start(f32[14,16,128]{2,1,0:T(8,128)S(1)} %constant_dynamic-update-slice_fusion), channel_id=1, source_target_pairs={{0,8},{8,16},{16,24},{24,32},{32,40},{40,48},{48,56},{56,64},{64,7... | collective-permute-start | bytes 344072 | tf_op jit(solution)/shard_map/ppermute | solution.py:173
  54.5 6.7 %collective-permute-start.9 = (f32[14,16,128]{2,1,0:T(8,128)S(1)}, f32[14,16,128]{2,1,0:T(8,128)S(1)}, u32[]{:S(2)}, u32[]{:S(2)}) collective-permute-start(f32[14,16,128]{2,1,0:T(8,128)S(1)} %constant_dynamic-update-slice_fusion.5), channel_id=1, source_target_pairs={{0,1016},{8,0},{16,8},{24,16},{32,24},{40,32},{48,40},{56,48},{64,... | collective-permute-start | bytes 344072 | tf_op jit(solution)/shard_map/ppermute | solution.py:173
  61.3 0.2 collective-permute-done.8.nlo
  61.4 1.6 %collective-permute-done.9.nhi = f32[14,16,128]{2,1,0:T(8,128)S(1)} collective-permute-done((f32[14,16,128]{2,1,0:T(8,128)S(1)}, f32[14,16,128]{2,1,0:T(8,128)S(1)}, u32[]{:S(2)}, u32[]{:S(2)}) %collective-permute-start.9) | collective-permute-done | bytes 114720 | tf_op jit(solution)/shard_map/ppermute | solution.py:173
  63.0 3.1 %collective-permute-start.11 = (f32[32,8,128]{2,1,0:T(8,128)S(1)}, f32[32,8,128]{2,1,0:T(8,128)S(1)}, u32[]{:S(2)}, u32[]{:S(2)}) collective-permute-start(f32[32,8,128]{2,1,0:T(8,128)S(1)} %get-tuple-element.29), channel_id=1, source_target_pairs={{0,7},{1,0},{2,1},{3,2},{4,3},{5,4},{6,5},{7,6},{8,15},{9,8},{10,9... | collective-permute-start | bytes 393224 | tf_op jit(solution)/shard_map/ppermute | solution.py:173
  66.1 0.2 collective-permute-start.10
  66.3 2.6 %collective-permute-done.11.zrows = f32[32,8,128]{2,1,0:T(8,128)S(1)} collective-permute-done((f32[32,8,128]{2,1,0:T(8,128)S(1)}, f32[32,8,128]{2,1,0:T(8,128)S(1)}, u32[]{:S(2)}, u32[]{:S(2)}) %collective-permute-start.11) | collective-permute-done | bytes 131104 | tf_op jit(solution)/shard_map/ppermute | solution.py:173
  68.9 0.0 collective-permute-done.10.yrows
  68.9 1.9 %shard_map.30 = f32[4,32,256]{2,1,0:T(8,128)} custom-call(f32[6,48,256]{2,1,0:T(8,128)S(1)} %get-tuple-element.17.smooth, f32[6,48,256]{2,1,0:T(8,128)S(1)} %get-tuple-element.18.dens, f32[4,16,128]{2,1,0:T(8,128)S(1)} %get-tuple-element.19.own, f32[4,16,128]{2,1,0:T(8,128)S(1)} %collective-permute-done.6.flo, f32[4,16,128]{2,1,0:T(8,128)S(1)} %collective-permute-done.7.fhi, ...), custom_call_target="tpu_custom_call" | custom-call | tf_op jit(solution)/shard_map/pallas_call | solution.py:161
  (20 shorter events, 0.2 us)
Async XLA Ops:
  0.0 0.9 %slice-start = ((f32[4,32,256]{2,1,0:T(8,128)}), f32[3,32,256]{2,1,0:T(8,128)S(1)}, s32[]{:S(2)}) async-start(f32[4,32,256]{2,1,0:T(8,128)} %field.3), calls=%async_computation | async-start | bytes 196608 | tf_op jit(solution)/shard_map/slice | solution.py:191
  0.0 0.9 %slice-start.1 = ((f32[4,32,256]{2,1,0:T(8,128)}), f32[2,32,256]{2,1,0:T(8,128)S(1)}, s32[]{:S(2)}) async-start(f32[4,32,256]{2,1,0:T(8,128)} %density.3), calls=%async_computation.1 | async-start | bytes 131072 | tf_op jit(solution)/shard_map/slice | solution.py:191
  0.9 32.5 %copy-start = (f32[4,32,256]{2,1,0:T(8,128)S(1)}, f32[4,32,256]{2,1,0:T(8,128)}, u32[]{:S(2)}) copy-start(f32[4,32,256]{2,1,0:T(8,128)} %field.3) | copy-start | bytes 393220
  0.9 32.5 %copy-start.1 = (f32[4,32,256]{2,1,0:T(8,128)S(1)}, f32[4,32,256]{2,1,0:T(8,128)}, u32[]{:S(2)}) copy-start(f32[4,32,256]{2,1,0:T(8,128)} %density.3) | copy-start | bytes 393220
  0.9 32.5 %collective-permute-start = (f32[5,32,256]{2,1,0:T(8,128)S(1)}, f32[5,32,256]{2,1,0:T(8,128)S(1)}, u32[]{:S(2)}, u32[]{:S(2)}) collective-permute-start(f32[5,32,256]{2,1,0:T(8,128)S(1)} %pad_maximum_fusion.1), channel_id=1, source_target_pairs={{0,8},{8,16},{16,24},{24,32},{32,40},{40,48},{48,56},{56,64},{64,7... | collective-permute-start | bytes 491528 | tf_op jit(solution)/shard_map/ppermute | solution.py:173
  7.1 29.0 %collective-permute-start.1 = (f32[5,4,256]{2,1,0:T(4,128)}, f32[5,4,256]{2,1,0:T(4,128)S(1)}, u32[]{:S(2)}, u32[]{:S(2)}) collective-permute-start(f32[5,4,256]{2,1,0:T(4,128)} %get-tuple-element.14), channel_id=1, source_target_pairs={{0,1017},{1,1018},{2,1019},{3,1020},{4,1021},{5,1022},{6,1023},{7,... | collective-permute-start | bytes 61448 | tf_op jit(solution)/shard_map/ppermute | solution.py:181
  27.8 8.3 %collective-permute-start.3 = (f32[5,4,256]{2,1,0:T(4,128)}, f32[5,4,256]{2,1,0:T(4,128)S(1)}, u32[]{:S(2)}, u32[]{:S(2)}) collective-permute-start(f32[5,4,256]{2,1,0:T(4,128)} %get-tuple-element.16), channel_id=1, source_target_pairs={{0,1023},{1,1016},{2,1017},{3,1018},{4,1019},{5,1020},{6,1021},{7,... | collective-permute-start | bytes 61448 | tf_op jit(solution)/shard_map/ppermute | solution.py:181
  30.0 6.3 %collective-permute-start.2 = (f32[5,32,256]{2,1,0:T(8,128)}, f32[5,32,256]{2,1,0:T(8,128)S(1)}, u32[]{:S(2)}, u32[]{:S(2)}) collective-permute-start(f32[5,32,256]{2,1,0:T(8,128)} %get-tuple-element.15), channel_id=1, source_target_pairs={{0,1016},{8,0},{16,8},{24,16},{32,24},{40,32},{48,40},{56,48},{64,... | collective-permute-start | bytes 491528 | tf_op jit(solution)/shard_map/ppermute | solution.py:173
  33.5 3.7 %collective-permute-start.4 = (f32[13,4,256]{2,1,0:T(4,128)S(1)}, f32[13,4,256]{2,1,0:T(4,128)S(1)}, u32[]{:S(2)}, u32[]{:S(2)}) collective-permute-start(f32[13,4,256]{2,1,0:T(4,128)S(1)} %pad_maximum_fusion.2), channel_id=1, source_target_pairs={{0,1},{1,2},{2,3},{3,4},{4,5},{5,6},{6,7},{7,0},{8,9},{9,10},{10,1... | collective-permute-start | bytes 159752 | tf_op jit(solution)/shard_map/ppermute | solution.py:173
  36.0 3.9 %collective-permute-start.5 = (f32[13,4,256]{2,1,0:T(4,128)S(1)}, f32[13,4,256]{2,1,0:T(4,128)S(1)}, u32[]{:S(2)}, u32[]{:S(2)}) collective-permute-start(f32[13,4,256]{2,1,0:T(4,128)S(1)} %pad_maximum_fusion.3), channel_id=1, source_target_pairs={{0,7},{1,0},{2,1},{3,2},{4,3},{5,4},{6,5},{7,6},{8,15},{9,8},{10,9... | collective-permute-start | bytes 159752 | tf_op jit(solution)/shard_map/ppermute | solution.py:173
  40.7 10.4 %collective-permute-start.6 = (f32[4,16,128]{2,1,0:T(8,128)S(1)}, f32[4,16,128]{2,1,0:T(8,128)S(1)}, u32[]{:S(2)}, u32[]{:S(2)}) collective-permute-start(f32[4,16,128]{2,1,0:T(8,128)S(1)} %get-tuple-element.19.own), channel_id=1, source_target_pairs={{0,24},{8,32},{16,40},{24,48},{32,56},{40,64},{48,72},{56,80},{64,... | collective-permute-start | bytes 98312 | tf_op jit(solution)/shard_map/ppermute | solution.py:173
  42.6 9.9 %collective-permute-start.7 = (f32[4,16,128]{2,1,0:T(8,128)S(1)}, f32[4,16,128]{2,1,0:T(8,128)S(1)}, u32[]{:S(2)}, u32[]{:S(2)}) collective-permute-start(f32[4,16,128]{2,1,0:T(8,128)S(1)} %get-tuple-element.20), channel_id=1, source_target_pairs={{0,1000},{8,1008},{16,1016},{24,0},{32,8},{40,16},{48,24},{56,32},... | collective-permute-start | bytes 98312 | tf_op jit(solution)/shard_map/ppermute | solution.py:173
  52.6 8.9 %collective-permute-start.8 = (f32[14,16,128]{2,1,0:T(8,128)S(1)}, f32[14,16,128]{2,1,0:T(8,128)S(1)}, u32[]{:S(2)}, u32[]{:S(2)}) collective-permute-start(f32[14,16,128]{2,1,0:T(8,128)S(1)} %constant_dynamic-update-slice_fusion), channel_id=1, source_target_pairs={{0,8},{8,16},{16,24},{24,32},{32,40},{40,48},{48,56},{56,64},{64,7... | collective-permute-start | bytes 344072 | tf_op jit(solution)/shard_map/ppermute | solution.py:173
  54.5 8.5 %collective-permute-start.9 = (f32[14,16,128]{2,1,0:T(8,128)S(1)}, f32[14,16,128]{2,1,0:T(8,128)S(1)}, u32[]{:S(2)}, u32[]{:S(2)}) collective-permute-start(f32[14,16,128]{2,1,0:T(8,128)S(1)} %constant_dynamic-update-slice_fusion.5), channel_id=1, source_target_pairs={{0,1016},{8,0},{16,8},{24,16},{32,24},{40,32},{48,40},{56,48},{64,... | collective-permute-start | bytes 344072 | tf_op jit(solution)/shard_map/ppermute | solution.py:173
  63.0 5.9 %collective-permute-start.11 = (f32[32,8,128]{2,1,0:T(8,128)S(1)}, f32[32,8,128]{2,1,0:T(8,128)S(1)}, u32[]{:S(2)}, u32[]{:S(2)}) collective-permute-start(f32[32,8,128]{2,1,0:T(8,128)S(1)} %get-tuple-element.29), channel_id=1, source_target_pairs={{0,7},{1,0},{2,1},{3,2},{4,3},{5,4},{6,5},{7,6},{8,15},{9,8},{10,9... | collective-permute-start | bytes 393224 | tf_op jit(solution)/shard_map/ppermute | solution.py:173
  66.1 2.8 %collective-permute-start.10 = (f32[32,8,128]{2,1,0:T(8,128)S(1)}, f32[32,8,128]{2,1,0:T(8,128)S(1)}, u32[]{:S(2)}, u32[]{:S(2)}) collective-permute-start(f32[32,8,128]{2,1,0:T(8,128)S(1)} %get-tuple-element.30), channel_id=1, source_target_pairs={{0,1},{1,2},{2,3},{3,4},{4,5},{5,6},{6,7},{7,0},{8,9},{9,10},{10,1... | collective-permute-start | bytes 393224 | tf_op jit(solution)/shard_map/ppermute | solution.py:173

commit v7 on v5

--- a/solution.py
+++ b/solution.py
@@ -7,6 +7,18 @@
 
 mass = 0.02
 damping = 0.8
+
+
+def pair_of(ref, i, start, rows):
+    return ref[i, start - 1 : start - 1 + rows] + ref[i, start + 1 : start + 1 + rows]
+
+
+def jacobi_rows(v, rows, below, above, source, inv_step):
+    around = below + above + rows
+    around = around + pltpu.roll(v, 1, 1) + pltpu.roll(v, v.shape[1] - 1, 1)
+    square = v * v
+    top = inv_step * around - source - v * ((6.0 * inv_step + mass) + (mass / 3.0) * square)
+    return v + top / ((6.0 * inv_step + mass) / damping + (mass / damping) * square)
 
 
 def jacobi(v, below, above, source, inv_step):
@@ -35,7 +47,7 @@
     return total + jnp.dot(high, weights, preferred_element_type=jnp.float32)
 
 
-def fine_kernel(field, density, xhi, xlo, clo, chi, smooth, dens, coarse, coarse2, up, down, f, d, s1, pair, rows):
+def fine_kernel(field, density, xlo, xhi, clo, chi, smooth, dens, forward, backward, f, d, s1, pair, rows):
     f[0:3, 8:40] = xlo[0:3]
     f[3:7, 8:40] = field[...]
     f[7:10, 8:40] = xhi[0:3]
@@ -69,44 +81,45 @@
     third = lax.broadcasted_iota(jnp.int32, (256, 128), 0)
     half = lax.broadcasted_iota(jnp.int32, (256, 128), 1)
     weights = jnp.where(third >> 1 == half, 0.125, 0.0).astype(jnp.bfloat16)
-    coarse[...] = exact_dot(rows[...], weights).reshape(4, 16, 128)
-    coarse2[...] = coarse[...]
-    for face, layer in ((up, 3), (down, 2)):
+    coarse = exact_dot(rows[...], weights).reshape(4, 16, 128)
+    forward[0:4] = coarse
+    backward[0:4] = coarse
+    for target, layer in ((forward, 3), (backward, 2)):
         for j in range(4):
             at, lane = 8 + 16 * (j // 2), 128 * (j % 2)
-            face[j] = smooth[layer, at : at + 16, lane : lane + 128]
+            target[4 + j] = smooth[layer, at : at + 16, lane : lane + 128]
 
 
 def coarse_kernel(
-    smooth, dens, own, flo, fhi, nlo, nhi, yrows, zrows,
+    smooth, dens, own, nlo, nhi, flo, fhi, yrows, zrows,
     out, a, r, g, c0, c1, wide, corrected, post,
 ):
-    def place(rows, mine, far_low, far_high, low, high):
+    def place(rows, mine, low, high, far_low, far_high):
         for ref, at in ((a, 0), (r, 1)):
-            ref[0:1, rows] = low[at : at + 1]
-            ref[1:3, rows] = far_low[2 * at : 2 * at + 2]
-            ref[3:5, rows] = high[2 * at + 6 : 2 * at + 8]
-            ref[5:7, rows] = low[2 * at + 2 : 2 * at + 4]
+            ref[0:1, rows] = far_low[at : at + 1]
+            ref[1:3, rows] = far_low[2 * at + 2 : 2 * at + 4]
+            ref[3:5, rows] = far_low[2 * at + 6 : 2 * at + 8]
+            ref[5:7, rows] = low[2 * at : 2 * at + 2]
             ref[7:9, rows] = mine[2 * at : 2 * at + 2]
-            ref[9:11, rows] = high[2 * at + 2 : 2 * at + 4]
-            ref[11:13, rows] = low[2 * at + 6 : 2 * at + 8]
-            ref[13:15, rows] = far_high[2 * at : 2 * at + 2]
-            ref[15:16, rows] = high[at : at + 1]
-
-    place(slice(8, 24), own, flo, fhi, nlo, nhi)
+            ref[9:11, rows] = high[2 * at : 2 * at + 2]
+            ref[11:13, rows] = far_high[2 * at + 6 : 2 * at + 8]
+            ref[13:15, rows] = far_high[2 * at + 2 : 2 * at + 4]
+            ref[15:16, rows] = far_high[at : at + 1]
+
+    place(slice(8, 24), own, nlo, nhi, flo, fhi)
     for rows, side in ((slice(0, 8), yrows), (slice(24, 32), zrows)):
         place(rows, side.at[0:4], side.at[4:8], side.at[8:12], side.at[12:22], side.at[22:32])
     for i in range(16):
         v = a[i]
-        c0[i] = v - r[i] / ((1.5 + mass) / damping + (mass / damping) * (v * v))
+        c0[i, 8:40] = v - r[i] / ((1.5 + mass) / damping + (mass / damping) * (v * v))
     for i in range(1, 15):
         g[i] = operator(a[i], a[i - 1], a[i + 1], 0.25) + r[i]
     now, later = c0, c1
     for sweep in range(1, 6):
         for i in range(sweep, 16 - sweep):
-            later[i] = jacobi(now[i], now[i - 1], now[i + 1], g[i], 0.25)
+            later[i, 8:40] = jacobi_rows(now[i, 8:40], pair_of(now, i, 8, 32), now[i - 1, 8:40], now[i + 1, 8:40], g[i], 0.25)
         now, later = later, now
-    change = (now[5:11] - a[5:11]).reshape(192, 128)
+    change = (now[5:11, 8:40] - a[5:11]).reshape(192, 128)
     half = lax.broadcasted_iota(jnp.int32, (128, 256), 0)
     third = lax.broadcasted_iota(jnp.int32, (128, 256), 1)
     beside = ((third >> 1) + 2 * (third & 1) - 1) & 127
@@ -121,8 +134,8 @@
             wide[i, k, pl.ds(1, 32, stride=2)] = odd[:, 128 * k : 128 * k + 128]
     for j in range(4):
         at, lane = 8 + 16 * (j // 2), 128 * (j % 2)
-        corrected[0, at : at + 16, lane : lane + 128] = nlo[10 + j]
-        corrected[7, at : at + 16, lane : lane + 128] = nhi[10 + j]
+        corrected[0, at : at + 16, lane : lane + 128] = nlo[4 + j]
+        corrected[7, at : at + 16, lane : lane + 128] = nhi[4 + j]
     for i in range(8):
         near = i // 2 + 1
         beside_layer = near - 1 if i % 2 == 0 else near + 1
@@ -166,21 +179,23 @@
     xhi = send(jnp.concatenate([field[0:3], density[0:2]], 0), "gx", -1)
     clo = send(jnp.concatenate([xlo[:, 28:32], xhi[:, 28:32], field[:, 28:32], density[:, 28:32]], 0), "gy", 1)
     chi = send(jnp.concatenate([xlo[:, 0:4], xhi[:, 0:4], field[:, 0:4], density[:, 0:4]], 0), "gy", -1)
-    smooth, dens, own, own2, up, down = call(
+    smooth, dens, forward, backward = call(
         fine_kernel,
-        [(6, 48, 256), (6, 48, 256), (4, 16, 128), (4, 16, 128), (4, 16, 128), (4, 16, 128)],
+        [(6, 48, 256), (6, 48, 256), (8, 16, 128), (8, 16, 128)],
         [(10, 48, 256), (8, 48, 256), (8, 48, 256), (4, 2, 48, 128), (64, 256)],
-        field, density, xhi, xlo, clo, chi,
+        field, density, xlo, xhi, clo, chi,
     )
-    flo, fhi = send(own, "gx", 3), send(own2, "gx", -3)
-    nlo = send(jnp.concatenate([flo[1:2], flo[3:4], own, fhi, up], 0), "gx", 1)
-    nhi = send(jnp.concatenate([fhi[0:1], fhi[2:3], own, flo, down], 0), "gx", -1)
-    yrows, zrows = rows_from_sides([own, flo, fhi, nlo[0:10], nhi[0:10]])
+    own = forward[0:4]
+    nlo, nhi = send(forward, "gx", 1), send(backward, "gx", -1)
+    flo = send(jnp.concatenate([nlo[1:2], nlo[3:4], own, nhi[0:4]], 0), "gx", 3)
+    own = backward[0:4]
+    fhi = send(jnp.concatenate([nhi[0:1], nhi[2:3], own, nlo[0:4]], 0), "gx", -3)
+    yrows, zrows = rows_from_sides([own, nlo[0:4], nhi[0:4], flo, fhi])
     (out,) = call(
         coarse_kernel,
         [(4, 32, 256)],
-        [(16, 32, 128)] * 5 + [(6, 2, 64, 128), (8, 48, 256), (6, 48, 256)],
-        smooth, dens, own, flo, fhi, nlo, nhi, yrows, zrows,
+        [(16, 32, 128)] * 3 + [(16, 48, 128)] * 2 + [(6, 2, 64, 128), (8, 48, 256), (6, 48, 256)],
+        smooth, dens, own, nlo, nhi, flo, fhi, yrows, zrows,
     )
     return out
 

time: 70.3 us -> 67.9 us (0.966)
  waiting for transfers between devices: 17.1 us -> 14.5 us
  local copies, waits for them, and re-layouts: 1.08 us -> 1.81 us
    ppermute x10, waiting for transfers between devices: 17.1 us -> 14.5 us  [send(): lax.ppermute(values, axis, [(i, (i + step) % count) for i in range(count)])]
    slice x2 -> x9, local copies, waits for them, and re-layouts: 0.93 us -> 1.69 us  [the longest x2 0.93 us: body(): xhi = send(jnp.concatenate([field[0:3], density[0:2]], 0), 'gx', -1)]
where the time goes in v7:
time: 67.9 us; the launch traced here: 67.4 us
  starting transfers between devices  48 us (71%)
  waiting for transfers between devices  14.5 us (21%)
  Pallas kernels  2.71 us (4%)
  local copies, waits for them, and re-layouts  1.81 us (3%)
    ppermute x10, starting transfers between devices, send(): lax.ppermute(values, axis, [(i, (i + step) % count) for i in range(count)])  48 us
    ppermute x10, waiting for transfers between devices, send(): lax.ppermute(values, axis, [(i, (i + step) % count) for i in range(count)])  14.5 us
    pallas_call x2, Pallas kernels, call(): pl.pallas_call(kernel, out_shape=shapes, in_specs=[vmem] * len(args), out...  2.71 us
  transfers between devices with their start and end apart: 10, of which 8 were waited for; matrix products, arithmetic and copies ran while one was open for 0% of the time, Pallas kernels for 0%

profile of v7, /device:TPU:1, one launch (start us, length us, event | category | flops | bytes accessed | tf_op | source)
XLA Modules:
  0.0 67.4 jit_solution(6972248925758329251)
XLA Ops:
  0.0 0.0 copy-start
  0.0 0.9 %fusion.5 = (f32[2,32,256]{2,1,0:T(8,128)S(1)}, f32[2,32,256]{2,1,0:T(8,128)S(1)}) fusion(f32[4,32,256]{2,1,0:T(8,128)} %density.1), kind=kLoop, calls=%fused_computation.21 | loop fusion | bytes 262144 | tf_op jit(solution)/shard_map/slice | solution.py:179
  0.9 0.0 copy-done
  1.0 4.4 %collective-permute-start = (f32[5,32,256]{2,1,0:T(8,128)S(1)}, f32[5,32,256]{2,1,0:T(8,128)S(1)}, u32[]{:S(2)}, u32[]{:S(2)}) collective-permute-start(f32[5,32,256]{2,1,0:T(8,128)S(1)} %pad_maximum_fusion), channel_id=1, source_target_pairs={{0,8},{8,16},{16,24},{24,32},{32,40},{40,48},{48,56},{56,64},{64,7... | collective-permute-start | bytes 491528 | tf_op jit(solution)/shard_map/ppermute | solution.py:168
  5.4 0.0 copy-start.1
  5.4 19.4 %collective-permute-start.1 = (f32[5,32,256]{2,1,0:T(8,128)S(1)}, f32[5,32,256]{2,1,0:T(8,128)S(1)}, u32[]{:S(2)}, u32[]{:S(2)}) collective-permute-start(f32[5,32,256]{2,1,0:T(8,128)S(1)} %pad_maximum_fusion.1), channel_id=1, source_target_pairs={{0,1016},{8,0},{16,8},{24,16},{32,24},{40,32},{48,40},{56,48},{64,... | collective-permute-start | bytes 491528 | tf_op jit(solution)/shard_map/ppermute | solution.py:168
  24.8 0.0 copy-done.1
  24.8 1.8 %collective-permute-done.xlo = f32[5,32,256]{2,1,0:T(8,128)S(1)} collective-permute-done((f32[5,32,256]{2,1,0:T(8,128)S(1)}, f32[5,32,256]{2,1,0:T(8,128)S(1)}, u32[]{:S(2)}, u32[]{:S(2)}) %collective-permute-start) | collective-permute-done | bytes 163872 | tf_op jit(solution)/shard_map/ppermute | solution.py:168
  26.6 1.0 %collective-permute-done.1.xhi = f32[5,32,256]{2,1,0:T(8,128)S(1)} collective-permute-done((f32[5,32,256]{2,1,0:T(8,128)S(1)}, f32[5,32,256]{2,1,0:T(8,128)S(1)}, u32[]{:S(2)}, u32[]{:S(2)}) %collective-permute-start.1) | collective-permute-done | bytes 163872 | tf_op jit(solution)/shard_map/ppermute | solution.py:168
  27.7 2.7 %collective-permute-start.2 = (f32[18,4,256]{2,1,0:T(4,128)S(1)}, f32[18,4,256]{2,1,0:T(4,128)S(1)}, u32[]{:S(2)}, u32[]{:S(2)}) collective-permute-start(f32[18,4,256]{2,1,0:T(4,128)S(1)} %pad_maximum_fusion.4), channel_id=1, source_target_pairs={{0,1},{1,2},{2,3},{3,4},{4,5},{5,6},{6,7},{7,0},{8,9},{9,10},{10,1... | collective-permute-start | bytes 221192 | tf_op jit(solution)/shard_map/ppermute | solution.py:168
  30.3 0.0 collective-permute-start.3
  30.4 1.4 %collective-permute-done.2.clo = f32[18,4,256]{2,1,0:T(4,128)S(1)} collective-permute-done((f32[18,4,256]{2,1,0:T(4,128)S(1)}, f32[18,4,256]{2,1,0:T(4,128)S(1)}, u32[]{:S(2)}, u32[]{:S(2)}) %collective-permute-start.2) | collective-permute-done | bytes 73760 | tf_op jit(solution)/shard_map/ppermute | solution.py:168
  31.7 2.4 %collective-permute-done.3.chi = f32[18,4,256]{2,1,0:T(4,128)S(1)} collective-permute-done((f32[18,4,256]{2,1,0:T(4,128)S(1)}, f32[18,4,256]{2,1,0:T(4,128)S(1)}, u32[]{:S(2)}, u32[]{:S(2)}) %collective-permute-start.3) | collective-permute-done | bytes 73760 | tf_op jit(solution)/shard_map/ppermute | solution.py:168
  34.1 0.8 %shard_map.28 = (f32[6,48,256]{2,1,0:T(8,128)S(1)}, f32[6,48,256]{2,1,0:T(8,128)S(1)}, f32[8,16,128]{2,1,0:T(8,128)S(1)}, f32[8,16,128]{2,1,0:T(8,128)S(1)}) custom-call(f32[4,32,256]{2,1,0:T(8,128)S(1)} %copy-done, f32[4,32,256]{2,1,0:T(8,128)S(1)} %copy-done.1, f32[5,32,256]{2,1,0:T(8,128)S(1)} %collective-permute-done.xlo, ...), custom_call_target="tpu_custom_call" | custom-call | tf_op jit(solution)/shard_map/pallas_call | solution.py:156
  35.0 1.9 %collective-permute-start.4 = (f32[8,16,128]{2,1,0:T(8,128)S(1)}, f32[8,16,128]{2,1,0:T(8,128)S(1)}, u32[]{:S(2)}, u32[]{:S(2)}) collective-permute-start(f32[8,16,128]{2,1,0:T(8,128)S(1)} %get-tuple-element.12), channel_id=1, source_target_pairs={{0,8},{8,16},{16,24},{24,32},{32,40},{40,48},{48,56},{56,64},{64,7... | collective-permute-start | bytes 196616 | tf_op jit(solution)/shard_map/ppermute | solution.py:168
  36.9 7.4 %collective-permute-start.5 = (f32[8,16,128]{2,1,0:T(8,128)S(1)}, f32[8,16,128]{2,1,0:T(8,128)S(1)}, u32[]{:S(2)}, u32[]{:S(2)}) collective-permute-start(f32[8,16,128]{2,1,0:T(8,128)S(1)} %get-tuple-element.11), channel_id=1, source_target_pairs={{0,1016},{8,0},{16,8},{24,16},{32,24},{40,32},{48,40},{56,48},{64,... | collective-permute-start | bytes 196616 | tf_op jit(solution)/shard_map/ppermute | solution.py:168
  44.4 0.4 collective-permute-done.4.nlo
  44.8 0.0 copy-start.2
  44.8 0.9 %collective-permute-done.5.nhi = f32[8,16,128]{2,1,0:T(8,128)S(1)} collective-permute-done((f32[8,16,128]{2,1,0:T(8,128)S(1)}, f32[8,16,128]{2,1,0:T(8,128)S(1)}, u32[]{:S(2)}, u32[]{:S(2)}) %collective-permute-start.5) | collective-permute-done | bytes 65568 | tf_op jit(solution)/shard_map/ppermute | solution.py:168
  45.7 1.9 %collective-permute-start.6 = (f32[10,16,128]{2,1,0:T(8,128)S(1)}, f32[10,16,128]{2,1,0:T(8,128)S(1)}, u32[]{:S(2)}, u32[]{:S(2)}) collective-permute-start(f32[10,16,128]{2,1,0:T(8,128)S(1)} %pad_maximum_fusion.2), channel_id=1, source_target_pairs={{0,24},{8,32},{16,40},{24,48},{32,56},{40,64},{48,72},{56,80},{64,... | collective-permute-start | bytes 245768 | tf_op jit(solution)/shard_map/ppermute | solution.py:168
  47.6 0.0 copy-done.2
  47.6 0.0 slice-start
  47.7 0.7 %slice-done = f32[4,16,128]{2,1,0:T(8,128)S(1)} async-done(((f32[8,16,128]{2,1,0:T(8,128)}), f32[4,16,128]{2,1,0:T(8,128)S(1)}, s32[]{:S(2)}) %slice-start) | async-done | bytes 32792 | tf_op jit(solution)/shard_map/slice | solution.py:192
  48.4 0.0 copy-start.3
  48.4 8.6 %collective-permute-start.7 = (f32[10,16,128]{2,1,0:T(8,128)S(1)}, f32[10,16,128]{2,1,0:T(8,128)S(1)}, u32[]{:S(2)}, u32[]{:S(2)}) collective-permute-start(f32[10,16,128]{2,1,0:T(8,128)S(1)} %pad_maximum_fusion.3), channel_id=1, source_target_pairs={{0,1000},{8,1008},{16,1016},{24,0},{32,8},{40,16},{48,24},{56,32},... | collective-permute-start | bytes 245768 | tf_op jit(solution)/shard_map/ppermute | solution.py:168
  57.0 0.0 copy-done.3
  57.1 0.0 collective-permute-done.6.flo
  57.1 4.0 %collective-permute-done.7.fhi = f32[10,16,128]{2,1,0:T(8,128)S(1)} collective-permute-done((f32[10,16,128]{2,1,0:T(8,128)S(1)}, f32[10,16,128]{2,1,0:T(8,128)S(1)}, u32[]{:S(2)}, u32[]{:S(2)}) %collective-permute-start.7) | collective-permute-done | bytes 81952 | tf_op jit(solution)/shard_map/ppermute | solution.py:168
  61.1 0.9 %collective-permute-start.9 = (f32[32,8,128]{2,1,0:T(8,128)S(1)}, f32[32,8,128]{2,1,0:T(8,128)S(1)}, u32[]{:S(2)}, u32[]{:S(2)}) collective-permute-start(f32[32,8,128]{2,1,0:T(8,128)S(1)} %get-tuple-element.25), channel_id=1, source_target_pairs={{0,7},{1,0},{2,1},{3,2},{4,3},{5,4},{6,5},{7,6},{8,15},{9,8},{10,9... | collective-permute-start | bytes 393224 | tf_op jit(solution)/shard_map/ppermute | solution.py:168
  62.0 0.9 %collective-permute-start.8 = (f32[32,8,128]{2,1,0:T(8,128)S(1)}, f32[32,8,128]{2,1,0:T(8,128)S(1)}, u32[]{:S(2)}, u32[]{:S(2)}) collective-permute-start(f32[32,8,128]{2,1,0:T(8,128)S(1)} %get-tuple-element.26), channel_id=1, source_target_pairs={{0,1},{1,2},{2,3},{3,4},{4,5},{5,6},{6,7},{7,0},{8,9},{9,10},{10,1... | collective-permute-start | bytes 393224 | tf_op jit(solution)/shard_map/ppermute | solution.py:168
  62.9 2.6 %collective-permute-done.9.zrows = f32[32,8,128]{2,1,0:T(8,128)S(1)} collective-permute-done((f32[32,8,128]{2,1,0:T(8,128)S(1)}, f32[32,8,128]{2,1,0:T(8,128)S(1)}, u32[]{:S(2)}, u32[]{:S(2)}) %collective-permute-start.9) | collective-permute-done | bytes 131104 | tf_op jit(solution)/shard_map/ppermute | solution.py:168
  65.5 0.0 collective-permute-done.8.yrows
  65.5 1.9 %shard_map.29 = f32[4,32,256]{2,1,0:T(8,128)} custom-call(f32[6,48,256]{2,1,0:T(8,128)S(1)} %get-tuple-element.9.smooth, f32[6,48,256]{2,1,0:T(8,128)S(1)} %get-tuple-element.10.dens, f32[4,16,128]{2,1,0:T(8,128)S(1)} %slice.110.own, f32[8,16,128]{2,1,0:T(8,128)S(1)} %copy-done.3, f32[8,16,128]{2,1,0:T(8,128)S(1)} %collective-permute-done.5.nhi, ...), custom_call_target="tpu_custom_call" | custom-call | tf_op jit(solution)/shard_map/pallas_call | solution.py:156
  (20 shorter events, 0.2 us)
Async XLA Ops:
  0.0 1.0 %copy-start = (f32[4,32,256]{2,1,0:T(8,128)S(1)}, f32[4,32,256]{2,1,0:T(8,128)}, u32[]{:S(2)}) copy-start(f32[4,32,256]{2,1,0:T(8,128)} %field.1) | copy-start | bytes 393220
  1.0 25.6 %collective-permute-start = (f32[5,32,256]{2,1,0:T(8,128)S(1)}, f32[5,32,256]{2,1,0:T(8,128)S(1)}, u32[]{:S(2)}, u32[]{:S(2)}) collective-permute-start(f32[5,32,256]{2,1,0:T(8,128)S(1)} %pad_maximum_fusion), channel_id=1, source_target_pairs={{0,8},{8,16},{16,24},{24,32},{32,40},{40,48},{48,56},{56,64},{64,7... | collective-permute-start | bytes 491528 | tf_op jit(solution)/shard_map/ppermute | solution.py:168
  5.4 19.4 %copy-start.1 = (f32[4,32,256]{2,1,0:T(8,128)S(1)}, f32[4,32,256]{2,1,0:T(8,128)}, u32[]{:S(2)}) copy-start(f32[4,32,256]{2,1,0:T(8,128)} %density.1) | copy-start | bytes 393220
  5.4 22.2 %collective-permute-start.1 = (f32[5,32,256]{2,1,0:T(8,128)S(1)}, f32[5,32,256]{2,1,0:T(8,128)S(1)}, u32[]{:S(2)}, u32[]{:S(2)}) collective-permute-start(f32[5,32,256]{2,1,0:T(8,128)S(1)} %pad_maximum_fusion.1), channel_id=1, source_target_pairs={{0,1016},{8,0},{16,8},{24,16},{32,24},{40,32},{48,40},{56,48},{64,... | collective-permute-start | bytes 491528 | tf_op jit(solution)/shard_map/ppermute | solution.py:168
  27.7 4.1 %collective-permute-start.2 = (f32[18,4,256]{2,1,0:T(4,128)S(1)}, f32[18,4,256]{2,1,0:T(4,128)S(1)}, u32[]{:S(2)}, u32[]{:S(2)}) collective-permute-start(f32[18,4,256]{2,1,0:T(4,128)S(1)} %pad_maximum_fusion.4), channel_id=1, source_target_pairs={{0,1},{1,2},{2,3},{3,4},{4,5},{5,6},{6,7},{7,0},{8,9},{9,10},{10,1... | collective-permute-start | bytes 221192 | tf_op jit(solution)/shard_map/ppermute | solution.py:168
  30.3 3.8 %collective-permute-start.3 = (f32[18,4,256]{2,1,0:T(4,128)S(1)}, f32[18,4,256]{2,1,0:T(4,128)S(1)}, u32[]{:S(2)}, u32[]{:S(2)}) collective-permute-start(f32[18,4,256]{2,1,0:T(4,128)S(1)} %pad_maximum_fusion.5), channel_id=1, source_target_pairs={{0,7},{1,0},{2,1},{3,2},{4,3},{5,4},{6,5},{7,6},{8,15},{9,8},{10,9... | collective-permute-start | bytes 221192 | tf_op jit(solution)/shard_map/ppermute | solution.py:168
  35.0 9.8 %collective-permute-start.4 = (f32[8,16,128]{2,1,0:T(8,128)S(1)}, f32[8,16,128]{2,1,0:T(8,128)S(1)}, u32[]{:S(2)}, u32[]{:S(2)}) collective-permute-start(f32[8,16,128]{2,1,0:T(8,128)S(1)} %get-tuple-element.12), channel_id=1, source_target_pairs={{0,8},{8,16},{16,24},{24,32},{32,40},{40,48},{48,56},{56,64},{64,7... | collective-permute-start | bytes 196616 | tf_op jit(solution)/shard_map/ppermute | solution.py:168
  36.9 8.8 %collective-permute-start.5 = (f32[8,16,128]{2,1,0:T(8,128)S(1)}, f32[8,16,128]{2,1,0:T(8,128)S(1)}, u32[]{:S(2)}, u32[]{:S(2)}) collective-permute-start(f32[8,16,128]{2,1,0:T(8,128)S(1)} %get-tuple-element.11), channel_id=1, source_target_pairs={{0,1016},{8,0},{16,8},{24,16},{32,24},{40,32},{48,40},{56,48},{64,... | collective-permute-start | bytes 196616 | tf_op jit(solution)/shard_map/ppermute | solution.py:168
  44.8 2.9 %copy-start.2 = (f32[8,16,128]{2,1,0:T(8,128)}, f32[8,16,128]{2,1,0:T(8,128)S(1)}, u32[]{:S(2)}) copy-start(f32[8,16,128]{2,1,0:T(8,128)S(1)} %collective-permute-done.4.nlo) | copy-start | bytes 196612
  45.7 11.4 %collective-permute-start.6 = (f32[10,16,128]{2,1,0:T(8,128)S(1)}, f32[10,16,128]{2,1,0:T(8,128)S(1)}, u32[]{:S(2)}, u32[]{:S(2)}) collective-permute-start(f32[10,16,128]{2,1,0:T(8,128)S(1)} %pad_maximum_fusion.2), channel_id=1, source_target_pairs={{0,24},{8,32},{16,40},{24,48},{32,56},{40,64},{48,72},{56,80},{64,... | collective-permute-start | bytes 245768 | tf_op jit(solution)/shard_map/ppermute | solution.py:168
  47.6 0.8 %slice-start = ((f32[8,16,128]{2,1,0:T(8,128)}), f32[4,16,128]{2,1,0:T(8,128)S(1)}, s32[]{:S(2)}) async-start(f32[8,16,128]{2,1,0:T(8,128)} %copy-done.2), calls=%async_computation | async-start | bytes 65536 | tf_op jit(solution)/shard_map/slice | solution.py:192
  48.4 8.6 %copy-start.3 = (f32[8,16,128]{2,1,0:T(8,128)S(1)}, f32[8,16,128]{2,1,0:T(8,128)}, u32[]{:S(2)}) copy-start(f32[8,16,128]{2,1,0:T(8,128)} %copy-done.2) | copy-start | bytes 196612
  48.4 12.7 %collective-permute-start.7 = (f32[10,16,128]{2,1,0:T(8,128)S(1)}, f32[10,16,128]{2,1,0:T(8,128)S(1)}, u32[]{:S(2)}, u32[]{:S(2)}) collective-permute-start(f32[10,16,128]{2,1,0:T(8,128)S(1)} %pad_maximum_fusion.3), channel_id=1, source_target_pairs={{0,1000},{8,1008},{16,1016},{24,0},{32,8},{40,16},{48,24},{56,32},... | collective-permute-start | bytes 245768 | tf_op jit(solution)/shard_map/ppermute | solution.py:168
  61.1 4.4 %collective-permute-start.9 = (f32[32,8,128]{2,1,0:T(8,128)S(1)}, f32[32,8,128]{2,1,0:T(8,128)S(1)}, u32[]{:S(2)}, u32[]{:S(2)}) collective-permute-start(f32[32,8,128]{2,1,0:T(8,128)S(1)} %get-tuple-element.25), channel_id=1, source_target_pairs={{0,7},{1,0},{2,1},{3,2},{4,3},{5,4},{6,5},{7,6},{8,15},{9,8},{10,9... | collective-permute-start | bytes 393224 | tf_op jit(solution)/shard_map/ppermute | solution.py:168
  62.0 3.5 %collective-permute-start.8 = (f32[32,8,128]{2,1,0:T(8,128)S(1)}, f32[32,8,128]{2,1,0:T(8,128)S(1)}, u32[]{:S(2)}, u32[]{:S(2)}) collective-permute-start(f32[32,8,128]{2,1,0:T(8,128)S(1)} %get-tuple-element.26), channel_id=1, source_target_pairs={{0,1},{1,2},{2,3},{3,4},{4,5},{5,6},{6,7},{7,0},{8,9},{9,10},{10,1... | collective-permute-start | bytes 393224 | tf_op jit(solution)/shard_map/ppermute | solution.py:168

commit v8 on v5

--- a/solution.py
+++ b/solution.py
@@ -7,6 +7,18 @@
 
 mass = 0.02
 damping = 0.8
+
+
+def pair_of(ref, i, start, rows):
+    return ref[i, start - 1 : start - 1 + rows] + ref[i, start + 1 : start + 1 + rows]
+
+
+def jacobi_rows(v, rows, below, above, source, inv_step):
+    around = below + above + rows
+    around = around + pltpu.roll(v, 1, 1) + pltpu.roll(v, v.shape[1] - 1, 1)
+    square = v * v
+    top = inv_step * around - source - v * ((6.0 * inv_step + mass) + (mass / 3.0) * square)
+    return v + top / ((6.0 * inv_step + mass) / damping + (mass / damping) * square)
 
 
 def jacobi(v, below, above, source, inv_step):
@@ -35,7 +47,7 @@
     return total + jnp.dot(high, weights, preferred_element_type=jnp.float32)
 
 
-def fine_kernel(field, density, xhi, xlo, clo, chi, smooth, dens, coarse, coarse2, up, down, f, d, s1, pair, rows):
+def fine_kernel(field, density, xlo, xhi, clo, chi, smooth, dens, coarse, coarse2, up, down, f, d, s1, pair, rows):
     f[0:3, 8:40] = xlo[0:3]
     f[3:7, 8:40] = field[...]
     f[7:10, 8:40] = xhi[0:3]
@@ -78,35 +90,41 @@
 
 
 def coarse_kernel(
-    smooth, dens, own, flo, fhi, nlo, nhi, yrows, zrows,
+    smooth, dens, own, flo, fhi, nlo, nhi, zrows, yrows,
     out, a, r, g, c0, c1, wide, corrected, post,
 ):
-    def place(rows, mine, far_low, far_high, low, high):
-        for ref, at in ((a, 0), (r, 1)):
-            ref[0:1, rows] = low[at : at + 1]
-            ref[1:3, rows] = far_low[2 * at : 2 * at + 2]
-            ref[3:5, rows] = high[2 * at + 6 : 2 * at + 8]
-            ref[5:7, rows] = low[2 * at + 2 : 2 * at + 4]
+    for ref, at in ((a, 0), (r, 1)):
+        ref[0:1, 8:24] = nlo[at : at + 1]
+        ref[1:3, 8:24] = flo[2 * at : 2 * at + 2]
+        ref[13:15, 8:24] = fhi[2 * at : 2 * at + 2]
+        ref[15:16, 8:24] = nhi[at : at + 1]
+        for rows, mine, low, high, start in (
+            (slice(8, 24), own, nlo, nhi, 2),
+            (slice(0, 8), yrows.at[0:4], yrows.at[4:12], yrows.at[12:20], 0),
+            (slice(24, 32), zrows.at[0:4], zrows.at[4:12], zrows.at[12:20], 0),
+        ):
+            at_own, at_two = start + 2 * at, start + 4 + 2 * at
+            ref[3:5, rows] = high[at_two : at_two + 2]
+            ref[5:7, rows] = low[at_own : at_own + 2]
             ref[7:9, rows] = mine[2 * at : 2 * at + 2]
-            ref[9:11, rows] = high[2 * at + 2 : 2 * at + 4]
-            ref[11:13, rows] = low[2 * at + 6 : 2 * at + 8]
-            ref[13:15, rows] = far_high[2 * at : 2 * at + 2]
-            ref[15:16, rows] = high[at : at + 1]
-
-    place(slice(8, 24), own, flo, fhi, nlo, nhi)
-    for rows, side in ((slice(0, 8), yrows), (slice(24, 32), zrows)):
-        place(rows, side.at[0:4], side.at[4:8], side.at[8:12], side.at[12:22], side.at[22:32])
+            ref[9:11, rows] = high[at_own : at_own + 2]
+            ref[11:13, rows] = low[at_two : at_two + 2]
+        for rows, side in ((slice(4, 8), yrows), (slice(24, 28), zrows)):
+            ref[1:3, rows] = side[20 + 2 * at : 22 + 2 * at, 0:4]
+            ref[0:1, rows] = side[24 + at : 25 + at, 0:4]
+            ref[13:15, rows] = side[20 + 2 * at : 22 + 2 * at, 4:8]
+            ref[15:16, rows] = side[24 + at : 25 + at, 4:8]
     for i in range(16):
         v = a[i]
-        c0[i] = v - r[i] / ((1.5 + mass) / damping + (mass / damping) * (v * v))
+        c0[i, 8:40] = v - r[i] / ((1.5 + mass) / damping + (mass / damping) * (v * v))
     for i in range(1, 15):
         g[i] = operator(a[i], a[i - 1], a[i + 1], 0.25) + r[i]
     now, later = c0, c1
     for sweep in range(1, 6):
         for i in range(sweep, 16 - sweep):
-            later[i] = jacobi(now[i], now[i - 1], now[i + 1], g[i], 0.25)
+            later[i, 8:40] = jacobi_rows(now[i, 8:40], pair_of(now, i, 8, 32), now[i - 1, 8:40], now[i + 1, 8:40], g[i], 0.25)
         now, later = later, now
-    change = (now[5:11] - a[5:11]).reshape(192, 128)
+    change = (now[5:11, 8:40] - a[5:11]).reshape(192, 128)
     half = lax.broadcasted_iota(jnp.int32, (128, 256), 0)
     third = lax.broadcasted_iota(jnp.int32, (128, 256), 1)
     beside = ((third >> 1) + 2 * (third & 1) - 1) & 127
@@ -155,10 +173,12 @@
     return lax.ppermute(values, axis, [(i, (i + step) % count) for i in range(count)])
 
 
-def rows_from_sides(pieces):
-    last = jnp.concatenate([piece[:, 8:16] for piece in pieces], 0)
-    first = jnp.concatenate([piece[:, 0:8] for piece in pieces], 0)
-    return send(last, "gy", 1), send(first, "gy", -1)
+def rows_from_sides(near, far):
+    last = [piece[:, 8:16] for piece in near]
+    last += [jnp.concatenate([low[:, 12:16], high[:, 12:16]], 1) for low, high in far]
+    first = [piece[:, 0:8] for piece in near]
+    first += [jnp.concatenate([low[:, 0:4], high[:, 0:4]], 1) for low, high in far]
+    return send(jnp.concatenate(last, 0), "gy", 1), send(jnp.concatenate(first, 0), "gy", -1)
 
 
 def body(density, field):
@@ -170,17 +190,17 @@
         fine_kernel,
         [(6, 48, 256), (6, 48, 256), (4, 16, 128), (4, 16, 128), (4, 16, 128), (4, 16, 128)],
         [(10, 48, 256), (8, 48, 256), (8, 48, 256), (4, 2, 48, 128), (64, 256)],
-        field, density, xhi, xlo, clo, chi,
+        field, density, xlo, xhi, clo, chi,
     )
     flo, fhi = send(own, "gx", 3), send(own2, "gx", -3)
     nlo = send(jnp.concatenate([flo[1:2], flo[3:4], own, fhi, up], 0), "gx", 1)
     nhi = send(jnp.concatenate([fhi[0:1], fhi[2:3], own, flo, down], 0), "gx", -1)
-    yrows, zrows = rows_from_sides([own, flo, fhi, nlo[0:10], nhi[0:10]])
+    yrows, zrows = rows_from_sides([own, nlo[2:10], nhi[2:10]], [(flo, fhi), (nlo[0:2], nhi[0:2])])
     (out,) = call(
         coarse_kernel,
         [(4, 32, 256)],
-        [(16, 32, 128)] * 5 + [(6, 2, 64, 128), (8, 48, 256), (6, 48, 256)],
-        smooth, dens, own, flo, fhi, nlo, nhi, yrows, zrows,
+        [(16, 32, 128)] * 3 + [(16, 48, 128)] * 2 + [(6, 2, 64, 128), (8, 48, 256), (6, 48, 256)],
+        smooth, dens, own, flo, fhi, nlo, nhi, zrows, yrows,
     )
     return out
 

time: 70.3 us -> 65.8 us (0.936)
  waiting for transfers between devices: 17.1 us -> 11.6 us
    ppermute x10, waiting for transfers between devices: 17.1 us -> 11.6 us  [send(): lax.ppermute(values, axis, [(i, (i + step) % count) for i in range(count)])]
    ppermute x10, starting transfers between devices: 48.4 us -> 49.1 us  [send(): lax.ppermute(values, axis, [(i, (i + step) % count) for i in range(count)])]
  transfers between devices with their start and end apart: 10 -> 10, of which waited for: 8 -> 7; matrix products, arithmetic and copies ran while one was open for 0% -> 0% of each run, Pallas kernels for 0% -> 0%
where the time goes in v8:
time: 65.8 us; the launch traced here: 65 us
  starting transfers between devices  49.1 us (75%)
  waiting for transfers between devices  11.6 us (18%)
  Pallas kernels  2.74 us (4%)
  local copies, waits for them, and re-layouts  1.09 us (2%)
    ppermute x10, starting transfers between devices, send(): lax.ppermute(values, axis, [(i, (i + step) % count) for i in range(count)])  49.1 us
    ppermute x10, waiting for transfers between devices, send(): lax.ppermute(values, axis, [(i, (i + step) % count) for i in range(count)])  11.6 us
    pallas_call x2, Pallas kernels, call(): pl.pallas_call(kernel, out_shape=shapes, in_specs=[vmem] * len(args), out...  2.74 us
  transfers between devices with their start and end apart: 10, of which 7 were waited for; matrix products, arithmetic and copies ran while one was open for 0% of the time, Pallas kernels for 0%

profile of v8, /device:TPU:1, one launch (start us, length us, event | category | flops | bytes accessed | tf_op | source)
XLA Modules:
  0.0 65.0 jit_solution(1957156200479166395)
XLA Ops:
  0.0 0.0 copy-start
  0.0 0.9 %fusion.5 = (f32[2,32,256]{2,1,0:T(8,128)S(1)}, f32[2,32,256]{2,1,0:T(8,128)S(1)}) fusion(f32[4,32,256]{2,1,0:T(8,128)} %density.1), kind=kLoop, calls=%fused_computation.29 | loop fusion | bytes 262144 | tf_op jit(solution)/shard_map/slice | solution.py:186
  0.9 0.0 copy-done
  1.0 4.4 %collective-permute-start = (f32[5,32,256]{2,1,0:T(8,128)S(1)}, f32[5,32,256]{2,1,0:T(8,128)S(1)}, u32[]{:S(2)}, u32[]{:S(2)}) collective-permute-start(f32[5,32,256]{2,1,0:T(8,128)S(1)} %pad_maximum_fusion), channel_id=1, source_target_pairs={{0,8},{8,16},{16,24},{24,32},{32,40},{40,48},{48,56},{56,64},{64,7... | collective-permute-start | bytes 491528 | tf_op jit(solution)/shard_map/ppermute | solution.py:173
  5.4 0.0 copy-start.1
  5.4 19.4 %collective-permute-start.1 = (f32[5,32,256]{2,1,0:T(8,128)S(1)}, f32[5,32,256]{2,1,0:T(8,128)S(1)}, u32[]{:S(2)}, u32[]{:S(2)}) collective-permute-start(f32[5,32,256]{2,1,0:T(8,128)S(1)} %pad_maximum_fusion.1), channel_id=1, source_target_pairs={{0,1016},{8,0},{16,8},{24,16},{32,24},{40,32},{48,40},{56,48},{64,... | collective-permute-start | bytes 491528 | tf_op jit(solution)/shard_map/ppermute | solution.py:173
  24.8 0.0 copy-done.1
  24.8 2.8 %collective-permute-done.1.xhi = f32[5,32,256]{2,1,0:T(8,128)S(1)} collective-permute-done((f32[5,32,256]{2,1,0:T(8,128)S(1)}, f32[5,32,256]{2,1,0:T(8,128)S(1)}, u32[]{:S(2)}, u32[]{:S(2)}) %collective-permute-start.1) | collective-permute-done | bytes 163872 | tf_op jit(solution)/shard_map/ppermute | solution.py:173
  27.6 0.0 collective-permute-done.xlo
  27.7 2.7 %collective-permute-start.2 = (f32[18,4,256]{2,1,0:T(4,128)S(1)}, f32[18,4,256]{2,1,0:T(4,128)S(1)}, u32[]{:S(2)}, u32[]{:S(2)}) collective-permute-start(f32[18,4,256]{2,1,0:T(4,128)S(1)} %pad_maximum_fusion.2), channel_id=1, source_target_pairs={{0,1},{1,2},{2,3},{3,4},{4,5},{5,6},{6,7},{7,0},{8,9},{9,10},{10,1... | collective-permute-start | bytes 221192 | tf_op jit(solution)/shard_map/ppermute | solution.py:173
  30.4 0.0 collective-permute-start.3
  30.4 1.4 %collective-permute-done.2.clo = f32[18,4,256]{2,1,0:T(4,128)S(1)} collective-permute-done((f32[18,4,256]{2,1,0:T(4,128)S(1)}, f32[18,4,256]{2,1,0:T(4,128)S(1)}, u32[]{:S(2)}, u32[]{:S(2)}) %collective-permute-start.2) | collective-permute-done | bytes 73760 | tf_op jit(solution)/shard_map/ppermute | solution.py:173
  31.8 2.4 %collective-permute-done.3.chi = f32[18,4,256]{2,1,0:T(4,128)S(1)} collective-permute-done((f32[18,4,256]{2,1,0:T(4,128)S(1)}, f32[18,4,256]{2,1,0:T(4,128)S(1)}, u32[]{:S(2)}, u32[]{:S(2)}) %collective-permute-start.3) | collective-permute-done | bytes 73760 | tf_op jit(solution)/shard_map/ppermute | solution.py:173
  34.2 0.8 %shard_map.28 = (f32[6,48,256]{2,1,0:T(8,128)S(1)}, f32[6,48,256]{2,1,0:T(8,128)S(1)}, f32[4,16,128]{2,1,0:T(8,128)S(1)}, f32[4,16,128]{2,1,0:T(8,128)S(1)}, f32...) custom-call(f32[4,32,256]{2,1,0:T(8,128)S(1)} %copy-done, f32[4,32,256]{2,1,0:T(8,128)S(1)} %copy-done.1, ...), custom_call_target="tpu_custom_call" | custom-call | tf_op jit(solution)/shard_map/pallas_call | solution.py:161
  35.0 1.9 %collective-permute-start.4 = (f32[4,16,128]{2,1,0:T(8,128)S(1)}, f32[4,16,128]{2,1,0:T(8,128)S(1)}, u32[]{:S(2)}, u32[]{:S(2)}) collective-permute-start(f32[4,16,128]{2,1,0:T(8,128)S(1)} %get-tuple-element.13.own), channel_id=1, source_target_pairs={{0,24},{8,32},{16,40},{24,48},{32,56},{40,64},{48,72},{56,80},{64,... | collective-permute-start | bytes 98312 | tf_op jit(solution)/shard_map/ppermute | solution.py:173
  36.9 8.5 %collective-permute-start.5 = (f32[4,16,128]{2,1,0:T(8,128)S(1)}, f32[4,16,128]{2,1,0:T(8,128)S(1)}, u32[]{:S(2)}, u32[]{:S(2)}) collective-permute-start(f32[4,16,128]{2,1,0:T(8,128)S(1)} %get-tuple-element.14), channel_id=1, source_target_pairs={{0,1000},{8,1008},{16,1016},{24,0},{32,8},{40,16},{48,24},{56,32},... | collective-permute-start | bytes 98312 | tf_op jit(solution)/shard_map/ppermute | solution.py:173
  45.5 1.0 %collective-permute-done.5.fhi = f32[4,16,128]{2,1,0:T(8,128)S(1)} collective-permute-done((f32[4,16,128]{2,1,0:T(8,128)S(1)}, f32[4,16,128]{2,1,0:T(8,128)S(1)}, u32[]{:S(2)}, u32[]{:S(2)}) %collective-permute-start.5) | collective-permute-done | bytes 32800 | tf_op jit(solution)/shard_map/ppermute | solution.py:173
  46.4 0.0 collective-permute-done.4.flo
  46.5 1.9 %collective-permute-start.6 = (f32[14,16,128]{2,1,0:T(8,128)S(1)}, f32[14,16,128]{2,1,0:T(8,128)S(1)}, u32[]{:S(2)}, u32[]{:S(2)}) collective-permute-start(f32[14,16,128]{2,1,0:T(8,128)S(1)} %constant_dynamic-update-slice_fusion), channel_id=1, source_target_pairs={{0,8},{8,16},{16,24},{24,32},{32,40},{40,48},{48,56},{56,64},{64,7... | collective-permute-start | bytes 344072 | tf_op jit(solution)/shard_map/ppermute | solution.py:173
  48.5 7.7 %collective-permute-start.7 = (f32[14,16,128]{2,1,0:T(8,128)S(1)}, f32[14,16,128]{2,1,0:T(8,128)S(1)}, u32[]{:S(2)}, u32[]{:S(2)}) collective-permute-start(f32[14,16,128]{2,1,0:T(8,128)S(1)} %constant_dynamic-update-slice_fusion.5), channel_id=1, source_target_pairs={{0,1016},{8,0},{16,8},{24,16},{32,24},{40,32},{48,40},{56,48},{64,... | collective-permute-start | bytes 344072 | tf_op jit(solution)/shard_map/ppermute | solution.py:173
  56.2 0.2 collective-permute-done.6.nlo
  56.4 1.6 %collective-permute-done.7.nhi = f32[14,16,128]{2,1,0:T(8,128)S(1)} collective-permute-done((f32[14,16,128]{2,1,0:T(8,128)S(1)}, f32[14,16,128]{2,1,0:T(8,128)S(1)}, u32[]{:S(2)}, u32[]{:S(2)}) %collective-permute-start.7) | collective-permute-done | bytes 114720 | tf_op jit(solution)/shard_map/ppermute | solution.py:173
  58.0 2.1 %collective-permute-start.8 = (f32[26,8,128]{2,1,0:T(8,128)S(1)}, f32[26,8,128]{2,1,0:T(8,128)S(1)}, u32[]{:S(2)}, u32[]{:S(2)}) collective-permute-start(f32[26,8,128]{2,1,0:T(8,128)S(1)} %constant_dynamic-update-slice_fusion.10), channel_id=1, source_target_pairs={{0,7},{1,0},{2,1},{3,2},{4,3},{5,4},{6,5},{7,6},{8,15},{9,8},{10,9... | collective-permute-start | bytes 319496 | tf_op jit(solution)/shard_map/ppermute | solution.py:173
  60.1 0.6 collective-permute-start.9
  60.7 2.3 %collective-permute-done.8.zrows = f32[26,8,128]{2,1,0:T(8,128)S(1)} collective-permute-done((f32[26,8,128]{2,1,0:T(8,128)S(1)}, f32[26,8,128]{2,1,0:T(8,128)S(1)}, u32[]{:S(2)}, u32[]{:S(2)}) %collective-permute-start.8) | collective-permute-done | bytes 106528 | tf_op jit(solution)/shard_map/ppermute | solution.py:173
  63.1 0.0 collective-permute-done.9.yrows
  63.1 1.9 %shard_map.29 = f32[4,32,256]{2,1,0:T(8,128)} custom-call(f32[6,48,256]{2,1,0:T(8,128)S(1)} %get-tuple-element.11.smooth, f32[6,48,256]{2,1,0:T(8,128)S(1)} %get-tuple-element.12.dens, f32[4,16,128]{2,1,0:T(8,128)S(1)} %get-tuple-element.13.own, f32[4,16,128]{2,1,0:T(8,128)S(1)} %collective-permute-done.4.flo, f32[4,16,128]{2,1,0:T(8,128)S(1)} %collective-permute-done.5.fhi, ...), custom_call_target="tpu_custom_call" | custom-call | tf_op jit(solution)/shard_map/pallas_call | solution.py:161
  (28 shorter events, 0.2 us)
Async XLA Ops:
  0.0 1.0 %copy-start = (f32[4,32,256]{2,1,0:T(8,128)S(1)}, f32[4,32,256]{2,1,0:T(8,128)}, u32[]{:S(2)}) copy-start(f32[4,32,256]{2,1,0:T(8,128)} %field.1) | copy-start | bytes 393220
  1.0 26.6 %collective-permute-start = (f32[5,32,256]{2,1,0:T(8,128)S(1)}, f32[5,32,256]{2,1,0:T(8,128)S(1)}, u32[]{:S(2)}, u32[]{:S(2)}) collective-permute-start(f32[5,32,256]{2,1,0:T(8,128)S(1)} %pad_maximum_fusion), channel_id=1, source_target_pairs={{0,8},{8,16},{16,24},{24,32},{32,40},{40,48},{48,56},{56,64},{64,7... | collective-permute-start | bytes 491528 | tf_op jit(solution)/shard_map/ppermute | solution.py:173
  5.4 19.4 %copy-start.1 = (f32[4,32,256]{2,1,0:T(8,128)S(1)}, f32[4,32,256]{2,1,0:T(8,128)}, u32[]{:S(2)}) copy-start(f32[4,32,256]{2,1,0:T(8,128)} %density.1) | copy-start | bytes 393220
  5.4 22.2 %collective-permute-start.1 = (f32[5,32,256]{2,1,0:T(8,128)S(1)}, f32[5,32,256]{2,1,0:T(8,128)S(1)}, u32[]{:S(2)}, u32[]{:S(2)}) collective-permute-start(f32[5,32,256]{2,1,0:T(8,128)S(1)} %pad_maximum_fusion.1), channel_id=1, source_target_pairs={{0,1016},{8,0},{16,8},{24,16},{32,24},{40,32},{48,40},{56,48},{64,... | collective-permute-start | bytes 491528 | tf_op jit(solution)/shard_map/ppermute | solution.py:173
  27.7 4.1 %collective-permute-start.2 = (f32[18,4,256]{2,1,0:T(4,128)S(1)}, f32[18,4,256]{2,1,0:T(4,128)S(1)}, u32[]{:S(2)}, u32[]{:S(2)}) collective-permute-start(f32[18,4,256]{2,1,0:T(4,128)S(1)} %pad_maximum_fusion.2), channel_id=1, source_target_pairs={{0,1},{1,2},{2,3},{3,4},{4,5},{5,6},{6,7},{7,0},{8,9},{9,10},{10,1... | collective-permute-start | bytes 221192 | tf_op jit(solution)/shard_map/ppermute | solution.py:173
  30.4 3.8 %collective-permute-start.3 = (f32[18,4,256]{2,1,0:T(4,128)S(1)}, f32[18,4,256]{2,1,0:T(4,128)S(1)}, u32[]{:S(2)}, u32[]{:S(2)}) collective-permute-start(f32[18,4,256]{2,1,0:T(4,128)S(1)} %pad_maximum_fusion.3), channel_id=1, source_target_pairs={{0,7},{1,0},{2,1},{3,2},{4,3},{5,4},{6,5},{7,6},{8,15},{9,8},{10,9... | collective-permute-start | bytes 221192 | tf_op jit(solution)/shard_map/ppermute | solution.py:173
  35.0 11.4 %collective-permute-start.4 = (f32[4,16,128]{2,1,0:T(8,128)S(1)}, f32[4,16,128]{2,1,0:T(8,128)S(1)}, u32[]{:S(2)}, u32[]{:S(2)}) collective-permute-start(f32[4,16,128]{2,1,0:T(8,128)S(1)} %get-tuple-element.13.own), channel_id=1, source_target_pairs={{0,24},{8,32},{16,40},{24,48},{32,56},{40,64},{48,72},{56,80},{64,... | collective-permute-start | bytes 98312 | tf_op jit(solution)/shard_map/ppermute | solution.py:173
  36.9 9.5 %collective-permute-start.5 = (f32[4,16,128]{2,1,0:T(8,128)S(1)}, f32[4,16,128]{2,1,0:T(8,128)S(1)}, u32[]{:S(2)}, u32[]{:S(2)}) collective-permute-start(f32[4,16,128]{2,1,0:T(8,128)S(1)} %get-tuple-element.14), channel_id=1, source_target_pairs={{0,1000},{8,1008},{16,1016},{24,0},{32,8},{40,16},{48,24},{56,32},... | collective-permute-start | bytes 98312 | tf_op jit(solution)/shard_map/ppermute | solution.py:173
  46.5 9.9 %collective-permute-start.6 = (f32[14,16,128]{2,1,0:T(8,128)S(1)}, f32[14,16,128]{2,1,0:T(8,128)S(1)}, u32[]{:S(2)}, u32[]{:S(2)}) collective-permute-start(f32[14,16,128]{2,1,0:T(8,128)S(1)} %constant_dynamic-update-slice_fusion), channel_id=1, source_target_pairs={{0,8},{8,16},{16,24},{24,32},{32,40},{40,48},{48,56},{56,64},{64,7... | collective-permute-start | bytes 344072 | tf_op jit(solution)/shard_map/ppermute | solution.py:173
  48.5 9.5 %collective-permute-start.7 = (f32[14,16,128]{2,1,0:T(8,128)S(1)}, f32[14,16,128]{2,1,0:T(8,128)S(1)}, u32[]{:S(2)}, u32[]{:S(2)}) collective-permute-start(f32[14,16,128]{2,1,0:T(8,128)S(1)} %constant_dynamic-update-slice_fusion.5), channel_id=1, source_target_pairs={{0,1016},{8,0},{16,8},{24,16},{32,24},{40,32},{48,40},{56,48},{64,... | collective-permute-start | bytes 344072 | tf_op jit(solution)/shard_map/ppermute | solution.py:173
  58.0 5.0 %collective-permute-start.8 = (f32[26,8,128]{2,1,0:T(8,128)S(1)}, f32[26,8,128]{2,1,0:T(8,128)S(1)}, u32[]{:S(2)}, u32[]{:S(2)}) collective-permute-start(f32[26,8,128]{2,1,0:T(8,128)S(1)} %constant_dynamic-update-slice_fusion.10), channel_id=1, source_target_pairs={{0,7},{1,0},{2,1},{3,2},{4,3},{5,4},{6,5},{7,6},{8,15},{9,8},{10,9... | collective-permute-start | bytes 319496 | tf_op jit(solution)/shard_map/ppermute | solution.py:173
  60.1 2.9 %collective-permute-start.9 = (f32[26,8,128]{2,1,0:T(8,128)S(1)}, f32[26,8,128]{2,1,0:T(8,128)S(1)}, u32[]{:S(2)}, u32[]{:S(2)}) collective-permute-start(f32[26,8,128]{2,1,0:T(8,128)S(1)} %constant_dynamic-update-slice_fusion.15), channel_id=1, source_target_pairs={{0,1},{1,2},{2,3},{3,4},{4,5},{5,6},{6,7},{7,0},{8,9},{9,10},{10,1... | collective-permute-start | bytes 319496 | tf_op jit(solution)/shard_map/ppermute | solution.py:173

commit v9 on v8

v9 whole, which is shorter than its diff:
```python
import jax
import jax.numpy as jnp
from jax import lax
from jax.experimental import pallas as pl
from jax.experimental.pallas import tpu as pltpu
from jax.sharding import PartitionSpec as P

mass = 0.02
damping = 0.8


def around(ref, i, rows):
    v, first, last = ref[i, rows], rows.start, rows.stop
    total = ref[i - 1, rows] + ref[i + 1, rows]
    total = total + (ref[i, first - 1 : last - 1] + ref[i, first + 1 : last + 1])
    return total + pltpu.roll(v, 1, 1) + pltpu.roll(v, v.shape[1] - 1, 1)


def jacobi(ref, i, rows, source, inv_step):
    v = ref[i, rows]
    square = v * v
    inner = (6.0 * inv_step + mass) + (mass / 3.0) * square
    top = inv_step * around(ref, i, rows) - source - v * inner
    return v + top / ((6.0 * inv_step + mass) / damping + (mass / damping) * square)


def operator(ref, i, rows, inv_step):
    v = ref[i, rows]
    return inv_step * around(ref, i, rows) - v * ((6.0 * inv_step + mass) + (mass / 3.0) * (v * v))


def exact_dot(values, weights):
    high = values.astype(jnp.bfloat16)
    rest = values - high.astype(jnp.float32)
    middle = rest.astype(jnp.bfloat16)
    low = (rest - middle.astype(jnp.float32)).astype(jnp.bfloat16)
    total = jnp.dot(low, weights, preferred_element_type=jnp.float32)
    total = total + jnp.dot(middle, weights, preferred_element_type=jnp.float32)
    return total + jnp.dot(high, weights, preferred_element_type=jnp.float32)


def fine_kernel(field, density, xlo, xhi, clo, chi, smooth, d, coarse, coarse2, up, down, f, s1, pair, rows):
    f[0:3, 16:48] = xlo[0:3]
    f[3:7, 16:48] = field[...]
    f[7:10, 16:48] = xhi[0:3]
    d[0:2, 8:40] = xlo[3:5]
    d[2:6, 8:40] = density[...]
    d[6:8, 8:40] = xhi[3:5]
    for side, at in ((clo, 4), (chi, 40)):
        f[0:3, at + 8 : at + 12] = side[0:3]
        f[3:7, at + 8 : at + 12] = side[10:14]
        f[7:10, at + 8 : at + 12] = side[5:8]
        d[0:2, at : at + 4] = side[3:5]
        d[2:6, at : at + 4] = side[14:18]
        d[6:8, at : at + 4] = side[8:10]
    for i in range(8):
        s1[i, 8:56] = jacobi(f, i + 1, slice(8, 56), d[i], 1.0)
    for i in range(6):
        smooth[i] = jacobi(s1, i + 1, slice(8, 56), d[i + 1], 1.0)
    for j in range(2):
        total = smooth[2 * j + 1, 8:40] + smooth[2 * j + 2, 8:40]
        pair[j, 0], pair[j, 1] = total[:, 0:128], total[:, 128:256]
        defect = [d[i + 2, 8:40] - operator(smooth, i + 1, slice(8, 40), 1.0) for i in (2 * j, 2 * j + 1)]
        total = defect[0] + defect[1]
        pair[j + 2, 0], pair[j + 2, 1] = total[:, 0:128], total[:, 128:256]
    for j in range(4):
        for k in range(2):
            total = pair[j, k, pl.ds(0, 16, stride=2)] + pair[j, k, pl.ds(1, 16, stride=2)]
            rows[16 * j : 16 * j + 16, 128 * k : 128 * k + 128] = total
    third = lax.broadcasted_iota(jnp.int32, (256, 128), 0)
    half = lax.broadcasted_iota(jnp.int32, (256, 128), 1)
    weights = jnp.where(third >> 1 == half, 0.125, 0.0).astype(jnp.bfloat16)
    coarse[...] = exact_dot(rows[...], weights).reshape(4, 16, 128)
    coarse2[...] = coarse[...]
    for face, layer in ((up, 3), (down, 2)):
        for j in range(4):
            at, lane = 8 + 16 * (j // 2), 128 * (j % 2)
            face[j] = smooth[layer, at : at + 16, lane : lane + 128]


def coarse_kernel(
    smooth, dens, own, flo, fhi, nlo, nhi, zrows, yrows,
    out, start, r, g, c0, c1, wide, corrected, post,
):
    for ref, at in ((start.at[:, 8:40], 0), (r, 1)):
        ref[0:1, 8:24] = nlo[at : at + 1]
        ref[1:3, 8:24] = flo[2 * at : 2 * at + 2]
        ref[13:15, 8:24] = fhi[2 * at : 2 * at + 2]
        ref[15:16, 8:24] = nhi[at : at + 1]
        for rows, mine, low, high, first in (
            (slice(8, 24), own, nlo, nhi, 2),
            (slice(0, 8), yrows.at[0:4], yrows.at[4:12], yrows.at[12:20], 0),
            (slice(24, 32), zrows.at[0:4], zrows.at[4:12], zrows.at[12:20], 0),
        ):
            at_own, at_two = first + 2 * at, first + 4 + 2 * at
            ref[3:5, rows] = high[at_two : at_two + 2]
            ref[5:7, rows] = low[at_own : at_own + 2]
            ref[7:9, rows] = mine[2 * at : 2 * at + 2]
            ref[9:11, rows] = high[at_own : at_own + 2]
            ref[11:13, rows] = low[at_two : at_two + 2]
        for rows, side in ((slice(4, 8), yrows), (slice(24, 28), zrows)):
            ref[1:3, rows] = side[20 + 2 * at : 22 + 2 * at, 0:4]
            ref[0:1, rows] = side[24 + at : 25 + at, 0:4]
            ref[13:15, rows] = side[20 + 2 * at : 22 + 2 * at, 4:8]
            ref[15:16, rows] = side[24 + at : 25 + at, 4:8]
    rows = slice(8, 40)
    for i in range(16):
        v = start[i, rows]
        c0[i, rows] = v - r[i] / ((1.5 + mass) / damping + (mass / damping) * (v * v))
    for i in range(1, 15):
        g[i] = operator(start, i, rows, 0.25) + r[i]
    now, later = c0, c1
    for sweep in range(1, 6):
        for i in range(sweep, 16 - sweep):
            later[i, rows] = jacobi(now, i, rows, g[i], 0.25)
        now, later = later, now
    change = (now[5:11, 8:40] - start[5:11, 8:40]).reshape(192, 128)
    half = lax.broadcasted_iota(jnp.int32, (128, 256), 0)
    third = lax.broadcasted_iota(jnp.int32, (128, 256), 1)
    beside = ((third >> 1) + 2 * (third & 1) - 1) & 127
    weights = jnp.where(third >> 1 == half, 0.75, jnp.where(beside == half, 0.25, 0.0)).astype(jnp.bfloat16)
    spread = exact_dot(change, weights).reshape(6, 32, 256)
    for i in range(6):
        v = spread[i]
        even = 0.75 * v + 0.25 * pltpu.roll(v, 1, 0)
        odd = 0.75 * v + 0.25 * pltpu.roll(v, 31, 0)
        for k in range(2):
            wide[i, k, pl.ds(0, 32, stride=2)] = even[:, 128 * k : 128 * k + 128]
            wide[i, k, pl.ds(1, 32, stride=2)] = odd[:, 128 * k : 128 * k + 128]
    for j in range(4):
        at, lane = 16 + 16 * (j // 2), 128 * (j % 2)
        corrected[0, at : at + 16, lane : lane + 128] = nlo[10 + j]
        corrected[7, at : at + 16, lane : lane + 128] = nhi[10 + j]
    for i in range(8):
        near = i // 2 + 1
        beside = near - 1 if i % 2 == 0 else near + 1
        for k in range(2):
            lanes = slice(128 * k, 128 * k + 128)
            if i in (0, 7):
                rows = slice(16, 48)
                before = corrected[i, rows, lanes]
            else:
                rows = slice(8, 56)
                before = smooth[i - 1, :, lanes]
            corrected[i, rows, lanes] = before + (0.75 * wide[near, k, rows] + 0.25 * wide[beside, k, rows])
    for i in range(6):
        rows = slice(16, 48) if i in (0, 5) else slice(8, 56)
        post[i, rows] = jacobi(corrected, i + 1, rows, dens[i + 1, rows.start - 8 : rows.stop - 8], 1.0)
    for i in range(4):
        out[i] = jacobi(post, i + 1, slice(16, 48), dens[i + 2, 8:40], 1.0)


def call(kernel, outs, scratch, *args):
    vmem = pl.BlockSpec(memory_space=pltpu.VMEM)
    shapes = [jax.ShapeDtypeStruct(shape, jnp.float32) for shape in outs]
    return pl.pallas_call(
        kernel,
        out_shape=shapes,
        in_specs=[vmem] * len(args),
        out_specs=[vmem] * len(outs),
        scratch_shapes=[pltpu.VMEM(shape, jnp.float32) for shape in scratch],
        compiler_params=pltpu.CompilerParams(vmem_limit_bytes=32 * 1024 * 1024),
    )(*args)


def send(values, axis, step):
    count = lax.axis_size(axis)
    return lax.ppermute(values, axis, [(i, (i + step) % count) for i in range(count)])


def rows_from_sides(near, far):
    last = [piece[:, 8:16] for piece in near]
    last += [jnp.concatenate([low[:, 12:16], high[:, 12:16]], 1) for low, high in far]
    first = [piece[:, 0:8] for piece in near]
    first += [jnp.concatenate([low[:, 0:4], high[:, 0:4]], 1) for low, high in far]
    return send(jnp.concatenate(last, 0), "gy", 1), send(jnp.concatenate(first, 0), "gy", -1)


def body(density, field):
    xlo = send(jnp.concatenate([field[1:4], density[2:4]], 0), "gx", 1)
    xhi = send(jnp.concatenate([field[0:3], density[0:2]], 0), "gx", -1)
    clo = send(jnp.concatenate([xlo[:, 28:32], xhi[:, 28:32], field[:, 28:32], density[:, 28:32]], 0), "gy", 1)
    chi = send(jnp.concatenate([xlo[:, 0:4], xhi[:, 0:4], field[:, 0:4], density[:, 0:4]], 0), "gy", -1)
    smooth, dens, own, own2, up, down = call(
        fine_kernel,
        [(6, 48, 256), (8, 48, 256), (4, 16, 128), (4, 16, 128), (4, 16, 128), (4, 16, 128)],
        [(10, 64, 256), (8, 64, 256), (4, 2, 32, 128), (64, 256)],
        field, density, xlo, xhi, clo, chi,
    )
    flo, fhi = send(own, "gx", 3), send(own2, "gx", -3)
    nlo = send(jnp.concatenate([flo[1:2], flo[3:4], own, fhi, up], 0), "gx", 1)
    nhi = send(jnp.concatenate([fhi[0:1], fhi[2:3], own, flo, down], 0), "gx", -1)
    yrows, zrows = rows_from_sides([own, nlo[2:10], nhi[2:10]], [(flo, fhi), (nlo[0:2], nhi[0:2])])
    (out,) = call(
        coarse_kernel,
        [(4, 32, 256)],
        [(16, 48, 128)] + [(16, 32, 128)] * 2 + [(16, 48, 128)] * 2 + [(6, 2, 64, 128), (8, 64, 256), (6, 64, 256)],
        smooth, dens, own, flo, fhi, nlo, nhi, zrows, yrows,
    )
    return out


def solution(mesh):
    placed = (P("gx", "gy", None), P("gx", "gy", None))
    return jax.shard_map(body, mesh=mesh, in_specs=placed, out_specs=P("gx", "gy", None), check_vma=False)
```

time: 65.8 us -> 65.7 us (level)
  no operation moved by 1% of the time
where the time goes in v9:
time: 65.7 us; the launch traced here: 64.9 us
  starting transfers between devices  49.1 us (75%)
  waiting for transfers between devices  11.6 us (18%)
  Pallas kernels  2.7 us (4%)
  local copies, waits for them, and re-layouts  1.09 us (2%)
    ppermute x10, starting transfers between devices, send(): lax.ppermute(values, axis, [(i, (i + step) % count) for i in range(count)])  49.1 us
    ppermute x10, waiting for transfers between devices, send(): lax.ppermute(values, axis, [(i, (i + step) % count) for i in range(count)])  11.6 us
    pallas_call x2, Pallas kernels, call(): pl.pallas_call(kernel, out_shape=shapes, in_specs=[vmem] * len(args), out...  2.7 us
  transfers between devices with their start and end apart: 10, of which 7 were waited for; matrix products, arithmetic and copies ran while one was open for 0% of the time, Pallas kernels for 0%

profile of v9, /device:TPU:1, one launch (start us, length us, event | category | flops | bytes accessed | tf_op | source)
XLA Modules:
  0.0 64.9 jit_solution(5719416751766073891)
XLA Ops:
  0.0 0.0 copy-start
  0.0 0.9 %fusion.5 = (f32[2,32,256]{2,1,0:T(8,128)S(1)}, f32[2,32,256]{2,1,0:T(8,128)S(1)}) fusion(f32[4,32,256]{2,1,0:T(8,128)} %density.1), kind=kLoop, calls=%fused_computation.29 | loop fusion | bytes 262144 | tf_op jit(solution)/shard_map/slice | solution.py:181
  0.9 0.0 copy-done
  1.0 4.4 %collective-permute-start = (f32[5,32,256]{2,1,0:T(8,128)S(1)}, f32[5,32,256]{2,1,0:T(8,128)S(1)}, u32[]{:S(2)}, u32[]{:S(2)}) collective-permute-start(f32[5,32,256]{2,1,0:T(8,128)S(1)} %pad_maximum_fusion), channel_id=1, source_target_pairs={{0,8},{8,16},{16,24},{24,32},{32,40},{40,48},{48,56},{56,64},{64,7... | collective-permute-start | bytes 491528 | tf_op jit(solution)/shard_map/ppermute | solution.py:168
  5.4 0.0 copy-start.1
  5.4 19.4 %collective-permute-start.1 = (f32[5,32,256]{2,1,0:T(8,128)S(1)}, f32[5,32,256]{2,1,0:T(8,128)S(1)}, u32[]{:S(2)}, u32[]{:S(2)}) collective-permute-start(f32[5,32,256]{2,1,0:T(8,128)S(1)} %pad_maximum_fusion.1), channel_id=1, source_target_pairs={{0,1016},{8,0},{16,8},{24,16},{32,24},{40,32},{48,40},{56,48},{64,... | collective-permute-start | bytes 491528 | tf_op jit(solution)/shard_map/ppermute | solution.py:168
  24.8 0.0 copy-done.1
  24.8 2.8 %collective-permute-done.1.xhi = f32[5,32,256]{2,1,0:T(8,128)S(1)} collective-permute-done((f32[5,32,256]{2,1,0:T(8,128)S(1)}, f32[5,32,256]{2,1,0:T(8,128)S(1)}, u32[]{:S(2)}, u32[]{:S(2)}) %collective-permute-start.1) | collective-permute-done | bytes 163872 | tf_op jit(solution)/shard_map/ppermute | solution.py:168
  27.6 0.0 collective-permute-done.xlo
  27.7 2.7 %collective-permute-start.2 = (f32[18,4,256]{2,1,0:T(4,128)S(1)}, f32[18,4,256]{2,1,0:T(4,128)S(1)}, u32[]{:S(2)}, u32[]{:S(2)}) collective-permute-start(f32[18,4,256]{2,1,0:T(4,128)S(1)} %pad_maximum_fusion.2), channel_id=1, source_target_pairs={{0,1},{1,2},{2,3},{3,4},{4,5},{5,6},{6,7},{7,0},{8,9},{9,10},{10,1... | collective-permute-start | bytes 221192 | tf_op jit(solution)/shard_map/ppermute | solution.py:168
  30.4 0.0 collective-permute-start.3
  30.4 1.4 %collective-permute-done.2.clo = f32[18,4,256]{2,1,0:T(4,128)S(1)} collective-permute-done((f32[18,4,256]{2,1,0:T(4,128)S(1)}, f32[18,4,256]{2,1,0:T(4,128)S(1)}, u32[]{:S(2)}, u32[]{:S(2)}) %collective-permute-start.2) | collective-permute-done | bytes 73760 | tf_op jit(solution)/shard_map/ppermute | solution.py:168
  31.8 2.4 %collective-permute-done.3.chi = f32[18,4,256]{2,1,0:T(4,128)S(1)} collective-permute-done((f32[18,4,256]{2,1,0:T(4,128)S(1)}, f32[18,4,256]{2,1,0:T(4,128)S(1)}, u32[]{:S(2)}, u32[]{:S(2)}) %collective-permute-start.3) | collective-permute-done | bytes 73760 | tf_op jit(solution)/shard_map/ppermute | solution.py:168
  34.2 0.8 %shard_map.28 = (f32[6,48,256]{2,1,0:T(8,128)S(1)}, f32[8,48,256]{2,1,0:T(8,128)S(1)}, f32[4,16,128]{2,1,0:T(8,128)S(1)}, f32[4,16,128]{2,1,0:T(8,128)S(1)}, f32...) custom-call(f32[4,32,256]{2,1,0:T(8,128)S(1)} %copy-done, f32[4,32,256]{2,1,0:T(8,128)S(1)} %copy-done.1, ...), custom_call_target="tpu_custom_call" | custom-call | tf_op jit(solution)/shard_map/pallas_call | solution.py:156
  35.0 1.9 %collective-permute-start.4 = (f32[4,16,128]{2,1,0:T(8,128)S(1)}, f32[4,16,128]{2,1,0:T(8,128)S(1)}, u32[]{:S(2)}, u32[]{:S(2)}) collective-permute-start(f32[4,16,128]{2,1,0:T(8,128)S(1)} %get-tuple-element.13.own), channel_id=1, source_target_pairs={{0,24},{8,32},{16,40},{24,48},{32,56},{40,64},{48,72},{56,80},{64,... | collective-permute-start | bytes 98312 | tf_op jit(solution)/shard_map/ppermute | solution.py:168
  36.9 8.5 %collective-permute-start.5 = (f32[4,16,128]{2,1,0:T(8,128)S(1)}, f32[4,16,128]{2,1,0:T(8,128)S(1)}, u32[]{:S(2)}, u32[]{:S(2)}) collective-permute-start(f32[4,16,128]{2,1,0:T(8,128)S(1)} %get-tuple-element.14), channel_id=1, source_target_pairs={{0,1000},{8,1008},{16,1016},{24,0},{32,8},{40,16},{48,24},{56,32},... | collective-permute-start | bytes 98312 | tf_op jit(solution)/shard_map/ppermute | solution.py:168
  45.4 1.0 %collective-permute-done.5.fhi = f32[4,16,128]{2,1,0:T(8,128)S(1)} collective-permute-done((f32[4,16,128]{2,1,0:T(8,128)S(1)}, f32[4,16,128]{2,1,0:T(8,128)S(1)}, u32[]{:S(2)}, u32[]{:S(2)}) %collective-permute-start.5) | collective-permute-done | bytes 32800 | tf_op jit(solution)/shard_map/ppermute | solution.py:168
  46.4 0.0 collective-permute-done.4.flo
  46.5 1.9 %collective-permute-start.6 = (f32[14,16,128]{2,1,0:T(8,128)S(1)}, f32[14,16,128]{2,1,0:T(8,128)S(1)}, u32[]{:S(2)}, u32[]{:S(2)}) collective-permute-start(f32[14,16,128]{2,1,0:T(8,128)S(1)} %constant_dynamic-update-slice_fusion), channel_id=1, source_target_pairs={{0,8},{8,16},{16,24},{24,32},{32,40},{40,48},{48,56},{56,64},{64,7... | collective-permute-start | bytes 344072 | tf_op jit(solution)/shard_map/ppermute | solution.py:168
  48.4 7.7 %collective-permute-start.7 = (f32[14,16,128]{2,1,0:T(8,128)S(1)}, f32[14,16,128]{2,1,0:T(8,128)S(1)}, u32[]{:S(2)}, u32[]{:S(2)}) collective-permute-start(f32[14,16,128]{2,1,0:T(8,128)S(1)} %constant_dynamic-update-slice_fusion.5), channel_id=1, source_target_pairs={{0,1016},{8,0},{16,8},{24,16},{32,24},{40,32},{48,40},{56,48},{64,... | collective-permute-start | bytes 344072 | tf_op jit(solution)/shard_map/ppermute | solution.py:168
  56.2 0.2 collective-permute-done.6.nlo
  56.4 1.6 %collective-permute-done.7.nhi = f32[14,16,128]{2,1,0:T(8,128)S(1)} collective-permute-done((f32[14,16,128]{2,1,0:T(8,128)S(1)}, f32[14,16,128]{2,1,0:T(8,128)S(1)}, u32[]{:S(2)}, u32[]{:S(2)}) %collective-permute-start.7) | collective-permute-done | bytes 114720 | tf_op jit(solution)/shard_map/ppermute | solution.py:168
  58.0 2.1 %collective-permute-start.8 = (f32[26,8,128]{2,1,0:T(8,128)S(1)}, f32[26,8,128]{2,1,0:T(8,128)S(1)}, u32[]{:S(2)}, u32[]{:S(2)}) collective-permute-start(f32[26,8,128]{2,1,0:T(8,128)S(1)} %constant_dynamic-update-slice_fusion.10), channel_id=1, source_target_pairs={{0,7},{1,0},{2,1},{3,2},{4,3},{5,4},{6,5},{7,6},{8,15},{9,8},{10,9... | collective-permute-start | bytes 319496 | tf_op jit(solution)/shard_map/ppermute | solution.py:168
  60.1 0.6 collective-permute-start.9
  60.7 2.3 %collective-permute-done.8.zrows = f32[26,8,128]{2,1,0:T(8,128)S(1)} collective-permute-done((f32[26,8,128]{2,1,0:T(8,128)S(1)}, f32[26,8,128]{2,1,0:T(8,128)S(1)}, u32[]{:S(2)}, u32[]{:S(2)}) %collective-permute-start.8) | collective-permute-done | bytes 106528 | tf_op jit(solution)/shard_map/ppermute | solution.py:168
  63.0 0.0 collective-permute-done.9.yrows
  63.0 1.9 %shard_map.29 = f32[4,32,256]{2,1,0:T(8,128)} custom-call(f32[6,48,256]{2,1,0:T(8,128)S(1)} %get-tuple-element.11.smooth, f32[8,48,256]{2,1,0:T(8,128)S(1)} %get-tuple-element.12.dens, f32[4,16,128]{2,1,0:T(8,128)S(1)} %get-tuple-element.13.own, f32[4,16,128]{2,1,0:T(8,128)S(1)} %collective-permute-done.4.flo, f32[4,16,128]{2,1,0:T(8,128)S(1)} %collective-permute-done.5.fhi, ...), custom_call_target="tpu_custom_call" | custom-call | tf_op jit(solution)/shard_map/pallas_call | solution.py:156
  (28 shorter events, 0.2 us)
Async XLA Ops:
  0.0 1.0 %copy-start = (f32[4,32,256]{2,1,0:T(8,128)S(1)}, f32[4,32,256]{2,1,0:T(8,128)}, u32[]{:S(2)}) copy-start(f32[4,32,256]{2,1,0:T(8,128)} %field.1) | copy-start | bytes 393220
  1.0 26.6 %collective-permute-start = (f32[5,32,256]{2,1,0:T(8,128)S(1)}, f32[5,32,256]{2,1,0:T(8,128)S(1)}, u32[]{:S(2)}, u32[]{:S(2)}) collective-permute-start(f32[5,32,256]{2,1,0:T(8,128)S(1)} %pad_maximum_fusion), channel_id=1, source_target_pairs={{0,8},{8,16},{16,24},{24,32},{32,40},{40,48},{48,56},{56,64},{64,7... | collective-permute-start | bytes 491528 | tf_op jit(solution)/shard_map/ppermute | solution.py:168
  5.4 19.4 %copy-start.1 = (f32[4,32,256]{2,1,0:T(8,128)S(1)}, f32[4,32,256]{2,1,0:T(8,128)}, u32[]{:S(2)}) copy-start(f32[4,32,256]{2,1,0:T(8,128)} %density.1) | copy-start | bytes 393220
  5.4 22.2 %collective-permute-start.1 = (f32[5,32,256]{2,1,0:T(8,128)S(1)}, f32[5,32,256]{2,1,0:T(8,128)S(1)}, u32[]{:S(2)}, u32[]{:S(2)}) collective-permute-start(f32[5,32,256]{2,1,0:T(8,128)S(1)} %pad_maximum_fusion.1), channel_id=1, source_target_pairs={{0,1016},{8,0},{16,8},{24,16},{32,24},{40,32},{48,40},{56,48},{64,... | collective-permute-start | bytes 491528 | tf_op jit(solution)/shard_map/ppermute | solution.py:168
  27.7 4.1 %collective-permute-start.2 = (f32[18,4,256]{2,1,0:T(4,128)S(1)}, f32[18,4,256]{2,1,0:T(4,128)S(1)}, u32[]{:S(2)}, u32[]{:S(2)}) collective-permute-start(f32[18,4,256]{2,1,0:T(4,128)S(1)} %pad_maximum_fusion.2), channel_id=1, source_target_pairs={{0,1},{1,2},{2,3},{3,4},{4,5},{5,6},{6,7},{7,0},{8,9},{9,10},{10,1... | collective-permute-start | bytes 221192 | tf_op jit(solution)/shard_map/ppermute | solution.py:168
  30.4 3.8 %collective-permute-start.3 = (f32[18,4,256]{2,1,0:T(4,128)S(1)}, f32[18,4,256]{2,1,0:T(4,128)S(1)}, u32[]{:S(2)}, u32[]{:S(2)}) collective-permute-start(f32[18,4,256]{2,1,0:T(4,128)S(1)} %pad_maximum_fusion.3), channel_id=1, source_target_pairs={{0,7},{1,0},{2,1},{3,2},{4,3},{5,4},{6,5},{7,6},{8,15},{9,8},{10,9... | collective-permute-start | bytes 221192 | tf_op jit(solution)/shard_map/ppermute | solution.py:168
  35.0 11.4 %collective-permute-start.4 = (f32[4,16,128]{2,1,0:T(8,128)S(1)}, f32[4,16,128]{2,1,0:T(8,128)S(1)}, u32[]{:S(2)}, u32[]{:S(2)}) collective-permute-start(f32[4,16,128]{2,1,0:T(8,128)S(1)} %get-tuple-element.13.own), channel_id=1, source_target_pairs={{0,24},{8,32},{16,40},{24,48},{32,56},{40,64},{48,72},{56,80},{64,... | collective-permute-start | bytes 98312 | tf_op jit(solution)/shard_map/ppermute | solution.py:168
  36.9 9.5 %collective-permute-start.5 = (f32[4,16,128]{2,1,0:T(8,128)S(1)}, f32[4,16,128]{2,1,0:T(8,128)S(1)}, u32[]{:S(2)}, u32[]{:S(2)}) collective-permute-start(f32[4,16,128]{2,1,0:T(8,128)S(1)} %get-tuple-element.14), channel_id=1, source_target_pairs={{0,1000},{8,1008},{16,1016},{24,0},{32,8},{40,16},{48,24},{56,32},... | collective-permute-start | bytes 98312 | tf_op jit(solution)/shard_map/ppermute | solution.py:168
  46.5 9.9 %collective-permute-start.6 = (f32[14,16,128]{2,1,0:T(8,128)S(1)}, f32[14,16,128]{2,1,0:T(8,128)S(1)}, u32[]{:S(2)}, u32[]{:S(2)}) collective-permute-start(f32[14,16,128]{2,1,0:T(8,128)S(1)} %constant_dynamic-update-slice_fusion), channel_id=1, source_target_pairs={{0,8},{8,16},{16,24},{24,32},{32,40},{40,48},{48,56},{56,64},{64,7... | collective-permute-start | bytes 344072 | tf_op jit(solution)/shard_map/ppermute | solution.py:168
  48.4 9.5 %collective-permute-start.7 = (f32[14,16,128]{2,1,0:T(8,128)S(1)}, f32[14,16,128]{2,1,0:T(8,128)S(1)}, u32[]{:S(2)}, u32[]{:S(2)}) collective-permute-start(f32[14,16,128]{2,1,0:T(8,128)S(1)} %constant_dynamic-update-slice_fusion.5), channel_id=1, source_target_pairs={{0,1016},{8,0},{16,8},{24,16},{32,24},{40,32},{48,40},{56,48},{64,... | collective-permute-start | bytes 344072 | tf_op jit(solution)/shard_map/ppermute | solution.py:168
  58.0 5.0 %collective-permute-start.8 = (f32[26,8,128]{2,1,0:T(8,128)S(1)}, f32[26,8,128]{2,1,0:T(8,128)S(1)}, u32[]{:S(2)}, u32[]{:S(2)}) collective-permute-start(f32[26,8,128]{2,1,0:T(8,128)S(1)} %constant_dynamic-update-slice_fusion.10), channel_id=1, source_target_pairs={{0,7},{1,0},{2,1},{3,2},{4,3},{5,4},{6,5},{7,6},{8,15},{9,8},{10,9... | collective-permute-start | bytes 319496 | tf_op jit(solution)/shard_map/ppermute | solution.py:168
  60.1 2.9 %collective-permute-start.9 = (f32[26,8,128]{2,1,0:T(8,128)S(1)}, f32[26,8,128]{2,1,0:T(8,128)S(1)}, u32[]{:S(2)}, u32[]{:S(2)}) collective-permute-start(f32[26,8,128]{2,1,0:T(8,128)S(1)} %constant_dynamic-update-slice_fusion.15), channel_id=1, source_target_pairs={{0,1},{1,2},{2,3},{3,4},{4,5},{5,6},{6,7},{7,0},{8,9},{9,10},{10,1... | collective-permute-start | bytes 319496 | tf_op jit(solution)/shard_map/ppermute | solution.py:168

commit v10 on v8

--- a/solution.py
+++ b/solution.py
@@ -47,7 +47,7 @@
     return total + jnp.dot(high, weights, preferred_element_type=jnp.float32)
 
 
-def fine_kernel(field, density, xlo, xhi, clo, chi, smooth, dens, coarse, coarse2, up, down, f, d, s1, pair, rows):
+def fine_kernel(field, density, xlo, xhi, chi, clo, smooth, dens, coarse, coarse2, up, down, f, d, s1, pair, rows):
     f[0:3, 8:40] = xlo[0:3]
     f[3:7, 8:40] = field[...]
     f[7:10, 8:40] = xhi[0:3]
@@ -190,7 +190,7 @@
         fine_kernel,
         [(6, 48, 256), (6, 48, 256), (4, 16, 128), (4, 16, 128), (4, 16, 128), (4, 16, 128)],
         [(10, 48, 256), (8, 48, 256), (8, 48, 256), (4, 2, 48, 128), (64, 256)],
-        field, density, xlo, xhi, clo, chi,
+        field, density, xlo, xhi, chi, clo,
     )
     flo, fhi = send(own, "gx", 3), send(own2, "gx", -3)
     nlo = send(jnp.concatenate([flo[1:2], flo[3:4], own, fhi, up], 0), "gx", 1)

time: 65.8 us -> 65.4 us (level)
  starting transfers between devices: 49.1 us -> 51.7 us
  waiting for transfers between devices: 11.6 us -> 9.24 us
    ppermute x10, starting transfers between devices: 49.1 us -> 51.7 us  [send(): lax.ppermute(values, axis, [(i, (i + step) % count) for i in range(count)])]
    ppermute x10, waiting for transfers between devices: 11.6 us -> 9.24 us  [send(): lax.ppermute(values, axis, [(i, (i + step) % count) for i in range(count)])]
where the time goes in v10:
time: 65.4 us; the launch traced here: 65.1 us
  starting transfers between devices  51.7 us (79%)
  waiting for transfers between devices  9.24 us (14%)
  Pallas kernels  2.74 us (4%)
  local copies, waits for them, and re-layouts  1.09 us (2%)
    ppermute x10, starting transfers between devices, send(): lax.ppermute(values, axis, [(i, (i + step) % count) for i in range(count)])  51.7 us
    ppermute x10, waiting for transfers between devices, send(): lax.ppermute(values, axis, [(i, (i + step) % count) for i in range(count)])  9.24 us
    pallas_call x2, Pallas kernels, call(): pl.pallas_call(kernel, out_shape=shapes, in_specs=[vmem] * len(args), out...  2.74 us
  transfers between devices with their start and end apart: 10, of which 7 were waited for; matrix products, arithmetic and copies ran while one was open for 0% of the time, Pallas kernels for 0%

profile of v10, /device:TPU:1, one launch (start us, length us, event | category | flops | bytes accessed | tf_op | source)
XLA Modules:
  0.0 65.1 jit_solution(8970404434262224748)
XLA Ops:
  0.0 0.0 copy-start
  0.0 0.9 %fusion.5 = (f32[2,32,256]{2,1,0:T(8,128)S(1)}, f32[2,32,256]{2,1,0:T(8,128)S(1)}) fusion(f32[4,32,256]{2,1,0:T(8,128)} %density.1), kind=kLoop, calls=%fused_computation.29 | loop fusion | bytes 262144 | tf_op jit(solution)/shard_map/slice | solution.py:186
  0.9 0.0 copy-done
  1.0 4.4 %collective-permute-start = (f32[5,32,256]{2,1,0:T(8,128)S(1)}, f32[5,32,256]{2,1,0:T(8,128)S(1)}, u32[]{:S(2)}, u32[]{:S(2)}) collective-permute-start(f32[5,32,256]{2,1,0:T(8,128)S(1)} %pad_maximum_fusion), channel_id=1, source_target_pairs={{0,8},{8,16},{16,24},{24,32},{32,40},{40,48},{48,56},{56,64},{64,7... | collective-permute-start | bytes 491528 | tf_op jit(solution)/shard_map/ppermute | solution.py:173
  5.4 0.0 copy-start.1
  5.4 19.4 %collective-permute-start.1 = (f32[5,32,256]{2,1,0:T(8,128)S(1)}, f32[5,32,256]{2,1,0:T(8,128)S(1)}, u32[]{:S(2)}, u32[]{:S(2)}) collective-permute-start(f32[5,32,256]{2,1,0:T(8,128)S(1)} %pad_maximum_fusion.1), channel_id=1, source_target_pairs={{0,1016},{8,0},{16,8},{24,16},{32,24},{40,32},{48,40},{56,48},{64,... | collective-permute-start | bytes 491528 | tf_op jit(solution)/shard_map/ppermute | solution.py:173
  24.8 0.0 copy-done.1
  24.8 2.8 %collective-permute-done.1.xhi = f32[5,32,256]{2,1,0:T(8,128)S(1)} collective-permute-done((f32[5,32,256]{2,1,0:T(8,128)S(1)}, f32[5,32,256]{2,1,0:T(8,128)S(1)}, u32[]{:S(2)}, u32[]{:S(2)}) %collective-permute-start.1) | collective-permute-done | bytes 163872 | tf_op jit(solution)/shard_map/ppermute | solution.py:173
  27.6 0.0 collective-permute-done.xlo
  27.7 1.6 %collective-permute-start.2 = (f32[18,4,256]{2,1,0:T(4,128)S(1)}, f32[18,4,256]{2,1,0:T(4,128)S(1)}, u32[]{:S(2)}, u32[]{:S(2)}) collective-permute-start(f32[18,4,256]{2,1,0:T(4,128)S(1)} %pad_maximum_fusion.2), channel_id=1, source_target_pairs={{0,7},{1,0},{2,1},{3,2},{4,3},{5,4},{6,5},{7,6},{8,15},{9,8},{10,9... | collective-permute-start | bytes 221192 | tf_op jit(solution)/shard_map/ppermute | solution.py:173
  29.3 1.1 %collective-permute-start.3 = (f32[18,4,256]{2,1,0:T(4,128)S(1)}, f32[18,4,256]{2,1,0:T(4,128)S(1)}, u32[]{:S(2)}, u32[]{:S(2)}) collective-permute-start(f32[18,4,256]{2,1,0:T(4,128)S(1)} %pad_maximum_fusion.3), channel_id=1, source_target_pairs={{0,1},{1,2},{2,3},{3,4},{4,5},{5,6},{6,7},{7,0},{8,9},{9,10},{10,1... | collective-permute-start | bytes 221192 | tf_op jit(solution)/shard_map/ppermute | solution.py:173
  30.4 2.0 %collective-permute-done.2.chi = f32[18,4,256]{2,1,0:T(4,128)S(1)} collective-permute-done((f32[18,4,256]{2,1,0:T(4,128)S(1)}, f32[18,4,256]{2,1,0:T(4,128)S(1)}, u32[]{:S(2)}, u32[]{:S(2)}) %collective-permute-start.2) | collective-permute-done | bytes 73760 | tf_op jit(solution)/shard_map/ppermute | solution.py:173
  32.4 0.0 collective-permute-done.3.clo
  32.4 0.8 %shard_map.28 = (f32[6,48,256]{2,1,0:T(8,128)S(1)}, f32[6,48,256]{2,1,0:T(8,128)S(1)}, f32[4,16,128]{2,1,0:T(8,128)S(1)}, f32[4,16,128]{2,1,0:T(8,128)S(1)}, f32...) custom-call(f32[4,32,256]{2,1,0:T(8,128)S(1)} %copy-done, f32[4,32,256]{2,1,0:T(8,128)S(1)} %copy-done.1, ...), custom_call_target="tpu_custom_call" | custom-call | tf_op jit(solution)/shard_map/pallas_call | solution.py:161
  33.2 1.9 %collective-permute-start.4 = (f32[4,16,128]{2,1,0:T(8,128)S(1)}, f32[4,16,128]{2,1,0:T(8,128)S(1)}, u32[]{:S(2)}, u32[]{:S(2)}) collective-permute-start(f32[4,16,128]{2,1,0:T(8,128)S(1)} %get-tuple-element.13.own), channel_id=1, source_target_pairs={{0,24},{8,32},{16,40},{24,48},{32,56},{40,64},{48,72},{56,80},{64,... | collective-permute-start | bytes 98312 | tf_op jit(solution)/shard_map/ppermute | solution.py:173
  35.2 8.5 %collective-permute-start.5 = (f32[4,16,128]{2,1,0:T(8,128)S(1)}, f32[4,16,128]{2,1,0:T(8,128)S(1)}, u32[]{:S(2)}, u32[]{:S(2)}) collective-permute-start(f32[4,16,128]{2,1,0:T(8,128)S(1)} %get-tuple-element.14), channel_id=1, source_target_pairs={{0,1000},{8,1008},{16,1016},{24,0},{32,8},{40,16},{48,24},{56,32},... | collective-permute-start | bytes 98312 | tf_op jit(solution)/shard_map/ppermute | solution.py:173
  43.7 1.0 %collective-permute-done.5.fhi = f32[4,16,128]{2,1,0:T(8,128)S(1)} collective-permute-done((f32[4,16,128]{2,1,0:T(8,128)S(1)}, f32[4,16,128]{2,1,0:T(8,128)S(1)}, u32[]{:S(2)}, u32[]{:S(2)}) %collective-permute-start.5) | collective-permute-done | bytes 32800 | tf_op jit(solution)/shard_map/ppermute | solution.py:173
  44.7 0.0 collective-permute-done.4.flo
  44.7 1.9 %collective-permute-start.6 = (f32[14,16,128]{2,1,0:T(8,128)S(1)}, f32[14,16,128]{2,1,0:T(8,128)S(1)}, u32[]{:S(2)}, u32[]{:S(2)}) collective-permute-start(f32[14,16,128]{2,1,0:T(8,128)S(1)} %constant_dynamic-update-slice_fusion), channel_id=1, source_target_pairs={{0,8},{8,16},{16,24},{24,32},{32,40},{40,48},{48,56},{56,64},{64,7... | collective-permute-start | bytes 344072 | tf_op jit(solution)/shard_map/ppermute | solution.py:173
  46.7 7.7 %collective-permute-start.7 = (f32[14,16,128]{2,1,0:T(8,128)S(1)}, f32[14,16,128]{2,1,0:T(8,128)S(1)}, u32[]{:S(2)}, u32[]{:S(2)}) collective-permute-start(f32[14,16,128]{2,1,0:T(8,128)S(1)} %constant_dynamic-update-slice_fusion.5), channel_id=1, source_target_pairs={{0,1016},{8,0},{16,8},{24,16},{32,24},{40,32},{48,40},{56,48},{64,... | collective-permute-start | bytes 344072 | tf_op jit(solution)/shard_map/ppermute | solution.py:173
  54.4 0.2 collective-permute-done.6.nlo
  54.6 1.6 %collective-permute-done.7.nhi = f32[14,16,128]{2,1,0:T(8,128)S(1)} collective-permute-done((f32[14,16,128]{2,1,0:T(8,128)S(1)}, f32[14,16,128]{2,1,0:T(8,128)S(1)}, u32[]{:S(2)}, u32[]{:S(2)}) %collective-permute-start.7) | collective-permute-done | bytes 114720 | tf_op jit(solution)/shard_map/ppermute | solution.py:173
  56.2 5.2 %collective-permute-start.8 = (f32[26,8,128]{2,1,0:T(8,128)S(1)}, f32[26,8,128]{2,1,0:T(8,128)S(1)}, u32[]{:S(2)}, u32[]{:S(2)}) collective-permute-start(f32[26,8,128]{2,1,0:T(8,128)S(1)} %constant_dynamic-update-slice_fusion.10), channel_id=1, source_target_pairs={{0,7},{1,0},{2,1},{3,2},{4,3},{5,4},{6,5},{7,6},{8,15},{9,8},{10,9... | collective-permute-start | bytes 319496 | tf_op jit(solution)/shard_map/ppermute | solution.py:173
  61.5 0.0 collective-permute-start.9
  61.5 0.9 %collective-permute-done.8.zrows = f32[26,8,128]{2,1,0:T(8,128)S(1)} collective-permute-done((f32[26,8,128]{2,1,0:T(8,128)S(1)}, f32[26,8,128]{2,1,0:T(8,128)S(1)}, u32[]{:S(2)}, u32[]{:S(2)}) %collective-permute-start.8) | collective-permute-done | bytes 106528 | tf_op jit(solution)/shard_map/ppermute | solution.py:173
  62.4 0.8 %collective-permute-done.9.yrows = f32[26,8,128]{2,1,0:T(8,128)S(1)} collective-permute-done((f32[26,8,128]{2,1,0:T(8,128)S(1)}, f32[26,8,128]{2,1,0:T(8,128)S(1)}, u32[]{:S(2)}, u32[]{:S(2)}) %collective-permute-start.9) | collective-permute-done | bytes 106528 | tf_op jit(solution)/shard_map/ppermute | solution.py:173
  63.2 1.9 %shard_map.29 = f32[4,32,256]{2,1,0:T(8,128)} custom-call(f32[6,48,256]{2,1,0:T(8,128)S(1)} %get-tuple-element.11.smooth, f32[6,48,256]{2,1,0:T(8,128)S(1)} %get-tuple-element.12.dens, f32[4,16,128]{2,1,0:T(8,128)S(1)} %get-tuple-element.13.own, f32[4,16,128]{2,1,0:T(8,128)S(1)} %collective-permute-done.4.flo, f32[4,16,128]{2,1,0:T(8,128)S(1)} %collective-permute-done.5.fhi, ...), custom_call_target="tpu_custom_call" | custom-call | tf_op jit(solution)/shard_map/pallas_call | solution.py:161
  (28 shorter events, 0.2 us)
Async XLA Ops:
  0.0 1.0 %copy-start = (f32[4,32,256]{2,1,0:T(8,128)S(1)}, f32[4,32,256]{2,1,0:T(8,128)}, u32[]{:S(2)}) copy-start(f32[4,32,256]{2,1,0:T(8,128)} %field.1) | copy-start | bytes 393220
  1.0 26.6 %collective-permute-start = (f32[5,32,256]{2,1,0:T(8,128)S(1)}, f32[5,32,256]{2,1,0:T(8,128)S(1)}, u32[]{:S(2)}, u32[]{:S(2)}) collective-permute-start(f32[5,32,256]{2,1,0:T(8,128)S(1)} %pad_maximum_fusion), channel_id=1, source_target_pairs={{0,8},{8,16},{16,24},{24,32},{32,40},{40,48},{48,56},{56,64},{64,7... | collective-permute-start | bytes 491528 | tf_op jit(solution)/shard_map/ppermute | solution.py:173
  5.4 19.4 %copy-start.1 = (f32[4,32,256]{2,1,0:T(8,128)S(1)}, f32[4,32,256]{2,1,0:T(8,128)}, u32[]{:S(2)}) copy-start(f32[4,32,256]{2,1,0:T(8,128)} %density.1) | copy-start | bytes 393220
  5.4 22.2 %collective-permute-start.1 = (f32[5,32,256]{2,1,0:T(8,128)S(1)}, f32[5,32,256]{2,1,0:T(8,128)S(1)}, u32[]{:S(2)}, u32[]{:S(2)}) collective-permute-start(f32[5,32,256]{2,1,0:T(8,128)S(1)} %pad_maximum_fusion.1), channel_id=1, source_target_pairs={{0,1016},{8,0},{16,8},{24,16},{32,24},{40,32},{48,40},{56,48},{64,... | collective-permute-start | bytes 491528 | tf_op jit(solution)/shard_map/ppermute | solution.py:173
  27.7 4.7 %collective-permute-start.2 = (f32[18,4,256]{2,1,0:T(4,128)S(1)}, f32[18,4,256]{2,1,0:T(4,128)S(1)}, u32[]{:S(2)}, u32[]{:S(2)}) collective-permute-start(f32[18,4,256]{2,1,0:T(4,128)S(1)} %pad_maximum_fusion.2), channel_id=1, source_target_pairs={{0,7},{1,0},{2,1},{3,2},{4,3},{5,4},{6,5},{7,6},{8,15},{9,8},{10,9... | collective-permute-start | bytes 221192 | tf_op jit(solution)/shard_map/ppermute | solution.py:173
  29.3 3.1 %collective-permute-start.3 = (f32[18,4,256]{2,1,0:T(4,128)S(1)}, f32[18,4,256]{2,1,0:T(4,128)S(1)}, u32[]{:S(2)}, u32[]{:S(2)}) collective-permute-start(f32[18,4,256]{2,1,0:T(4,128)S(1)} %pad_maximum_fusion.3), channel_id=1, source_target_pairs={{0,1},{1,2},{2,3},{3,4},{4,5},{5,6},{6,7},{7,0},{8,9},{9,10},{10,1... | collective-permute-start | bytes 221192 | tf_op jit(solution)/shard_map/ppermute | solution.py:173
  33.2 11.4 %collective-permute-start.4 = (f32[4,16,128]{2,1,0:T(8,128)S(1)}, f32[4,16,128]{2,1,0:T(8,128)S(1)}, u32[]{:S(2)}, u32[]{:S(2)}) collective-permute-start(f32[4,16,128]{2,1,0:T(8,128)S(1)} %get-tuple-element.13.own), channel_id=1, source_target_pairs={{0,24},{8,32},{16,40},{24,48},{32,56},{40,64},{48,72},{56,80},{64,... | collective-permute-start | bytes 98312 | tf_op jit(solution)/shard_map/ppermute | solution.py:173
  35.2 9.5 %collective-permute-start.5 = (f32[4,16,128]{2,1,0:T(8,128)S(1)}, f32[4,16,128]{2,1,0:T(8,128)S(1)}, u32[]{:S(2)}, u32[]{:S(2)}) collective-permute-start(f32[4,16,128]{2,1,0:T(8,128)S(1)} %get-tuple-element.14), channel_id=1, source_target_pairs={{0,1000},{8,1008},{16,1016},{24,0},{32,8},{40,16},{48,24},{56,32},... | collective-permute-start | bytes 98312 | tf_op jit(solution)/shard_map/ppermute | solution.py:173
  44.7 9.9 %collective-permute-start.6 = (f32[14,16,128]{2,1,0:T(8,128)S(1)}, f32[14,16,128]{2,1,0:T(8,128)S(1)}, u32[]{:S(2)}, u32[]{:S(2)}) collective-permute-start(f32[14,16,128]{2,1,0:T(8,128)S(1)} %constant_dynamic-update-slice_fusion), channel_id=1, source_target_pairs={{0,8},{8,16},{16,24},{24,32},{32,40},{40,48},{48,56},{56,64},{64,7... | collective-permute-start | bytes 344072 | tf_op jit(solution)/shard_map/ppermute | solution.py:173
  46.7 9.5 %collective-permute-start.7 = (f32[14,16,128]{2,1,0:T(8,128)S(1)}, f32[14,16,128]{2,1,0:T(8,128)S(1)}, u32[]{:S(2)}, u32[]{:S(2)}) collective-permute-start(f32[14,16,128]{2,1,0:T(8,128)S(1)} %constant_dynamic-update-slice_fusion.5), channel_id=1, source_target_pairs={{0,1016},{8,0},{16,8},{24,16},{32,24},{40,32},{48,40},{56,48},{64,... | collective-permute-start | bytes 344072 | tf_op jit(solution)/shard_map/ppermute | solution.py:173
  56.2 6.2 %collective-permute-start.8 = (f32[26,8,128]{2,1,0:T(8,128)S(1)}, f32[26,8,128]{2,1,0:T(8,128)S(1)}, u32[]{:S(2)}, u32[]{:S(2)}) collective-permute-start(f32[26,8,128]{2,1,0:T(8,128)S(1)} %constant_dynamic-update-slice_fusion.10), channel_id=1, source_target_pairs={{0,7},{1,0},{2,1},{3,2},{4,3},{5,4},{6,5},{7,6},{8,15},{9,8},{10,9... | collective-permute-start | bytes 319496 | tf_op jit(solution)/shard_map/ppermute | solution.py:173
  61.5 1.7 %collective-permute-start.9 = (f32[26,8,128]{2,1,0:T(8,128)S(1)}, f32[26,8,128]{2,1,0:T(8,128)S(1)}, u32[]{:S(2)}, u32[]{:S(2)}) collective-permute-start(f32[26,8,128]{2,1,0:T(8,128)S(1)} %constant_dynamic-update-slice_fusion.15), channel_id=1, source_target_pairs={{0,1},{1,2},{2,3},{3,4},{4,5},{5,6},{6,7},{7,0},{8,9},{9,10},{10,1... | collective-permute-start | bytes 319496 | tf_op jit(solution)/shard_map/ppermute | solution.py:173

commit v11 on v9

--- a/solution.py
+++ b/solution.py
@@ -39,7 +39,7 @@
     return total + jnp.dot(high, weights, preferred_element_type=jnp.float32)
 
 
-def fine_kernel(field, density, xlo, xhi, clo, chi, smooth, d, coarse, coarse2, up, down, f, s1, pair, rows):
+def fine_kernel(field, density, xlo, xhi, chi, clo, smooth, d, coarse, coarse2, up, down, f, s1, pair, rows):
     f[0:3, 16:48] = xlo[0:3]
     f[3:7, 16:48] = field[...]
     f[7:10, 16:48] = xhi[0:3]
@@ -185,7 +185,7 @@
         fine_kernel,
         [(6, 48, 256), (8, 48, 256), (4, 16, 128), (4, 16, 128), (4, 16, 128), (4, 16, 128)],
         [(10, 64, 256), (8, 64, 256), (4, 2, 32, 128), (64, 256)],
-        field, density, xlo, xhi, clo, chi,
+        field, density, xlo, xhi, chi, clo,
     )
     flo, fhi = send(own, "gx", 3), send(own2, "gx", -3)
     nlo = send(jnp.concatenate([flo[1:2], flo[3:4], own, fhi, up], 0), "gx", 1)

time: 65.7 us -> 65.4 us (level)
  starting transfers between devices: 49.1 us -> 51.7 us
  waiting for transfers between devices: 11.6 us -> 9.24 us
    ppermute x10, starting transfers between devices: 49.1 us -> 51.7 us  [send(): lax.ppermute(values, axis, [(i, (i + step) % count) for i in range(count)])]
    ppermute x10, waiting for transfers between devices: 11.6 us -> 9.24 us  [send(): lax.ppermute(values, axis, [(i, (i + step) % count) for i in range(count)])]
where the time goes in v11:
time: 65.4 us; the launch traced here: 65.1 us
  starting transfers between devices  51.7 us (79%)
  waiting for transfers between devices  9.24 us (14%)
  Pallas kernels  2.7 us (4%)
  local copies, waits for them, and re-layouts  1.09 us (2%)
    ppermute x10, starting transfers between devices, send(): lax.ppermute(values, axis, [(i, (i + step) % count) for i in range(count)])  51.7 us
    ppermute x10, waiting for transfers between devices, send(): lax.ppermute(values, axis, [(i, (i + step) % count) for i in range(count)])  9.24 us
    pallas_call x2, Pallas kernels, call(): pl.pallas_call(kernel, out_shape=shapes, in_specs=[vmem] * len(args), out...  2.7 us
  transfers between devices with their start and end apart: 10, of which 7 were waited for; matrix products, arithmetic and copies ran while one was open for 0% of the time, Pallas kernels for 0%

profile of v11, /device:TPU:1, one launch (start us, length us, event | category | flops | bytes accessed | tf_op | source)
XLA Modules:
  0.0 65.1 jit_solution(12402537146953239223)
XLA Ops:
  0.0 0.0 copy-start
  0.0 0.9 %fusion.5 = (f32[2,32,256]{2,1,0:T(8,128)S(1)}, f32[2,32,256]{2,1,0:T(8,128)S(1)}) fusion(f32[4,32,256]{2,1,0:T(8,128)} %density.1), kind=kLoop, calls=%fused_computation.29 | loop fusion | bytes 262144 | tf_op jit(solution)/shard_map/slice | solution.py:181
  0.9 0.0 copy-done
  1.0 4.4 %collective-permute-start = (f32[5,32,256]{2,1,0:T(8,128)S(1)}, f32[5,32,256]{2,1,0:T(8,128)S(1)}, u32[]{:S(2)}, u32[]{:S(2)}) collective-permute-start(f32[5,32,256]{2,1,0:T(8,128)S(1)} %pad_maximum_fusion), channel_id=1, source_target_pairs={{0,8},{8,16},{16,24},{24,32},{32,40},{40,48},{48,56},{56,64},{64,7... | collective-permute-start | bytes 491528 | tf_op jit(solution)/shard_map/ppermute | solution.py:168
  5.4 0.0 copy-start.1
  5.4 19.4 %collective-permute-start.1 = (f32[5,32,256]{2,1,0:T(8,128)S(1)}, f32[5,32,256]{2,1,0:T(8,128)S(1)}, u32[]{:S(2)}, u32[]{:S(2)}) collective-permute-start(f32[5,32,256]{2,1,0:T(8,128)S(1)} %pad_maximum_fusion.1), channel_id=1, source_target_pairs={{0,1016},{8,0},{16,8},{24,16},{32,24},{40,32},{48,40},{56,48},{64,... | collective-permute-start | bytes 491528 | tf_op jit(solution)/shard_map/ppermute | solution.py:168
  24.8 0.0 copy-done.1
  24.8 2.8 %collective-permute-done.1.xhi = f32[5,32,256]{2,1,0:T(8,128)S(1)} collective-permute-done((f32[5,32,256]{2,1,0:T(8,128)S(1)}, f32[5,32,256]{2,1,0:T(8,128)S(1)}, u32[]{:S(2)}, u32[]{:S(2)}) %collective-permute-start.1) | collective-permute-done | bytes 163872 | tf_op jit(solution)/shard_map/ppermute | solution.py:168
  27.6 0.0 collective-permute-done.xlo
  27.7 1.6 %collective-permute-start.2 = (f32[18,4,256]{2,1,0:T(4,128)S(1)}, f32[18,4,256]{2,1,0:T(4,128)S(1)}, u32[]{:S(2)}, u32[]{:S(2)}) collective-permute-start(f32[18,4,256]{2,1,0:T(4,128)S(1)} %pad_maximum_fusion.2), channel_id=1, source_target_pairs={{0,7},{1,0},{2,1},{3,2},{4,3},{5,4},{6,5},{7,6},{8,15},{9,8},{10,9... | collective-permute-start | bytes 221192 | tf_op jit(solution)/shard_map/ppermute | solution.py:168
  29.3 1.1 %collective-permute-start.3 = (f32[18,4,256]{2,1,0:T(4,128)S(1)}, f32[18,4,256]{2,1,0:T(4,128)S(1)}, u32[]{:S(2)}, u32[]{:S(2)}) collective-permute-start(f32[18,4,256]{2,1,0:T(4,128)S(1)} %pad_maximum_fusion.3), channel_id=1, source_target_pairs={{0,1},{1,2},{2,3},{3,4},{4,5},{5,6},{6,7},{7,0},{8,9},{9,10},{10,1... | collective-permute-start | bytes 221192 | tf_op jit(solution)/shard_map/ppermute | solution.py:168
  30.4 2.0 %collective-permute-done.2.chi = f32[18,4,256]{2,1,0:T(4,128)S(1)} collective-permute-done((f32[18,4,256]{2,1,0:T(4,128)S(1)}, f32[18,4,256]{2,1,0:T(4,128)S(1)}, u32[]{:S(2)}, u32[]{:S(2)}) %collective-permute-start.2) | collective-permute-done | bytes 73760 | tf_op jit(solution)/shard_map/ppermute | solution.py:168
  32.4 0.0 collective-permute-done.3.clo
  32.4 0.8 %shard_map.28 = (f32[6,48,256]{2,1,0:T(8,128)S(1)}, f32[8,48,256]{2,1,0:T(8,128)S(1)}, f32[4,16,128]{2,1,0:T(8,128)S(1)}, f32[4,16,128]{2,1,0:T(8,128)S(1)}, f32...) custom-call(f32[4,32,256]{2,1,0:T(8,128)S(1)} %copy-done, f32[4,32,256]{2,1,0:T(8,128)S(1)} %copy-done.1, ...), custom_call_target="tpu_custom_call" | custom-call | tf_op jit(solution)/shard_map/pallas_call | solution.py:156
  33.2 1.9 %collective-permute-start.4 = (f32[4,16,128]{2,1,0:T(8,128)S(1)}, f32[4,16,128]{2,1,0:T(8,128)S(1)}, u32[]{:S(2)}, u32[]{:S(2)}) collective-permute-start(f32[4,16,128]{2,1,0:T(8,128)S(1)} %get-tuple-element.13.own), channel_id=1, source_target_pairs={{0,24},{8,32},{16,40},{24,48},{32,56},{40,64},{48,72},{56,80},{64,... | collective-permute-start | bytes 98312 | tf_op jit(solution)/shard_map/ppermute | solution.py:168
  35.1 8.5 %collective-permute-start.5 = (f32[4,16,128]{2,1,0:T(8,128)S(1)}, f32[4,16,128]{2,1,0:T(8,128)S(1)}, u32[]{:S(2)}, u32[]{:S(2)}) collective-permute-start(f32[4,16,128]{2,1,0:T(8,128)S(1)} %get-tuple-element.14), channel_id=1, source_target_pairs={{0,1000},{8,1008},{16,1016},{24,0},{32,8},{40,16},{48,24},{56,32},... | collective-permute-start | bytes 98312 | tf_op jit(solution)/shard_map/ppermute | solution.py:168
  43.6 1.0 %collective-permute-done.5.fhi = f32[4,16,128]{2,1,0:T(8,128)S(1)} collective-permute-done((f32[4,16,128]{2,1,0:T(8,128)S(1)}, f32[4,16,128]{2,1,0:T(8,128)S(1)}, u32[]{:S(2)}, u32[]{:S(2)}) %collective-permute-start.5) | collective-permute-done | bytes 32800 | tf_op jit(solution)/shard_map/ppermute | solution.py:168
  44.6 0.0 collective-permute-done.4.flo
  44.7 1.9 %collective-permute-start.6 = (f32[14,16,128]{2,1,0:T(8,128)S(1)}, f32[14,16,128]{2,1,0:T(8,128)S(1)}, u32[]{:S(2)}, u32[]{:S(2)}) collective-permute-start(f32[14,16,128]{2,1,0:T(8,128)S(1)} %constant_dynamic-update-slice_fusion), channel_id=1, source_target_pairs={{0,8},{8,16},{16,24},{24,32},{32,40},{40,48},{48,56},{56,64},{64,7... | collective-permute-start | bytes 344072 | tf_op jit(solution)/shard_map/ppermute | solution.py:168
  46.6 7.7 %collective-permute-start.7 = (f32[14,16,128]{2,1,0:T(8,128)S(1)}, f32[14,16,128]{2,1,0:T(8,128)S(1)}, u32[]{:S(2)}, u32[]{:S(2)}) collective-permute-start(f32[14,16,128]{2,1,0:T(8,128)S(1)} %constant_dynamic-update-slice_fusion.5), channel_id=1, source_target_pairs={{0,1016},{8,0},{16,8},{24,16},{32,24},{40,32},{48,40},{56,48},{64,... | collective-permute-start | bytes 344072 | tf_op jit(solution)/shard_map/ppermute | solution.py:168
  54.4 0.2 collective-permute-done.6.nlo
  54.6 1.6 %collective-permute-done.7.nhi = f32[14,16,128]{2,1,0:T(8,128)S(1)} collective-permute-done((f32[14,16,128]{2,1,0:T(8,128)S(1)}, f32[14,16,128]{2,1,0:T(8,128)S(1)}, u32[]{:S(2)}, u32[]{:S(2)}) %collective-permute-start.7) | collective-permute-done | bytes 114720 | tf_op jit(solution)/shard_map/ppermute | solution.py:168
  56.2 5.2 %collective-permute-start.8 = (f32[26,8,128]{2,1,0:T(8,128)S(1)}, f32[26,8,128]{2,1,0:T(8,128)S(1)}, u32[]{:S(2)}, u32[]{:S(2)}) collective-permute-start(f32[26,8,128]{2,1,0:T(8,128)S(1)} %constant_dynamic-update-slice_fusion.10), channel_id=1, source_target_pairs={{0,7},{1,0},{2,1},{3,2},{4,3},{5,4},{6,5},{7,6},{8,15},{9,8},{10,9... | collective-permute-start | bytes 319496 | tf_op jit(solution)/shard_map/ppermute | solution.py:168
  61.4 0.0 collective-permute-start.9
  61.5 0.9 %collective-permute-done.8.zrows = f32[26,8,128]{2,1,0:T(8,128)S(1)} collective-permute-done((f32[26,8,128]{2,1,0:T(8,128)S(1)}, f32[26,8,128]{2,1,0:T(8,128)S(1)}, u32[]{:S(2)}, u32[]{:S(2)}) %collective-permute-start.8) | collective-permute-done | bytes 106528 | tf_op jit(solution)/shard_map/ppermute | solution.py:168
  62.4 0.8 %collective-permute-done.9.yrows = f32[26,8,128]{2,1,0:T(8,128)S(1)} collective-permute-done((f32[26,8,128]{2,1,0:T(8,128)S(1)}, f32[26,8,128]{2,1,0:T(8,128)S(1)}, u32[]{:S(2)}, u32[]{:S(2)}) %collective-permute-start.9) | collective-permute-done | bytes 106528 | tf_op jit(solution)/shard_map/ppermute | solution.py:168
  63.2 1.9 %shard_map.29 = f32[4,32,256]{2,1,0:T(8,128)} custom-call(f32[6,48,256]{2,1,0:T(8,128)S(1)} %get-tuple-element.11.smooth, f32[8,48,256]{2,1,0:T(8,128)S(1)} %get-tuple-element.12.dens, f32[4,16,128]{2,1,0:T(8,128)S(1)} %get-tuple-element.13.own, f32[4,16,128]{2,1,0:T(8,128)S(1)} %collective-permute-done.4.flo, f32[4,16,128]{2,1,0:T(8,128)S(1)} %collective-permute-done.5.fhi, ...), custom_call_target="tpu_custom_call" | custom-call | tf_op jit(solution)/shard_map/pallas_call | solution.py:156
  (28 shorter events, 0.2 us)
Async XLA Ops:
  0.0 1.0 %copy-start = (f32[4,32,256]{2,1,0:T(8,128)S(1)}, f32[4,32,256]{2,1,0:T(8,128)}, u32[]{:S(2)}) copy-start(f32[4,32,256]{2,1,0:T(8,128)} %field.1) | copy-start | bytes 393220
  1.0 26.6 %collective-permute-start = (f32[5,32,256]{2,1,0:T(8,128)S(1)}, f32[5,32,256]{2,1,0:T(8,128)S(1)}, u32[]{:S(2)}, u32[]{:S(2)}) collective-permute-start(f32[5,32,256]{2,1,0:T(8,128)S(1)} %pad_maximum_fusion), channel_id=1, source_target_pairs={{0,8},{8,16},{16,24},{24,32},{32,40},{40,48},{48,56},{56,64},{64,7... | collective-permute-start | bytes 491528 | tf_op jit(solution)/shard_map/ppermute | solution.py:168
  5.4 19.4 %copy-start.1 = (f32[4,32,256]{2,1,0:T(8,128)S(1)}, f32[4,32,256]{2,1,0:T(8,128)}, u32[]{:S(2)}) copy-start(f32[4,32,256]{2,1,0:T(8,128)} %density.1) | copy-start | bytes 393220
  5.4 22.2 %collective-permute-start.1 = (f32[5,32,256]{2,1,0:T(8,128)S(1)}, f32[5,32,256]{2,1,0:T(8,128)S(1)}, u32[]{:S(2)}, u32[]{:S(2)}) collective-permute-start(f32[5,32,256]{2,1,0:T(8,128)S(1)} %pad_maximum_fusion.1), channel_id=1, source_target_pairs={{0,1016},{8,0},{16,8},{24,16},{32,24},{40,32},{48,40},{56,48},{64,... | collective-permute-start | bytes 491528 | tf_op jit(solution)/shard_map/ppermute | solution.py:168
  27.7 4.7 %collective-permute-start.2 = (f32[18,4,256]{2,1,0:T(4,128)S(1)}, f32[18,4,256]{2,1,0:T(4,128)S(1)}, u32[]{:S(2)}, u32[]{:S(2)}) collective-permute-start(f32[18,4,256]{2,1,0:T(4,128)S(1)} %pad_maximum_fusion.2), channel_id=1, source_target_pairs={{0,7},{1,0},{2,1},{3,2},{4,3},{5,4},{6,5},{7,6},{8,15},{9,8},{10,9... | collective-permute-start | bytes 221192 | tf_op jit(solution)/shard_map/ppermute | solution.py:168
  29.3 3.1 %collective-permute-start.3 = (f32[18,4,256]{2,1,0:T(4,128)S(1)}, f32[18,4,256]{2,1,0:T(4,128)S(1)}, u32[]{:S(2)}, u32[]{:S(2)}) collective-permute-start(f32[18,4,256]{2,1,0:T(4,128)S(1)} %pad_maximum_fusion.3), channel_id=1, source_target_pairs={{0,1},{1,2},{2,3},{3,4},{4,5},{5,6},{6,7},{7,0},{8,9},{9,10},{10,1... | collective-permute-start | bytes 221192 | tf_op jit(solution)/shard_map/ppermute | solution.py:168
  33.2 11.4 %collective-permute-start.4 = (f32[4,16,128]{2,1,0:T(8,128)S(1)}, f32[4,16,128]{2,1,0:T(8,128)S(1)}, u32[]{:S(2)}, u32[]{:S(2)}) collective-permute-start(f32[4,16,128]{2,1,0:T(8,128)S(1)} %get-tuple-element.13.own), channel_id=1, source_target_pairs={{0,24},{8,32},{16,40},{24,48},{32,56},{40,64},{48,72},{56,80},{64,... | collective-permute-start | bytes 98312 | tf_op jit(solution)/shard_map/ppermute | solution.py:168
  35.1 9.5 %collective-permute-start.5 = (f32[4,16,128]{2,1,0:T(8,128)S(1)}, f32[4,16,128]{2,1,0:T(8,128)S(1)}, u32[]{:S(2)}, u32[]{:S(2)}) collective-permute-start(f32[4,16,128]{2,1,0:T(8,128)S(1)} %get-tuple-element.14), channel_id=1, source_target_pairs={{0,1000},{8,1008},{16,1016},{24,0},{32,8},{40,16},{48,24},{56,32},... | collective-permute-start | bytes 98312 | tf_op jit(solution)/shard_map/ppermute | solution.py:168
  44.7 9.9 %collective-permute-start.6 = (f32[14,16,128]{2,1,0:T(8,128)S(1)}, f32[14,16,128]{2,1,0:T(8,128)S(1)}, u32[]{:S(2)}, u32[]{:S(2)}) collective-permute-start(f32[14,16,128]{2,1,0:T(8,128)S(1)} %constant_dynamic-update-slice_fusion), channel_id=1, source_target_pairs={{0,8},{8,16},{16,24},{24,32},{32,40},{40,48},{48,56},{56,64},{64,7... | collective-permute-start | bytes 344072 | tf_op jit(solution)/shard_map/ppermute | solution.py:168
  46.6 9.5 %collective-permute-start.7 = (f32[14,16,128]{2,1,0:T(8,128)S(1)}, f32[14,16,128]{2,1,0:T(8,128)S(1)}, u32[]{:S(2)}, u32[]{:S(2)}) collective-permute-start(f32[14,16,128]{2,1,0:T(8,128)S(1)} %constant_dynamic-update-slice_fusion.5), channel_id=1, source_target_pairs={{0,1016},{8,0},{16,8},{24,16},{32,24},{40,32},{48,40},{56,48},{64,... | collective-permute-start | bytes 344072 | tf_op jit(solution)/shard_map/ppermute | solution.py:168
  56.2 6.2 %collective-permute-start.8 = (f32[26,8,128]{2,1,0:T(8,128)S(1)}, f32[26,8,128]{2,1,0:T(8,128)S(1)}, u32[]{:S(2)}, u32[]{:S(2)}) collective-permute-start(f32[26,8,128]{2,1,0:T(8,128)S(1)} %constant_dynamic-update-slice_fusion.10), channel_id=1, source_target_pairs={{0,7},{1,0},{2,1},{3,2},{4,3},{5,4},{6,5},{7,6},{8,15},{9,8},{10,9... | collective-permute-start | bytes 319496 | tf_op jit(solution)/shard_map/ppermute | solution.py:168
  61.4 1.7 %collective-permute-start.9 = (f32[26,8,128]{2,1,0:T(8,128)S(1)}, f32[26,8,128]{2,1,0:T(8,128)S(1)}, u32[]{:S(2)}, u32[]{:S(2)}) collective-permute-start(f32[26,8,128]{2,1,0:T(8,128)S(1)} %constant_dynamic-update-slice_fusion.15), channel_id=1, source_target_pairs={{0,1},{1,2},{2,3},{3,4},{4,5},{5,6},{6,7},{7,0},{8,9},{9,10},{10,1... | collective-permute-start | bytes 319496 | tf_op jit(solution)/shard_map/ppermute | solution.py:168

commit v12 on v11

--- a/solution.py
+++ b/solution.py
@@ -46,13 +46,15 @@
     d[0:2, 8:40] = xlo[3:5]
     d[2:6, 8:40] = density[...]
     d[6:8, 8:40] = xhi[3:5]
-    for side, at in ((clo, 4), (chi, 40)):
-        f[0:3, at + 8 : at + 12] = side[0:3]
-        f[3:7, at + 8 : at + 12] = side[10:14]
-        f[7:10, at + 8 : at + 12] = side[5:8]
-        d[0:2, at : at + 4] = side[3:5]
-        d[2:6, at : at + 4] = side[14:18]
-        d[6:8, at : at + 4] = side[8:10]
+    for side, at, two in ((clo, 4, 6), (chi, 40, 40)):
+        f[0:2, two + 8 : two + 10] = side[0:2, 2:4]
+        f[8:10, two + 8 : two + 10] = side[0:2, 0:2]
+        d[0:2, two : two + 2] = side[2:4, 2:4]
+        d[6:8, two : two + 2] = side[2:4, 0:2]
+        f[2, at + 8 : at + 12] = side[5]
+        f[7, at + 8 : at + 12] = side[4]
+        f[3:7, at + 8 : at + 12] = side[6:10]
+        d[2:6, at : at + 4] = side[10:14]
     for i in range(8):
         s1[i, 8:56] = jacobi(f, i + 1, slice(8, 56), d[i], 1.0)
     for i in range(6):
@@ -168,6 +170,11 @@
     return lax.ppermute(values, axis, [(i, (i + step) % count) for i in range(count)])
 
 
+def edge_rows(field, density, xlo, xhi, four, two):
+    outer = [jnp.concatenate([xhi[j, two], xlo[i, two]], 1) for i, j in ((slice(0, 2), slice(1, 3)), (slice(3, 5), slice(3, 5)))]
+    return jnp.concatenate(outer + [xhi[0:1, four], xlo[2:3, four], field[:, four], density[:, four]], 0)
+
+
 def rows_from_sides(near, far):
     last = [piece[:, 8:16] for piece in near]
     last += [jnp.concatenate([low[:, 12:16], high[:, 12:16]], 1) for low, high in far]
@@ -179,8 +186,8 @@
 def body(density, field):
     xlo = send(jnp.concatenate([field[1:4], density[2:4]], 0), "gx", 1)
     xhi = send(jnp.concatenate([field[0:3], density[0:2]], 0), "gx", -1)
-    clo = send(jnp.concatenate([xlo[:, 28:32], xhi[:, 28:32], field[:, 28:32], density[:, 28:32]], 0), "gy", 1)
-    chi = send(jnp.concatenate([xlo[:, 0:4], xhi[:, 0:4], field[:, 0:4], density[:, 0:4]], 0), "gy", -1)
+    clo = send(edge_rows(field, density, xlo, xhi, slice(28, 32), slice(30, 32)), "gy", 1)
+    chi = send(edge_rows(field, density, xlo, xhi, slice(0, 4), slice(0, 2)), "gy", -1)
     smooth, dens, own, own2, up, down = call(
         fine_kernel,
         [(6, 48, 256), (8, 48, 256), (4, 16, 128), (4, 16, 128), (4, 16, 128), (4, 16, 128)],

time: 65.4 us -> 65.2 us (level)
  transfers between devices with their start and end apart: 10 -> 10, of which waited for: 7 -> 8; matrix products, arithmetic and copies ran while one was open for 0% -> 0% of each run, Pallas kernels for 0% -> 0%
where the time goes in v12:
time: 65.2 us; the launch traced here: 64.9 us
  starting transfers between devices  51.7 us (79%)
  waiting for transfers between devices  9.11 us (14%)
  Pallas kernels  2.7 us (4%)
  local copies, waits for them, and re-layouts  1.12 us (2%)
    ppermute x10, starting transfers between devices, send(): lax.ppermute(values, axis, [(i, (i + step) % count) for i in range(count)])  51.7 us
    ppermute x10, waiting for transfers between devices, send(): lax.ppermute(values, axis, [(i, (i + step) % count) for i in range(count)])  9.11 us
    pallas_call x2, Pallas kernels, call(): pl.pallas_call(kernel, out_shape=shapes, in_specs=[vmem] * len(args), out...  2.7 us
  transfers between devices with their start and end apart: 10, of which 8 were waited for; matrix products, arithmetic and copies ran while one was open for 0% of the time, Pallas kernels for 0%

profile of v12, /device:TPU:1, one launch (start us, length us, event | category | flops | bytes accessed | tf_op | source)
XLA Modules:
  0.0 64.9 jit_solution(5853643863792950576)
XLA Ops:
  0.0 0.0 copy-start
  0.0 0.9 %fusion.3 = (f32[2,32,256]{2,1,0:T(8,128)S(1)}, f32[2,32,256]{2,1,0:T(8,128)S(1)}) fusion(f32[4,32,256]{2,1,0:T(8,128)} %density.1), kind=kLoop, calls=%fused_computation.37 | loop fusion | bytes 262144 | tf_op jit(solution)/shard_map/slice | solution.py:188
  0.9 0.0 copy-done
  1.0 4.4 %collective-permute-start = (f32[5,32,256]{2,1,0:T(8,128)S(1)}, f32[5,32,256]{2,1,0:T(8,128)S(1)}, u32[]{:S(2)}, u32[]{:S(2)}) collective-permute-start(f32[5,32,256]{2,1,0:T(8,128)S(1)} %pad_maximum_fusion), channel_id=1, source_target_pairs={{0,8},{8,16},{16,24},{24,32},{32,40},{40,48},{48,56},{56,64},{64,7... | collective-permute-start | bytes 491528 | tf_op jit(solution)/shard_map/ppermute | solution.py:170
  5.4 0.0 copy-start.1
  5.4 19.4 %collective-permute-start.1 = (f32[5,32,256]{2,1,0:T(8,128)S(1)}, f32[5,32,256]{2,1,0:T(8,128)S(1)}, u32[]{:S(2)}, u32[]{:S(2)}) collective-permute-start(f32[5,32,256]{2,1,0:T(8,128)S(1)} %pad_maximum_fusion.1), channel_id=1, source_target_pairs={{0,1016},{8,0},{16,8},{24,16},{32,24},{40,32},{48,40},{56,48},{64,... | collective-permute-start | bytes 491528 | tf_op jit(solution)/shard_map/ppermute | solution.py:170
  24.8 1.8 %collective-permute-done.xlo = f32[5,32,256]{2,1,0:T(8,128)S(1)} collective-permute-done((f32[5,32,256]{2,1,0:T(8,128)S(1)}, f32[5,32,256]{2,1,0:T(8,128)S(1)}, u32[]{:S(2)}, u32[]{:S(2)}) %collective-permute-start) | collective-permute-done | bytes 163872 | tf_op jit(solution)/shard_map/ppermute | solution.py:170
  26.6 1.0 %collective-permute-done.1.xhi = f32[5,32,256]{2,1,0:T(8,128)S(1)} collective-permute-done((f32[5,32,256]{2,1,0:T(8,128)S(1)}, f32[5,32,256]{2,1,0:T(8,128)S(1)}, u32[]{:S(2)}, u32[]{:S(2)}) %collective-permute-start.1) | collective-permute-done | bytes 163872 | tf_op jit(solution)/shard_map/ppermute | solution.py:170
  27.7 0.0 copy-done.1
  27.8 1.6 %collective-permute-start.2 = (f32[14,4,256]{2,1,0:T(4,128)S(1)}, f32[14,4,256]{2,1,0:T(4,128)S(1)}, u32[]{:S(2)}, u32[]{:S(2)}) collective-permute-start(f32[14,4,256]{2,1,0:T(4,128)S(1)} %get-tuple-element.30), channel_id=1, source_target_pairs={{0,7},{1,0},{2,1},{3,2},{4,3},{5,4},{6,5},{7,6},{8,15},{9,8},{10,9... | collective-permute-start | bytes 172040 | tf_op jit(solution)/shard_map/ppermute | solution.py:170
  29.3 1.1 %collective-permute-start.3 = (f32[14,4,256]{2,1,0:T(4,128)S(1)}, f32[14,4,256]{2,1,0:T(4,128)S(1)}, u32[]{:S(2)}, u32[]{:S(2)}) collective-permute-start(f32[14,4,256]{2,1,0:T(4,128)S(1)} %get-tuple-element.29), channel_id=1, source_target_pairs={{0,1},{1,2},{2,3},{3,4},{4,5},{5,6},{6,7},{7,0},{8,9},{9,10},{10,1... | collective-permute-start | bytes 172040 | tf_op jit(solution)/shard_map/ppermute | solution.py:170
  30.4 1.8 %collective-permute-done.2.chi = f32[14,4,256]{2,1,0:T(4,128)S(1)} collective-permute-done((f32[14,4,256]{2,1,0:T(4,128)S(1)}, f32[14,4,256]{2,1,0:T(4,128)S(1)}, u32[]{:S(2)}, u32[]{:S(2)}) %collective-permute-start.2) | collective-permute-done | bytes 57376 | tf_op jit(solution)/shard_map/ppermute | solution.py:170
  32.3 0.0 collective-permute-done.3.clo
  32.3 0.8 %shard_map.28 = (f32[6,48,256]{2,1,0:T(8,128)S(1)}, f32[8,48,256]{2,1,0:T(8,128)S(1)}, f32[4,16,128]{2,1,0:T(8,128)S(1)}, f32[4,16,128]{2,1,0:T(8,128)S(1)}, f32...) custom-call(f32[4,32,256]{2,1,0:T(8,128)S(1)} %copy-done, f32[4,32,256]{2,1,0:T(8,128)S(1)} %copy-done.1, ...), custom_call_target="tpu_custom_call" | custom-call | tf_op jit(solution)/shard_map/pallas_call | solution.py:158
  33.1 1.9 %collective-permute-start.4 = (f32[4,16,128]{2,1,0:T(8,128)S(1)}, f32[4,16,128]{2,1,0:T(8,128)S(1)}, u32[]{:S(2)}, u32[]{:S(2)}) collective-permute-start(f32[4,16,128]{2,1,0:T(8,128)S(1)} %get-tuple-element.13.own), channel_id=1, source_target_pairs={{0,24},{8,32},{16,40},{24,48},{32,56},{40,64},{48,72},{56,80},{64,... | collective-permute-start | bytes 98312 | tf_op jit(solution)/shard_map/ppermute | solution.py:170
  35.0 8.5 %collective-permute-start.5 = (f32[4,16,128]{2,1,0:T(8,128)S(1)}, f32[4,16,128]{2,1,0:T(8,128)S(1)}, u32[]{:S(2)}, u32[]{:S(2)}) collective-permute-start(f32[4,16,128]{2,1,0:T(8,128)S(1)} %get-tuple-element.14), channel_id=1, source_target_pairs={{0,1000},{8,1008},{16,1016},{24,0},{32,8},{40,16},{48,24},{56,32},... | collective-permute-start | bytes 98312 | tf_op jit(solution)/shard_map/ppermute | solution.py:170
  43.5 1.0 %collective-permute-done.5.fhi = f32[4,16,128]{2,1,0:T(8,128)S(1)} collective-permute-done((f32[4,16,128]{2,1,0:T(8,128)S(1)}, f32[4,16,128]{2,1,0:T(8,128)S(1)}, u32[]{:S(2)}, u32[]{:S(2)}) %collective-permute-start.5) | collective-permute-done | bytes 32800 | tf_op jit(solution)/shard_map/ppermute | solution.py:170
  44.5 0.0 collective-permute-done.4.flo
  44.6 1.9 %collective-permute-start.6 = (f32[14,16,128]{2,1,0:T(8,128)S(1)}, f32[14,16,128]{2,1,0:T(8,128)S(1)}, u32[]{:S(2)}, u32[]{:S(2)}) collective-permute-start(f32[14,16,128]{2,1,0:T(8,128)S(1)} %constant_dynamic-update-slice_fusion.12), channel_id=1, source_target_pairs={{0,8},{8,16},{16,24},{24,32},{32,40},{40,48},{48,56},{56,64},{64,7... | collective-permute-start | bytes 344072 | tf_op jit(solution)/shard_map/ppermute | solution.py:170
  46.5 7.7 %collective-permute-start.7 = (f32[14,16,128]{2,1,0:T(8,128)S(1)}, f32[14,16,128]{2,1,0:T(8,128)S(1)}, u32[]{:S(2)}, u32[]{:S(2)}) collective-permute-start(f32[14,16,128]{2,1,0:T(8,128)S(1)} %constant_dynamic-update-slice_fusion.17), channel_id=1, source_target_pairs={{0,1016},{8,0},{16,8},{24,16},{32,24},{40,32},{48,40},{56,48},{64,... | collective-permute-start | bytes 344072 | tf_op jit(solution)/shard_map/ppermute | solution.py:170
  54.3 0.2 collective-permute-done.6.nlo
  54.5 1.6 %collective-permute-done.7.nhi = f32[14,16,128]{2,1,0:T(8,128)S(1)} collective-permute-done((f32[14,16,128]{2,1,0:T(8,128)S(1)}, f32[14,16,128]{2,1,0:T(8,128)S(1)}, u32[]{:S(2)}, u32[]{:S(2)}) %collective-permute-start.7) | collective-permute-done | bytes 114720 | tf_op jit(solution)/shard_map/ppermute | solution.py:170
  56.1 5.2 %collective-permute-start.8 = (f32[26,8,128]{2,1,0:T(8,128)S(1)}, f32[26,8,128]{2,1,0:T(8,128)S(1)}, u32[]{:S(2)}, u32[]{:S(2)}) collective-permute-start(f32[26,8,128]{2,1,0:T(8,128)S(1)} %constant_dynamic-update-slice_fusion.22), channel_id=1, source_target_pairs={{0,7},{1,0},{2,1},{3,2},{4,3},{5,4},{6,5},{7,6},{8,15},{9,8},{10,9... | collective-permute-start | bytes 319496 | tf_op jit(solution)/shard_map/ppermute | solution.py:170
  61.3 0.0 collective-permute-start.9
  61.3 0.9 %collective-permute-done.8.zrows = f32[26,8,128]{2,1,0:T(8,128)S(1)} collective-permute-done((f32[26,8,128]{2,1,0:T(8,128)S(1)}, f32[26,8,128]{2,1,0:T(8,128)S(1)}, u32[]{:S(2)}, u32[]{:S(2)}) %collective-permute-start.8) | collective-permute-done | bytes 106528 | tf_op jit(solution)/shard_map/ppermute | solution.py:170
  62.3 0.8 %collective-permute-done.9.yrows = f32[26,8,128]{2,1,0:T(8,128)S(1)} collective-permute-done((f32[26,8,128]{2,1,0:T(8,128)S(1)}, f32[26,8,128]{2,1,0:T(8,128)S(1)}, u32[]{:S(2)}, u32[]{:S(2)}) %collective-permute-start.9) | collective-permute-done | bytes 106528 | tf_op jit(solution)/shard_map/ppermute | solution.py:170
  63.0 1.9 %shard_map.29 = f32[4,32,256]{2,1,0:T(8,128)} custom-call(f32[6,48,256]{2,1,0:T(8,128)S(1)} %get-tuple-element.11.smooth, f32[8,48,256]{2,1,0:T(8,128)S(1)} %get-tuple-element.12.dens, f32[4,16,128]{2,1,0:T(8,128)S(1)} %get-tuple-element.13.own, f32[4,16,128]{2,1,0:T(8,128)S(1)} %collective-permute-done.4.flo, f32[4,16,128]{2,1,0:T(8,128)S(1)} %collective-permute-done.5.fhi, ...), custom_call_target="tpu_custom_call" | custom-call | tf_op jit(solution)/shard_map/pallas_call | solution.py:158
  (32 shorter events, 0.3 us)
Async XLA Ops:
  0.0 1.0 %copy-start = (f32[4,32,256]{2,1,0:T(8,128)S(1)}, f32[4,32,256]{2,1,0:T(8,128)}, u32[]{:S(2)}) copy-start(f32[4,32,256]{2,1,0:T(8,128)} %field.1) | copy-start | bytes 393220
  1.0 25.6 %collective-permute-start = (f32[5,32,256]{2,1,0:T(8,128)S(1)}, f32[5,32,256]{2,1,0:T(8,128)S(1)}, u32[]{:S(2)}, u32[]{:S(2)}) collective-permute-start(f32[5,32,256]{2,1,0:T(8,128)S(1)} %pad_maximum_fusion), channel_id=1, source_target_pairs={{0,8},{8,16},{16,24},{24,32},{32,40},{40,48},{48,56},{56,64},{64,7... | collective-permute-start | bytes 491528 | tf_op jit(solution)/shard_map/ppermute | solution.py:170
  5.4 22.3 %copy-start.1 = (f32[4,32,256]{2,1,0:T(8,128)S(1)}, f32[4,32,256]{2,1,0:T(8,128)}, u32[]{:S(2)}) copy-start(f32[4,32,256]{2,1,0:T(8,128)} %density.1) | copy-start | bytes 393220
  5.4 22.2 %collective-permute-start.1 = (f32[5,32,256]{2,1,0:T(8,128)S(1)}, f32[5,32,256]{2,1,0:T(8,128)S(1)}, u32[]{:S(2)}, u32[]{:S(2)}) collective-permute-start(f32[5,32,256]{2,1,0:T(8,128)S(1)} %pad_maximum_fusion.1), channel_id=1, source_target_pairs={{0,1016},{8,0},{16,8},{24,16},{32,24},{40,32},{48,40},{56,48},{64,... | collective-permute-start | bytes 491528 | tf_op jit(solution)/shard_map/ppermute | solution.py:170
  27.8 4.5 %collective-permute-start.2 = (f32[14,4,256]{2,1,0:T(4,128)S(1)}, f32[14,4,256]{2,1,0:T(4,128)S(1)}, u32[]{:S(2)}, u32[]{:S(2)}) collective-permute-start(f32[14,4,256]{2,1,0:T(4,128)S(1)} %get-tuple-element.30), channel_id=1, source_target_pairs={{0,7},{1,0},{2,1},{3,2},{4,3},{5,4},{6,5},{7,6},{8,15},{9,8},{10,9... | collective-permute-start | bytes 172040 | tf_op jit(solution)/shard_map/ppermute | solution.py:170
  29.3 3.0 %collective-permute-start.3 = (f32[14,4,256]{2,1,0:T(4,128)S(1)}, f32[14,4,256]{2,1,0:T(4,128)S(1)}, u32[]{:S(2)}, u32[]{:S(2)}) collective-permute-start(f32[14,4,256]{2,1,0:T(4,128)S(1)} %get-tuple-element.29), channel_id=1, source_target_pairs={{0,1},{1,2},{2,3},{3,4},{4,5},{5,6},{6,7},{7,0},{8,9},{9,10},{10,1... | collective-permute-start | bytes 172040 | tf_op jit(solution)/shard_map/ppermute | solution.py:170
  33.1 11.4 %collective-permute-start.4 = (f32[4,16,128]{2,1,0:T(8,128)S(1)}, f32[4,16,128]{2,1,0:T(8,128)S(1)}, u32[]{:S(2)}, u32[]{:S(2)}) collective-permute-start(f32[4,16,128]{2,1,0:T(8,128)S(1)} %get-tuple-element.13.own), channel_id=1, source_target_pairs={{0,24},{8,32},{16,40},{24,48},{32,56},{40,64},{48,72},{56,80},{64,... | collective-permute-start | bytes 98312 | tf_op jit(solution)/shard_map/ppermute | solution.py:170
  35.0 9.5 %collective-permute-start.5 = (f32[4,16,128]{2,1,0:T(8,128)S(1)}, f32[4,16,128]{2,1,0:T(8,128)S(1)}, u32[]{:S(2)}, u32[]{:S(2)}) collective-permute-start(f32[4,16,128]{2,1,0:T(8,128)S(1)} %get-tuple-element.14), channel_id=1, source_target_pairs={{0,1000},{8,1008},{16,1016},{24,0},{32,8},{40,16},{48,24},{56,32},... | collective-permute-start | bytes 98312 | tf_op jit(solution)/shard_map/ppermute | solution.py:170
  44.6 9.9 %collective-permute-start.6 = (f32[14,16,128]{2,1,0:T(8,128)S(1)}, f32[14,16,128]{2,1,0:T(8,128)S(1)}, u32[]{:S(2)}, u32[]{:S(2)}) collective-permute-start(f32[14,16,128]{2,1,0:T(8,128)S(1)} %constant_dynamic-update-slice_fusion.12), channel_id=1, source_target_pairs={{0,8},{8,16},{16,24},{24,32},{32,40},{40,48},{48,56},{56,64},{64,7... | collective-permute-start | bytes 344072 | tf_op jit(solution)/shard_map/ppermute | solution.py:170
  46.5 9.5 %collective-permute-start.7 = (f32[14,16,128]{2,1,0:T(8,128)S(1)}, f32[14,16,128]{2,1,0:T(8,128)S(1)}, u32[]{:S(2)}, u32[]{:S(2)}) collective-permute-start(f32[14,16,128]{2,1,0:T(8,128)S(1)} %constant_dynamic-update-slice_fusion.17), channel_id=1, source_target_pairs={{0,1016},{8,0},{16,8},{24,16},{32,24},{40,32},{48,40},{56,48},{64,... | collective-permute-start | bytes 344072 | tf_op jit(solution)/shard_map/ppermute | solution.py:170
  56.1 6.2 %collective-permute-start.8 = (f32[26,8,128]{2,1,0:T(8,128)S(1)}, f32[26,8,128]{2,1,0:T(8,128)S(1)}, u32[]{:S(2)}, u32[]{:S(2)}) collective-permute-start(f32[26,8,128]{2,1,0:T(8,128)S(1)} %constant_dynamic-update-slice_fusion.22), channel_id=1, source_target_pairs={{0,7},{1,0},{2,1},{3,2},{4,3},{5,4},{6,5},{7,6},{8,15},{9,8},{10,9... | collective-permute-start | bytes 319496 | tf_op jit(solution)/shard_map/ppermute | solution.py:170
  61.3 1.7 %collective-permute-start.9 = (f32[26,8,128]{2,1,0:T(8,128)S(1)}, f32[26,8,128]{2,1,0:T(8,128)S(1)}, u32[]{:S(2)}, u32[]{:S(2)}) collective-permute-start(f32[26,8,128]{2,1,0:T(8,128)S(1)} %constant_dynamic-update-slice_fusion.27), channel_id=1, source_target_pairs={{0,1},{1,2},{2,3},{3,4},{4,5},{5,6},{6,7},{7,0},{8,9},{9,10},{10,1... | collective-permute-start | bytes 319496 | tf_op jit(solution)/shard_map/ppermute | solution.py:170

commit v13 on v12

--- a/solution.py
+++ b/solution.py
@@ -16,17 +16,16 @@
     return total + pltpu.roll(v, 1, 1) + pltpu.roll(v, v.shape[1] - 1, 1)
 
 
-def jacobi(ref, i, rows, source, inv_step):
+def jacobi(ref, i, rows, source, area):
     v = ref[i, rows]
     square = v * v
-    inner = (6.0 * inv_step + mass) + (mass / 3.0) * square
-    top = inv_step * around(ref, i, rows) - source - v * inner
-    return v + top / ((6.0 * inv_step + mass) / damping + (mass / damping) * square)
-
-
-def operator(ref, i, rows, inv_step):
+    top = around(ref, i, rows) - source - v * ((6.0 + area * mass) + (area * mass / 3.0) * square)
+    return v + top / ((6.0 + area * mass) / damping + (area * mass / damping) * square)
+
+
+def operator(ref, i, rows, area):
     v = ref[i, rows]
-    return inv_step * around(ref, i, rows) - v * ((6.0 * inv_step + mass) + (mass / 3.0) * (v * v))
+    return around(ref, i, rows) - v * ((6.0 + area * mass) + (area * mass / 3.0) * (v * v))
 
 
 def exact_dot(values, weights):
@@ -110,11 +109,11 @@
         v = start[i, rows]
         c0[i, rows] = v - r[i] / ((1.5 + mass) / damping + (mass / damping) * (v * v))
     for i in range(1, 15):
-        g[i] = operator(start, i, rows, 0.25) + r[i]
+        g[i] = operator(start, i, rows, 4.0) + 4.0 * r[i]
     now, later = c0, c1
     for sweep in range(1, 6):
         for i in range(sweep, 16 - sweep):
-            later[i, rows] = jacobi(now, i, rows, g[i], 0.25)
+            later[i, rows] = jacobi(now, i, rows, g[i], 4.0)
         now, later = later, now
     change = (now[5:11, 8:40] - start[5:11, 8:40]).reshape(192, 128)
     half = lax.broadcasted_iota(jnp.int32, (128, 256), 0)

time: 65.2 us -> 65.2 us (level)
  no operation moved by 1% of the time
where the time goes in v13:
time: 65.2 us; the launch traced here: 64.9 us
  starting transfers between devices  51.7 us (79%)
  waiting for transfers between devices  9.11 us (14%)
  Pallas kernels  2.69 us (4%)
  local copies, waits for them, and re-layouts  1.12 us (2%)
    ppermute x10, starting transfers between devices, send(): lax.ppermute(values, axis, [(i, (i + step) % count) for i in range(count)])  51.7 us
    ppermute x10, waiting for transfers between devices, send(): lax.ppermute(values, axis, [(i, (i + step) % count) for i in range(count)])  9.11 us
    pallas_call x2, Pallas kernels, call(): pl.pallas_call(kernel, out_shape=shapes, in_specs=[vmem] * len(args), out...  2.69 us
  transfers between devices with their start and end apart: 10, of which 8 were waited for; matrix products, arithmetic and copies ran while one was open for 0% of the time, Pallas kernels for 0%

profile of v13, /device:TPU:1, one launch (start us, length us, event | category | flops | bytes accessed | tf_op | source)
XLA Modules:
  0.0 64.9 jit_solution(12578293057571937842)
XLA Ops:
  0.0 0.0 copy-start
  0.0 0.9 %fusion.3 = (f32[2,32,256]{2,1,0:T(8,128)S(1)}, f32[2,32,256]{2,1,0:T(8,128)S(1)}) fusion(f32[4,32,256]{2,1,0:T(8,128)} %density.1), kind=kLoop, calls=%fused_computation.37 | loop fusion | bytes 262144 | tf_op jit(solution)/shard_map/slice | solution.py:187
  0.9 0.0 copy-done
  1.0 4.4 %collective-permute-start = (f32[5,32,256]{2,1,0:T(8,128)S(1)}, f32[5,32,256]{2,1,0:T(8,128)S(1)}, u32[]{:S(2)}, u32[]{:S(2)}) collective-permute-start(f32[5,32,256]{2,1,0:T(8,128)S(1)} %pad_maximum_fusion), channel_id=1, source_target_pairs={{0,8},{8,16},{16,24},{24,32},{32,40},{40,48},{48,56},{56,64},{64,7... | collective-permute-start | bytes 491528 | tf_op jit(solution)/shard_map/ppermute | solution.py:169
  5.4 0.0 copy-start.1
  5.4 19.4 %collective-permute-start.1 = (f32[5,32,256]{2,1,0:T(8,128)S(1)}, f32[5,32,256]{2,1,0:T(8,128)S(1)}, u32[]{:S(2)}, u32[]{:S(2)}) collective-permute-start(f32[5,32,256]{2,1,0:T(8,128)S(1)} %pad_maximum_fusion.1), channel_id=1, source_target_pairs={{0,1016},{8,0},{16,8},{24,16},{32,24},{40,32},{48,40},{56,48},{64,... | collective-permute-start | bytes 491528 | tf_op jit(solution)/shard_map/ppermute | solution.py:169
  24.8 1.8 %collective-permute-done.xlo = f32[5,32,256]{2,1,0:T(8,128)S(1)} collective-permute-done((f32[5,32,256]{2,1,0:T(8,128)S(1)}, f32[5,32,256]{2,1,0:T(8,128)S(1)}, u32[]{:S(2)}, u32[]{:S(2)}) %collective-permute-start) | collective-permute-done | bytes 163872 | tf_op jit(solution)/shard_map/ppermute | solution.py:169
  26.6 1.0 %collective-permute-done.1.xhi = f32[5,32,256]{2,1,0:T(8,128)S(1)} collective-permute-done((f32[5,32,256]{2,1,0:T(8,128)S(1)}, f32[5,32,256]{2,1,0:T(8,128)S(1)}, u32[]{:S(2)}, u32[]{:S(2)}) %collective-permute-start.1) | collective-permute-done | bytes 163872 | tf_op jit(solution)/shard_map/ppermute | solution.py:169
  27.7 0.0 copy-done.1
  27.8 1.6 %collective-permute-start.2 = (f32[14,4,256]{2,1,0:T(4,128)S(1)}, f32[14,4,256]{2,1,0:T(4,128)S(1)}, u32[]{:S(2)}, u32[]{:S(2)}) collective-permute-start(f32[14,4,256]{2,1,0:T(4,128)S(1)} %get-tuple-element.30), channel_id=1, source_target_pairs={{0,7},{1,0},{2,1},{3,2},{4,3},{5,4},{6,5},{7,6},{8,15},{9,8},{10,9... | collective-permute-start | bytes 172040 | tf_op jit(solution)/shard_map/ppermute | solution.py:169
  29.3 1.1 %collective-permute-start.3 = (f32[14,4,256]{2,1,0:T(4,128)S(1)}, f32[14,4,256]{2,1,0:T(4,128)S(1)}, u32[]{:S(2)}, u32[]{:S(2)}) collective-permute-start(f32[14,4,256]{2,1,0:T(4,128)S(1)} %get-tuple-element.29), channel_id=1, source_target_pairs={{0,1},{1,2},{2,3},{3,4},{4,5},{5,6},{6,7},{7,0},{8,9},{9,10},{10,1... | collective-permute-start | bytes 172040 | tf_op jit(solution)/shard_map/ppermute | solution.py:169
  30.4 1.8 %collective-permute-done.2.chi = f32[14,4,256]{2,1,0:T(4,128)S(1)} collective-permute-done((f32[14,4,256]{2,1,0:T(4,128)S(1)}, f32[14,4,256]{2,1,0:T(4,128)S(1)}, u32[]{:S(2)}, u32[]{:S(2)}) %collective-permute-start.2) | collective-permute-done | bytes 57376 | tf_op jit(solution)/shard_map/ppermute | solution.py:169
  32.3 0.0 collective-permute-done.3.clo
  32.3 0.8 %shard_map.28 = (f32[6,48,256]{2,1,0:T(8,128)S(1)}, f32[8,48,256]{2,1,0:T(8,128)S(1)}, f32[4,16,128]{2,1,0:T(8,128)S(1)}, f32[4,16,128]{2,1,0:T(8,128)S(1)}, f32...) custom-call(f32[4,32,256]{2,1,0:T(8,128)S(1)} %copy-done, f32[4,32,256]{2,1,0:T(8,128)S(1)} %copy-done.1, ...), custom_call_target="tpu_custom_call" | custom-call | tf_op jit(solution)/shard_map/pallas_call | solution.py:157
  33.1 1.9 %collective-permute-start.4 = (f32[4,16,128]{2,1,0:T(8,128)S(1)}, f32[4,16,128]{2,1,0:T(8,128)S(1)}, u32[]{:S(2)}, u32[]{:S(2)}) collective-permute-start(f32[4,16,128]{2,1,0:T(8,128)S(1)} %get-tuple-element.13.own), channel_id=1, source_target_pairs={{0,24},{8,32},{16,40},{24,48},{32,56},{40,64},{48,72},{56,80},{64,... | collective-permute-start | bytes 98312 | tf_op jit(solution)/shard_map/ppermute | solution.py:169
  35.0 8.5 %collective-permute-start.5 = (f32[4,16,128]{2,1,0:T(8,128)S(1)}, f32[4,16,128]{2,1,0:T(8,128)S(1)}, u32[]{:S(2)}, u32[]{:S(2)}) collective-permute-start(f32[4,16,128]{2,1,0:T(8,128)S(1)} %get-tuple-element.14), channel_id=1, source_target_pairs={{0,1000},{8,1008},{16,1016},{24,0},{32,8},{40,16},{48,24},{56,32},... | collective-permute-start | bytes 98312 | tf_op jit(solution)/shard_map/ppermute | solution.py:169
  43.5 1.0 %collective-permute-done.5.fhi = f32[4,16,128]{2,1,0:T(8,128)S(1)} collective-permute-done((f32[4,16,128]{2,1,0:T(8,128)S(1)}, f32[4,16,128]{2,1,0:T(8,128)S(1)}, u32[]{:S(2)}, u32[]{:S(2)}) %collective-permute-start.5) | collective-permute-done | bytes 32800 | tf_op jit(solution)/shard_map/ppermute | solution.py:169
  44.5 0.0 collective-permute-done.4.flo
  44.6 1.9 %collective-permute-start.6 = (f32[14,16,128]{2,1,0:T(8,128)S(1)}, f32[14,16,128]{2,1,0:T(8,128)S(1)}, u32[]{:S(2)}, u32[]{:S(2)}) collective-permute-start(f32[14,16,128]{2,1,0:T(8,128)S(1)} %constant_dynamic-update-slice_fusion.12), channel_id=1, source_target_pairs={{0,8},{8,16},{16,24},{24,32},{32,40},{40,48},{48,56},{56,64},{64,7... | collective-permute-start | bytes 344072 | tf_op jit(solution)/shard_map/ppermute | solution.py:169
  46.5 7.7 %collective-permute-start.7 = (f32[14,16,128]{2,1,0:T(8,128)S(1)}, f32[14,16,128]{2,1,0:T(8,128)S(1)}, u32[]{:S(2)}, u32[]{:S(2)}) collective-permute-start(f32[14,16,128]{2,1,0:T(8,128)S(1)} %constant_dynamic-update-slice_fusion.17), channel_id=1, source_target_pairs={{0,1016},{8,0},{16,8},{24,16},{32,24},{40,32},{48,40},{56,48},{64,... | collective-permute-start | bytes 344072 | tf_op jit(solution)/shard_map/ppermute | solution.py:169
  54.3 0.2 collective-permute-done.6.nlo
  54.5 1.6 %collective-permute-done.7.nhi = f32[14,16,128]{2,1,0:T(8,128)S(1)} collective-permute-done((f32[14,16,128]{2,1,0:T(8,128)S(1)}, f32[14,16,128]{2,1,0:T(8,128)S(1)}, u32[]{:S(2)}, u32[]{:S(2)}) %collective-permute-start.7) | collective-permute-done | bytes 114720 | tf_op jit(solution)/shard_map/ppermute | solution.py:169
  56.1 5.2 %collective-permute-start.8 = (f32[26,8,128]{2,1,0:T(8,128)S(1)}, f32[26,8,128]{2,1,0:T(8,128)S(1)}, u32[]{:S(2)}, u32[]{:S(2)}) collective-permute-start(f32[26,8,128]{2,1,0:T(8,128)S(1)} %constant_dynamic-update-slice_fusion.22), channel_id=1, source_target_pairs={{0,7},{1,0},{2,1},{3,2},{4,3},{5,4},{6,5},{7,6},{8,15},{9,8},{10,9... | collective-permute-start | bytes 319496 | tf_op jit(solution)/shard_map/ppermute | solution.py:169
  61.3 0.0 collective-permute-start.9
  61.3 0.9 %collective-permute-done.8.zrows = f32[26,8,128]{2,1,0:T(8,128)S(1)} collective-permute-done((f32[26,8,128]{2,1,0:T(8,128)S(1)}, f32[26,8,128]{2,1,0:T(8,128)S(1)}, u32[]{:S(2)}, u32[]{:S(2)}) %collective-permute-start.8) | collective-permute-done | bytes 106528 | tf_op jit(solution)/shard_map/ppermute | solution.py:169
  62.3 0.8 %collective-permute-done.9.yrows = f32[26,8,128]{2,1,0:T(8,128)S(1)} collective-permute-done((f32[26,8,128]{2,1,0:T(8,128)S(1)}, f32[26,8,128]{2,1,0:T(8,128)S(1)}, u32[]{:S(2)}, u32[]{:S(2)}) %collective-permute-start.9) | collective-permute-done | bytes 106528 | tf_op jit(solution)/shard_map/ppermute | solution.py:169
  63.0 1.9 %shard_map.29 = f32[4,32,256]{2,1,0:T(8,128)} custom-call(f32[6,48,256]{2,1,0:T(8,128)S(1)} %get-tuple-element.11.smooth, f32[8,48,256]{2,1,0:T(8,128)S(1)} %get-tuple-element.12.dens, f32[4,16,128]{2,1,0:T(8,128)S(1)} %get-tuple-element.13.own, f32[4,16,128]{2,1,0:T(8,128)S(1)} %collective-permute-done.4.flo, f32[4,16,128]{2,1,0:T(8,128)S(1)} %collective-permute-done.5.fhi, ...), custom_call_target="tpu_custom_call" | custom-call | tf_op jit(solution)/shard_map/pallas_call | solution.py:157
  (32 shorter events, 0.3 us)
Async XLA Ops:
  0.0 1.0 %copy-start = (f32[4,32,256]{2,1,0:T(8,128)S(1)}, f32[4,32,256]{2,1,0:T(8,128)}, u32[]{:S(2)}) copy-start(f32[4,32,256]{2,1,0:T(8,128)} %field.1) | copy-start | bytes 393220
  1.0 25.6 %collective-permute-start = (f32[5,32,256]{2,1,0:T(8,128)S(1)}, f32[5,32,256]{2,1,0:T(8,128)S(1)}, u32[]{:S(2)}, u32[]{:S(2)}) collective-permute-start(f32[5,32,256]{2,1,0:T(8,128)S(1)} %pad_maximum_fusion), channel_id=1, source_target_pairs={{0,8},{8,16},{16,24},{24,32},{32,40},{40,48},{48,56},{56,64},{64,7... | collective-permute-start | bytes 491528 | tf_op jit(solution)/shard_map/ppermute | solution.py:169
  5.4 22.3 %copy-start.1 = (f32[4,32,256]{2,1,0:T(8,128)S(1)}, f32[4,32,256]{2,1,0:T(8,128)}, u32[]{:S(2)}) copy-start(f32[4,32,256]{2,1,0:T(8,128)} %density.1) | copy-start | bytes 393220
  5.4 22.2 %collective-permute-start.1 = (f32[5,32,256]{2,1,0:T(8,128)S(1)}, f32[5,32,256]{2,1,0:T(8,128)S(1)}, u32[]{:S(2)}, u32[]{:S(2)}) collective-permute-start(f32[5,32,256]{2,1,0:T(8,128)S(1)} %pad_maximum_fusion.1), channel_id=1, source_target_pairs={{0,1016},{8,0},{16,8},{24,16},{32,24},{40,32},{48,40},{56,48},{64,... | collective-permute-start | bytes 491528 | tf_op jit(solution)/shard_map/ppermute | solution.py:169
  27.8 4.5 %collective-permute-start.2 = (f32[14,4,256]{2,1,0:T(4,128)S(1)}, f32[14,4,256]{2,1,0:T(4,128)S(1)}, u32[]{:S(2)}, u32[]{:S(2)}) collective-permute-start(f32[14,4,256]{2,1,0:T(4,128)S(1)} %get-tuple-element.30), channel_id=1, source_target_pairs={{0,7},{1,0},{2,1},{3,2},{4,3},{5,4},{6,5},{7,6},{8,15},{9,8},{10,9... | collective-permute-start | bytes 172040 | tf_op jit(solution)/shard_map/ppermute | solution.py:169
  29.3 3.0 %collective-permute-start.3 = (f32[14,4,256]{2,1,0:T(4,128)S(1)}, f32[14,4,256]{2,1,0:T(4,128)S(1)}, u32[]{:S(2)}, u32[]{:S(2)}) collective-permute-start(f32[14,4,256]{2,1,0:T(4,128)S(1)} %get-tuple-element.29), channel_id=1, source_target_pairs={{0,1},{1,2},{2,3},{3,4},{4,5},{5,6},{6,7},{7,0},{8,9},{9,10},{10,1... | collective-permute-start | bytes 172040 | tf_op jit(solution)/shard_map/ppermute | solution.py:169
  33.1 11.4 %collective-permute-start.4 = (f32[4,16,128]{2,1,0:T(8,128)S(1)}, f32[4,16,128]{2,1,0:T(8,128)S(1)}, u32[]{:S(2)}, u32[]{:S(2)}) collective-permute-start(f32[4,16,128]{2,1,0:T(8,128)S(1)} %get-tuple-element.13.own), channel_id=1, source_target_pairs={{0,24},{8,32},{16,40},{24,48},{32,56},{40,64},{48,72},{56,80},{64,... | collective-permute-start | bytes 98312 | tf_op jit(solution)/shard_map/ppermute | solution.py:169
  35.0 9.5 %collective-permute-start.5 = (f32[4,16,128]{2,1,0:T(8,128)S(1)}, f32[4,16,128]{2,1,0:T(8,128)S(1)}, u32[]{:S(2)}, u32[]{:S(2)}) collective-permute-start(f32[4,16,128]{2,1,0:T(8,128)S(1)} %get-tuple-element.14), channel_id=1, source_target_pairs={{0,1000},{8,1008},{16,1016},{24,0},{32,8},{40,16},{48,24},{56,32},... | collective-permute-start | bytes 98312 | tf_op jit(solution)/shard_map/ppermute | solution.py:169
  44.6 9.9 %collective-permute-start.6 = (f32[14,16,128]{2,1,0:T(8,128)S(1)}, f32[14,16,128]{2,1,0:T(8,128)S(1)}, u32[]{:S(2)}, u32[]{:S(2)}) collective-permute-start(f32[14,16,128]{2,1,0:T(8,128)S(1)} %constant_dynamic-update-slice_fusion.12), channel_id=1, source_target_pairs={{0,8},{8,16},{16,24},{24,32},{32,40},{40,48},{48,56},{56,64},{64,7... | collective-permute-start | bytes 344072 | tf_op jit(solution)/shard_map/ppermute | solution.py:169
  46.5 9.5 %collective-permute-start.7 = (f32[14,16,128]{2,1,0:T(8,128)S(1)}, f32[14,16,128]{2,1,0:T(8,128)S(1)}, u32[]{:S(2)}, u32[]{:S(2)}) collective-permute-start(f32[14,16,128]{2,1,0:T(8,128)S(1)} %constant_dynamic-update-slice_fusion.17), channel_id=1, source_target_pairs={{0,1016},{8,0},{16,8},{24,16},{32,24},{40,32},{48,40},{56,48},{64,... | collective-permute-start | bytes 344072 | tf_op jit(solution)/shard_map/ppermute | solution.py:169
  56.1 6.2 %collective-permute-start.8 = (f32[26,8,128]{2,1,0:T(8,128)S(1)}, f32[26,8,128]{2,1,0:T(8,128)S(1)}, u32[]{:S(2)}, u32[]{:S(2)}) collective-permute-start(f32[26,8,128]{2,1,0:T(8,128)S(1)} %constant_dynamic-update-slice_fusion.22), channel_id=1, source_target_pairs={{0,7},{1,0},{2,1},{3,2},{4,3},{5,4},{6,5},{7,6},{8,15},{9,8},{10,9... | collective-permute-start | bytes 319496 | tf_op jit(solution)/shard_map/ppermute | solution.py:169
  61.3 1.7 %collective-permute-start.9 = (f32[26,8,128]{2,1,0:T(8,128)S(1)}, f32[26,8,128]{2,1,0:T(8,128)S(1)}, u32[]{:S(2)}, u32[]{:S(2)}) collective-permute-start(f32[26,8,128]{2,1,0:T(8,128)S(1)} %constant_dynamic-update-slice_fusion.27), channel_id=1, source_target_pairs={{0,1},{1,2},{2,3},{3,4},{4,5},{5,6},{6,7},{7,0},{8,9},{9,10},{10,1... | collective-permute-start | bytes 319496 | tf_op jit(solution)/shard_map/ppermute | solution.py:169
